TPU v7x, 32 devices: a whole 2x2x4 slice. The times are simulated.
32 devices in a mesh: groups: 2 (over y), tm: 8 (over z, x), cells: 2 (over core).
Axes of the slice: x: 2, y: 2, z: 4, core: 2. Of those that a mesh axis runs over, the one named last changes fastest.
Arguments:
- propagator: bfloat16 [272, 48, 4, 256], P(('groups', 'tm'), None, None, 'cells'), parts along dimension 0, as said below
- tile_blocks: int32 [272, 2], P(('groups', 'tm')), parts along dimension 0, may hold values from 0 to 15, as said below
- histories: bfloat16 [16, 12, 48], P('tm'), may hold values from -6 to 6
Outputs:
- concentration: float32 [32, 12, 4, 256], P(('groups', 'tm'), None, None, 'cells'), parts along dimension 0
There are 2 independent parts, one for each index of `groups`. A program takes and returns all parts, laid end to end along the dimension named above; an argument that names none is the same for every part. Nothing has to cross between parts.
Inputs may be any that keep to these rules, and one draw needn't show every extreme that they name: `tile_blocks`: rows s * 17 to (s + 1) * 17 - 1 belong to two mirrored source blocks p and 15 - p, where p runs over a permutation of 0 to 7 from one such row group to the next; for each of the two source blocks every arrival block from it up to 15 appears in exactly one row, rows in any order. Tile n holds the propagator from source block tile_blocks[n, 0] to arrival block tile_blocks[n, 1].
All inputs are finite; a program needn't handle non-finite values.
Results may differ from a plain program's by a relative error of at most 0.0003.
Values may be sent and summed in bfloat16 or wider, within the bound.
No kernel may reach another device: no remote copies, remote signals or barrier semaphores. Data moves between devices by JAX's collectives and lax.ppermute only.
A program may use at most 64 MiB of HBM per device.

v0:
```python
import jax
import jax.numpy as jnp
from jax import lax
from jax.sharding import PartitionSpec as P


def shards(propagator, tile_blocks, histories):
    all_histories = lax.all_gather(histories, "tm", axis=0, tiled=True)
    block_count = all_histories.shape[0]
    tracer_count = all_histories.shape[1]
    slot_count, source_width, months, cell_count = propagator.shape
    tile_rows = propagator.reshape(slot_count, source_width, months * cell_count)
    sources = tile_blocks[:, 0]
    arrivals = tile_blocks[:, 1]
    selector = (sources[:, None] == jnp.arange(block_count, dtype=jnp.int32)[None, :]).astype(
        jnp.bfloat16
    )
    chosen = jnp.dot(
        selector,
        all_histories.reshape(block_count, tracer_count * source_width),
        preferred_element_type=jnp.float32,
    )
    chosen = chosen.astype(jnp.bfloat16).reshape(slot_count, tracer_count, source_width)
    contribution = jnp.einsum("nrk,nkm->nrm", chosen, tile_rows, preferred_element_type=jnp.float32)
    partial_sums = (
        jnp.zeros((block_count, tracer_count, months * cell_count), jnp.float32)
        .at[arrivals]
        .add(contribution)
    )
    owned = lax.psum_scatter(partial_sums, "tm", scatter_dimension=0, tiled=True)
    return owned.reshape(owned.shape[0], tracer_count, months, cell_count)


def solution(mesh):
    in_specs = (
        P(("groups", "tm"), None, None, "cells"),
        P(("groups", "tm"), None),
        P("tm", None, None),
    )
    out_specs = P(("groups", "tm"), None, None, "cells")
    return jax.shard_map(shards, mesh=mesh, in_specs=in_specs, out_specs=out_specs, check_vma=False)
```

profile of v0, /device:TPU:0, one launch (start us, length us, event | category | flops | bytes accessed | tf_op | source)
XLA Modules:
  0.0 117.3 jit_solution(11963903710635323625)
XLA Ops:
  6.5 0.0 reduce-scatter.2.cloned.1.call-start
  6.5 0.8 slice_bitcast_fusion
  7.3 0.7 copy.9
  8.0 32.3 %all_gather.3 = bf16[16,12,48]{2,1,0:T(8,128)(2,1)S(1)} all-gather(bf16[2,12,48]{2,1,0:T(8,128)(2,1)S(1)} %copy.9), channel_id=1, replica_groups=mesh['groups'=2,'tm'=8,'cells'=2] {'tm'}, dimensions={0}, use_global_device_ids=true | all-gather | bytes 20736 | tf_op jit(solution)/shard_map/all_gather | solution.py:8
  40.3 0.1 reshape.12
  40.4 0.2 convolution_convert_fusion
  40.6 0.1 reshape.13
  40.7 1.7 %reshape.14 = bf16[17,48,512]{2,1,0:T(8,128)(2,1)S(1)} reshape(bf16[17,48,4,128]{3,2,1,0:T(4,128)(2,1)} %param.3) | data formatting | bytes 1671168 | tf_op jit(solution)/shard_map/reshape | solution.py:12
  42.4 0.2 fusion.2
  42.6 0.1 broadcast_in_dim.2
  42.7 2.1 %scatter_fusion = f32[16,12,512]{2,1,0:T(8,128)S(1)} fusion(f32[16,12,512]{2,1,0:T(8,128)S(1)} %broadcast_in_dim.2, s32[17]{0:T(128)S(1)} %get-tuple-element.6, f32[17,12,512]{2,1,0:T(8,128)S(1)} %fusion.2), kind=kCustom, calls=%fused_computation | custom fusion | flops 104448 | bytes 1253444 | tf_op jit(solution)/shard_map/scatter-add | solution.py:28
  44.8 0.0 copy-start
  44.8 0.8 copy-done
  45.6 0.0 reduce-scatter.2.cloned.1.call-update
  45.6 63.4 %reduce-scatter.2.cloned.1.call-done = f32[2,12,512]{2,1,0:T(8,128)} async-done(((f32[16,12,512]{2,1,0:T(8,128)}), f32[2,12,512]{2,1,0:T(8,128)}) %reduce-scatter.2.cloned.1.call-update) | async-done | bytes 49168 | tf_op jit(solution)/shard_map/reduce_scatter | solution.py:30
  109.0 1.5 %reshape.24 = f32[2,12,4,128]{3,2,1,0:T(4,128)} reshape(f32[2,12,512]{2,1,0:T(8,128)} %reduce-scatter.2.cloned.1.call-done) | data formatting | bytes 98304 | tf_op jit(solution)/shard_map/reshape | solution.py:31
Async XLA Ops:
  6.5 102.5 %reduce-scatter.2.cloned.1.call-start = ((), (), s32[]{:S(2)}) async-start(), calls=%async_computation.1 | async-start | bytes 589824 | tf_op jit(solution)/shard_map/reduce_scatter | solution.py:30
  44.8 0.8 copy-start
Sparse Core Ops, SparseCore 0:
  45.8 63.2 reduce-scatter.1
where the time goes:
time: 118 us; the launch traced here: 117 us
  waiting for transfers between devices  63.4 us (54%)
  blocking collectives  32.3 us (27%)
  between operations  13.4 us (11%)
  local copies, waits for them, and re-layouts  4.92 us (4%)
  other arithmetic  2.87 us (2%)
    reduce_scatter x1, waiting for transfers between devices, shards(): lax.psum_scatter(partial_sums, 'tm', scatter_dimension=0, tiled=True)  63.4 us
    all_gather x1, blocking collectives, shards(): all_histories = lax.all_gather(histories, 'tm', axis=0, tiled=True)  32.3 us
  transfers between devices with their start and end apart: 1, of which 1 were waited for; matrix products, arithmetic and copies ran while one was open for 0% of the time, Pallas kernels for 0%

commit v1 on v0

v1 whole, which is shorter than its diff:
```python
import jax
import jax.numpy as jnp
from jax import lax
from jax.experimental import pallas as pl
from jax.experimental.pallas import tpu as pltpu
from jax.sharding import PartitionSpec as P


def tile_sums(months, blocks_ref, histories_ref, tiles_ref, sums_ref, wide_ref):
    size, packed_rows, packed_width = histories_ref.shape
    slot_count, tile_height, cell_count = tiles_ref.shape
    block_count, height, cell_count = sums_ref.shape
    own_blocks = block_count // size

    first = blocks_ref[0, 0]
    row_of = lax.broadcasted_iota(jnp.int32, (height, packed_rows), 0) // months * own_blocks
    packed_row = lax.broadcasted_iota(jnp.int32, (height, packed_rows), 1)
    column_of = lax.broadcasted_iota(jnp.int32, (packed_width, tile_height), 1) // months
    packed_column = lax.broadcasted_iota(jnp.int32, (packed_width, tile_height), 0)
    repeat_columns = (column_of == packed_column).astype(jnp.bfloat16)
    month_of_row = lax.broadcasted_iota(jnp.int32, (height, tile_height), 0) % months
    month_of_column = lax.broadcasted_iota(jnp.int32, (height, tile_height), 1) % months
    same_month = month_of_row == month_of_column
    for which, source in enumerate((first, block_count - 1 - first)):
        repeat_rows = (row_of + source % own_blocks == packed_row).astype(jnp.bfloat16)
        tall = jnp.dot(
            repeat_rows, histories_ref[source // own_blocks], preferred_element_type=jnp.float32
        )
        wide = jnp.dot(tall.astype(jnp.bfloat16), repeat_columns, preferred_element_type=jnp.float32)
        wide_ref[which] = jnp.where(same_month, wide, 0.0).astype(jnp.bfloat16)

    sums_ref[...] = jnp.zeros(sums_ref.shape, sums_ref.dtype)

    def add_tile(slot):
        which = (blocks_ref[0, slot] != first).astype(jnp.int32)
        arrival = blocks_ref[1, slot]
        sums_ref[arrival] += jnp.dot(wide_ref[which], tiles_ref[slot], preferred_element_type=jnp.float32)

    unrolled = 17
    rounds = slot_count // unrolled

    def add_round(turn, carry):
        for step in range(unrolled):
            add_tile(turn * unrolled + step)
        return carry

    if rounds == 1:
        add_round(0, 0)
    else:
        lax.fori_loop(0, rounds, add_round, 0)
    for slot in range(rounds * unrolled, slot_count):
        add_tile(slot)


def shards(propagator, tile_blocks, histories):
    size = lax.axis_size("tm")
    own_blocks, tracer_count, source_width = histories.shape
    slot_count, source_width, months, cell_count = propagator.shape
    block_count = size * own_blocks
    height = tracer_count * months

    used_rows = tracer_count * own_blocks
    packed = jnp.pad(
        jnp.swapaxes(histories, 0, 1).reshape(used_rows, source_width),
        ((0, -used_rows % 16), (0, -source_width % 128)),
    )
    copies = jnp.broadcast_to(packed[None], (size,) + packed.shape)
    received = lax.all_to_all(copies, "tm", 0, 0, tiled=True)

    tiles = propagator.reshape(slot_count, source_width * months, cell_count)
    vmem = pl.BlockSpec(memory_space=pltpu.VMEM)
    partial_sums = pl.pallas_call(
        lambda *refs: tile_sums(months, *refs),
        out_shape=jax.ShapeDtypeStruct((block_count, height, cell_count), jnp.float32),
        in_specs=[pl.BlockSpec(memory_space=pltpu.SMEM), vmem, vmem],
        out_specs=vmem,
        scratch_shapes=[pltpu.VMEM((2, height, source_width * months), jnp.bfloat16)],
        compiler_params=pltpu.CompilerParams(vmem_limit_bytes=32 * 1024 * 1024),
        cost_estimate=pl.CostEstimate(
            flops=2 * slot_count * height * source_width * months * cell_count,
            bytes_accessed=propagator.size * 2 + block_count * height * cell_count * 4,
            transcendentals=0,
        ),
    )(tile_blocks.T, received, tiles)

    exchanged = lax.all_to_all(partial_sums, "tm", 0, 0, tiled=True)
    owned = exchanged.reshape(size, own_blocks, height, cell_count).sum(0)
    return owned.reshape(own_blocks, tracer_count, months, cell_count)


def solution(mesh):
    in_specs = (
        P(("groups", "tm"), None, None, "cells"),
        P(("groups", "tm"), None),
        P("tm", None, None),
    )
    out_specs = P(("groups", "tm"), None, None, "cells")
    return jax.shard_map(shards, mesh=mesh, in_specs=in_specs, out_specs=out_specs, check_vma=False)
```

time: 118 us -> 31.9 us (0.27)
  waiting for transfers between devices: 63.4 us -> 0 us
  between operations: 13.4 us -> 0.01 us
  blocking collectives: 32.3 us -> 27.2 us
  local copies, waits for them, and re-layouts: 4.92 us -> 2.54 us
  other arithmetic: 2.87 us -> 0.64 us
    reduce_scatter x1 -> x0, waiting for transfers between devices: 63.4 us -> none  [shards(): lax.psum_scatter(partial_sums, 'tm', scatter_dimension=0, tiled=True)]
    all_gather x1 -> x0, blocking collectives: 32.3 us -> none  [shards(): all_histories = lax.all_gather(histories, 'tm', axis=0, tiled=True)]
    all_to_all x0 -> x2, blocking collectives: none -> 27.2 us  [the longest x1 14 us: shards(): received = lax.all_to_all(copies, 'tm', 0, 0, tiled=True)]
    reshape x4 -> x0, local copies, waits for them, and re-layouts: 3.39 us -> none  [the longest x1 1.69 us: shards(): propagator.reshape(slot_count, source_width, months * cell_count)]
    scatter-add x1 -> x0, other arithmetic: 2.11 us -> none  [shards(): partial_sums = jnp.zeros((block_count, tracer_count, months * cell_count)...]
  transfers between devices with their start and end apart: 1 -> 0, of which waited for: 1 -> 0; matrix products, arithmetic and copies ran while one was open for 0% -> 0% of each run, Pallas kernels for 0% -> 0%
where the time goes in v1:
time: 31.9 us; the launch traced here: 31.6 us
  blocking collectives  27.2 us (85%)
  local copies, waits for them, and re-layouts  2.54 us (8%)
  Pallas kernels  1.15 us (4%)
  other arithmetic  0.64 us (2%)
    all_to_all x1, blocking collectives, shards(): received = lax.all_to_all(copies, 'tm', 0, 0, tiled=True)  14 us
    all_to_all x1, blocking collectives, shards(): exchanged = lax.all_to_all(partial_sums, 'tm', 0, 0, tiled=True)  13.3 us
    unnamed x4, local copies, waits for them, and re-layouts  1.83 us
    pallas_call x1, Pallas kernels, shards(): pl.pallas_call(lambda *refs: tile_sums(months, *refs), out_shape=jax.Shap...  1.15 us
    pad x1, local copies, waits for them, and re-layouts, shards(): jnp.pad(jnp.swapaxes(histories, 0, 1).reshape(used_rows, source_width), (...  0.7 us
    reduce_sum x1, other arithmetic, shards(): owned = exchanged.reshape(size, own_blocks, height, cell_count).sum(0)  0.64 us

profile of v1, /device:TPU:0, one launch (start us, length us, event | category | flops | bytes accessed | tf_op | source)
XLA Modules:
  0.0 31.6 jit_solution(4708043641714086784)
XLA Ops:
  0.0 0.7 %pad.4 = bf16[32,128]{1,0:T(8,128)(2,1)S(1)} pad(bf16[24,48]{1,0:T(8,128)(2,1)} %bitcast.10, bf16[]{:T(256)} %constant.1.clone.1), padding=0_8x0_80 | pad | bytes 10498 | tf_op jit(solution)/shard_map/jit(_pad)/pad | solution.py:63
  0.7 14.0 %all_to_all.10.refs_1_ = bf16[8,32,128]{2,1,0:T(8,128)(2,1)S(1)} all-to-all(bf16[8,32,128]{2,1,0:T(8,128)(2,1)S(1)} %broadcast_in_dim.2), channel_id=1, replica_groups=mesh['groups'=2,'tm'=8,'cells'=2] {'tm'}, dimensions={0} | all-to-all | bytes 131072 | tf_op jit(solution)/shard_map/all_to_all | solution.py:68
  14.7 0.0 copy-start.1
  14.7 0.7 %copy-done.1 = s32[17,2]{0,1:T(2,128)S(1)} copy-done((s32[17,2]{0,1:T(2,128)S(1)}, s32[17,2]{0,1:T(2,128)}, u32[]{:S(2)}) %copy-start.1) | copy-done | bytes 160
  15.3 0.0 copy-start
  15.3 1.1 %copy-done = bf16[17,48,4,128]{3,2,1,0:T(4,128)(2,1)S(1)} copy-done((bf16[17,48,4,128]{3,2,1,0:T(4,128)(2,1)S(1)}, bf16[17,48,4,128]{3,2,1,0:T(4,128)(2,1)}, u32[]{:S(2)}) %copy-start) | copy-done | bytes 835608
  16.5 1.1 %shard_map.37 = f32[16,48,128]{2,1,0:T(8,128)S(1)} custom-call(s32[2,17]{1,0:T(2,128)S(1)} %bitcast.8, bf16[8,32,128]{2,1,0:T(8,128)(2,1)S(1)} %all_to_all.10.refs_1_, bf16[17,192,128]{2,1,0:T(8,128)(2,1)S(1)} %bitcast.7), custom_call_target="tpu_custom_call" | custom-call | flops 40108032 | bytes 1228800 | tf_op jit(solution)/shard_map/pallas_call | solution.py:72
  17.7 13.3 %all_to_all.11 = f32[16,48,128]{2,1,0:T(8,128)S(1)} all-to-all(f32[16,48,128]{2,1,0:T(8,128)S(1)} %shard_map.37), channel_id=1, replica_groups=mesh['groups'=2,'tm'=8,'cells'=2] {'tm'}, dimensions={0} | all-to-all | bytes 786432 | tf_op jit(solution)/shard_map/all_to_all | solution.py:86
  30.9 0.6 %reduce_sum.9 = f32[2,48,128]{2,1,0:T(8,128)} reduce(f32[8,2,48,128]{3,2,1,0:T(8,128)S(1)} %bitcast.9, f32[]{:T(128)} %constant.4.clone.1), dimensions={0}, to_apply=%region_0.1 | reduce | flops 86016 | bytes 442372 | tf_op jit(solution)/shard_map/reduce_sum | solution.py:87
  (1 shorter events, 0.0 us)
Async XLA Ops:
  14.7 0.7 %copy-start.1 = (s32[17,2]{0,1:T(2,128)S(1)}, s32[17,2]{0,1:T(2,128)}, u32[]{:S(2)}) copy-start(s32[17,2]{0,1:T(2,128)} %param.4) | copy-start | bytes 412
  15.3 1.1 %copy-start = (bf16[17,48,4,128]{3,2,1,0:T(4,128)(2,1)S(1)}, bf16[17,48,4,128]{3,2,1,0:T(4,128)(2,1)}, u32[]{:S(2)}) copy-start(bf16[17,48,4,128]{3,2,1,0:T(4,128)(2,1)} %param.3) | copy-start | bytes 2506756

commit v2 on v1

--- a/solution.py
+++ b/solution.py
@@ -6,8 +6,9 @@
 from jax.sharding import PartitionSpec as P
 
 
-def tile_sums(months, blocks_ref, histories_ref, tiles_ref, sums_ref, wide_ref):
+def tile_sums(months, me_ref, blocks_ref, histories_ref, tiles_ref, sums_ref, wide_ref):
     size, packed_rows, packed_width = histories_ref.shape
+    me = me_ref[0]
     slot_count, tile_height, cell_count = tiles_ref.shape
     block_count, height, cell_count = sums_ref.shape
     own_blocks = block_count // size
@@ -24,7 +25,7 @@
     for which, source in enumerate((first, block_count - 1 - first)):
         repeat_rows = (row_of + source % own_blocks == packed_row).astype(jnp.bfloat16)
         tall = jnp.dot(
-            repeat_rows, histories_ref[source // own_blocks], preferred_element_type=jnp.float32
+            repeat_rows, histories_ref[(source // own_blocks) ^ me], preferred_element_type=jnp.float32
         )
         wide = jnp.dot(tall.astype(jnp.bfloat16), repeat_columns, preferred_element_type=jnp.float32)
         wide_ref[which] = jnp.where(same_month, wide, 0.0).astype(jnp.bfloat16)
@@ -52,6 +53,21 @@
         add_tile(slot)
 
 
+def stage(blocks_in, tiles_in, blocks_out, tiles_out, semaphores):
+    copies = [
+        pltpu.make_async_copy(blocks_in, blocks_out, semaphores.at[0]),
+        pltpu.make_async_copy(tiles_in, tiles_out, semaphores.at[1]),
+    ]
+    for copy in copies:
+        copy.start()
+    for copy in copies:
+        copy.wait()
+
+
+def swap(value, step, size):
+    return lax.ppermute(value, "tm", [(i, i ^ step) for i in range(size)])
+
+
 def shards(propagator, tile_blocks, histories):
     size = lax.axis_size("tm")
     own_blocks, tracer_count, source_width = histories.shape
@@ -60,19 +76,37 @@
     height = tracer_count * months
 
     used_rows = tracer_count * own_blocks
-    packed = jnp.pad(
-        jnp.swapaxes(histories, 0, 1).reshape(used_rows, source_width),
-        ((0, -used_rows % 16), (0, -source_width % 128)),
-    )
-    copies = jnp.broadcast_to(packed[None], (size,) + packed.shape)
-    received = lax.all_to_all(copies, "tm", 0, 0, tiled=True)
+    tail = ((0, 0), (0, -used_rows % 16), (0, -source_width % 128))
+    held = jnp.swapaxes(histories, 0, 1).reshape(1, used_rows, source_width)
+
+    step = 1
+    while step < size:
+        held = jnp.concatenate([held, swap(held, step, size)])
+        step *= 2
+    received = jnp.pad(held, tail)
 
     tiles = propagator.reshape(slot_count, source_width * months, cell_count)
+    blocks = tile_blocks.T
     vmem = pl.BlockSpec(memory_space=pltpu.VMEM)
+    smem = pl.BlockSpec(memory_space=pltpu.SMEM)
+    hbm = pl.BlockSpec(memory_space=pltpu.HBM)
+    blocks, tiles = pl.pallas_call(
+        stage,
+        out_shape=[
+            jax.ShapeDtypeStruct(blocks.shape, blocks.dtype),
+            jax.ShapeDtypeStruct(tiles.shape, tiles.dtype),
+        ],
+        in_specs=[hbm, hbm],
+        out_specs=[vmem, vmem],
+        scratch_shapes=[pltpu.SemaphoreType.DMA((2,))],
+        compiler_params=pltpu.CompilerParams(vmem_limit_bytes=16 * 1024 * 1024),
+        cost_estimate=pl.CostEstimate(flops=0, bytes_accessed=propagator.size * 4, transcendentals=0),
+    )(blocks, tiles)
+    me = lax.axis_index("tm").astype(jnp.int32)[None]
     partial_sums = pl.pallas_call(
         lambda *refs: tile_sums(months, *refs),
         out_shape=jax.ShapeDtypeStruct((block_count, height, cell_count), jnp.float32),
-        in_specs=[pl.BlockSpec(memory_space=pltpu.SMEM), vmem, vmem],
+        in_specs=[smem, smem, vmem, vmem],
         out_specs=vmem,
         scratch_shapes=[pltpu.VMEM((2, height, source_width * months), jnp.bfloat16)],
         compiler_params=pltpu.CompilerParams(vmem_limit_bytes=32 * 1024 * 1024),
@@ -81,7 +115,7 @@
             bytes_accessed=propagator.size * 2 + block_count * height * cell_count * 4,
             transcendentals=0,
         ),
-    )(tile_blocks.T, received, tiles)
+    )(me, blocks, received, tiles)
 
     exchanged = lax.all_to_all(partial_sums, "tm", 0, 0, tiled=True)
     owned = exchanged.reshape(size, own_blocks, height, cell_count).sum(0)

time: 31.9 us -> 31.8 us (level)
  blocking collectives: 27.2 us -> 15.4 us
  starting transfers between devices: 0 us -> 8.08 us
  waiting for transfers between devices: 0 us -> 3.56 us
  other arithmetic: 0.64 us -> 1.38 us
  local copies, waits for them, and re-layouts: 2.54 us -> 1.83 us
    all_to_all x1 -> x0, blocking collectives: 14 us -> none  [shards(): received = lax.all_to_all(copies, 'tm', 0, 0, tiled=True)]
    ppermute x0 -> x3, starting transfers between devices: none -> 8.08 us  [swap(): return lax.ppermute(value, 'tm', [(i, i ^ step) for i in range(size)])]
    ppermute x0 -> x3, waiting for transfers between devices: none -> 3.56 us  [swap(): return lax.ppermute(value, 'tm', [(i, i ^ step) for i in range(size)])]
    all_to_all x1, blocking collectives: 13.3 us -> 15.4 us  [shards(): exchanged = lax.all_to_all(partial_sums, 'tm', 0, 0, tiled=True)]
    concatenate x0 -> x3, other arithmetic: none -> 0.73 us  [shards(): held = jnp.concatenate([held, swap(held, step, size)])]
    pad x1 -> x0, local copies, waits for them, and re-layouts: 0.7 us -> none  [shards(): jnp.pad(jnp.swapaxes(histories, 0, 1).reshape(used_rows, source_width), (...]
    unnamed x4 -> x6, local copies, waits for them, and re-layouts: 1.83 us -> 1.83 us
  transfers between devices with their start and end apart: 0 -> 3, of which waited for: 0 -> 2; matrix products, arithmetic and copies ran while one was open for 0% -> 0% of each run, Pallas kernels for 0% -> 0%
where the time goes in v2:
time: 31.8 us; the launch traced here: 31.5 us
  blocking collectives  15.4 us (48%)
  starting transfers between devices  8.08 us (25%)
  waiting for transfers between devices  3.56 us (11%)
  local copies, waits for them, and re-layouts  1.83 us (6%)
  other arithmetic  1.38 us (4%)
  Pallas kernels  1.29 us (4%)
    all_to_all x1, blocking collectives, shards(): exchanged = lax.all_to_all(partial_sums, 'tm', 0, 0, tiled=True)  15.4 us
    ppermute x3, starting transfers between devices, swap(): return lax.ppermute(value, 'tm', [(i, i ^ step) for i in range(size)])  8.08 us
    ppermute x3, waiting for transfers between devices, swap(): return lax.ppermute(value, 'tm', [(i, i ^ step) for i in range(size)])  3.56 us
    unnamed x6, local copies, waits for them, and re-layouts  1.83 us
    pallas_call x1, Pallas kernels, shards(): pl.pallas_call(lambda *refs: tile_sums(months, *refs), out_shape=jax.Shap...  1.16 us
    concatenate x3, other arithmetic, shards(): held = jnp.concatenate([held, swap(held, step, size)])  0.73 us
    reduce_sum x1, other arithmetic, shards(): owned = exchanged.reshape(size, own_blocks, height, cell_count).sum(0)  0.64 us
  transfers between devices with their start and end apart: 3, of which 2 were waited for; matrix products, arithmetic and copies ran while one was open for 0% of the time, Pallas kernels for 0%

profile of v2, /device:TPU:0, one launch (start us, length us, event | category | flops | bytes accessed | tf_op | source)
XLA Modules:
  0.0 31.5 jit_solution(2522341531216655610)
XLA Ops:
  0.0 0.0 copy-start.2
  0.0 2.9 %collective-permute-start = (bf16[1,24,48]{2,1,0:T(8,128)(2,1)}, bf16[1,24,48]{2,1,0:T(8,128)(2,1)S(1)}, u32[]{:S(2)}, u32[]{:S(2)}) collective-permute-start(bf16[1,24,48]{2,1,0:T(8,128)(2,1)} %bitcast.11), channel_id=1, source_target_pairs={{0,2},{2,0},{4,6},{6,4},{8,10},{10,8},{12,14},{14,12},{1,3},{3,1},... | collective-permute-start | bytes 6920 | tf_op jit(solution)/shard_map/ppermute | solution.py:68
  2.9 1.9 %collective-permute-done = bf16[1,24,48]{2,1,0:T(8,128)(2,1)S(1)} collective-permute-done((bf16[1,24,48]{2,1,0:T(8,128)(2,1)}, bf16[1,24,48]{2,1,0:T(8,128)(2,1)S(1)}, u32[]{:S(2)}, u32[]{:S(2)}) %collective-permute-start) | collective-permute-done | bytes 2336 | tf_op jit(solution)/shard_map/ppermute | solution.py:68
  4.8 0.7 %pad_maximum_fusion.1 = bf16[2,24,48]{2,1,0:T(8,128)(2,1)S(1)} fusion(bf16[1,24,48]{2,1,0:T(8,128)(2,1)S(1)} %collective-permute-done, bf16[1,24,48]{2,1,0:T(8,128)(2,1)} %bitcast.12), kind=kLoop, calls=%fused_computation.15 | loop fusion | flops 2304 | bytes 9216 | tf_op jit(solution)/shard_map/concatenate | solution.py:84
  5.5 2.0 %collective-permute-start.1 = (bf16[2,24,48]{2,1,0:T(8,128)(2,1)S(1)}, bf16[2,24,48]{2,1,0:T(8,128)(2,1)S(1)}, u32[]{:S(2)}, u32[]{:S(2)}) collective-permute-start(bf16[2,24,48]{2,1,0:T(8,128)(2,1)S(1)} %pad_maximum_fusion.1), channel_id=1, source_target_pairs={{0,4},{2,6},{4,0},{6,2},{8,12},{10,14},{12,8},{14,10},{1,5},{3,7},... | collective-permute-start | bytes 13832 | tf_op jit(solution)/shard_map/ppermute | solution.py:68
  7.6 1.7 %collective-permute-done.1 = bf16[2,24,48]{2,1,0:T(8,128)(2,1)S(1)} collective-permute-done((bf16[2,24,48]{2,1,0:T(8,128)(2,1)S(1)}, bf16[2,24,48]{2,1,0:T(8,128)(2,1)S(1)}, u32[]{:S(2)}, u32[]{:S(2)}) %collective-permute-start.1) | collective-permute-done | bytes 4640 | tf_op jit(solution)/shard_map/ppermute | solution.py:68
  9.2 0.0 copy-done.2
  9.3 3.1 %collective-permute-start.2 = (bf16[4,24,48]{2,1,0:T(8,128)(2,1)S(1)}, bf16[4,24,48]{2,1,0:T(8,128)(2,1)S(1)}, u32[]{:S(2)}, u32[]{:S(2)}) collective-permute-start(bf16[4,24,48]{2,1,0:T(8,128)(2,1)S(1)} %pad_maximum_fusion), channel_id=1, source_target_pairs={{0,8},{2,10},{4,12},{6,14},{8,0},{10,2},{12,4},{14,6},{1,9},{3,11}... | collective-permute-start | bytes 27656 | tf_op jit(solution)/shard_map/ppermute | solution.py:68
  12.4 0.0 copy-start.1
  12.4 0.7 %copy-done.1 = s32[17,2]{0,1:T(2,128)S(1)} copy-done((s32[17,2]{0,1:T(2,128)S(1)}, s32[17,2]{0,1:T(2,128)}, u32[]{:S(2)}) %copy-start.1) | copy-done | bytes 160
  13.0 0.0 copy-start
  13.0 1.1 %copy-done = bf16[17,48,4,128]{3,2,1,0:T(4,128)(2,1)S(1)} copy-done((bf16[17,48,4,128]{3,2,1,0:T(4,128)(2,1)S(1)}, bf16[17,48,4,128]{3,2,1,0:T(4,128)(2,1)}, u32[]{:S(2)}) %copy-start) | copy-done | bytes 835608
  14.2 0.1 shard_map.37
  14.3 0.0 collective-permute-done.2
  14.4 1.2 %shard_map.38 = f32[16,48,128]{2,1,0:T(8,128)S(1)} custom-call(s32[1]{0:T(128)} %bitcast.refs_0_, s32[2,17]{1,0:T(2,128)S(1)} %get-tuple-element.7.refs_1_, bf16[8,32,128]{2,1,0:T(8,128)(2,1)S(1)} %fusion.8.refs_2_, bf16[17,192,128]{2,1,0:T(8,128)(2,1)S(1)} %get-tuple-element.8.refs_3_), custom_call_target="tpu_custom_call" | custom-call | flops 40108032 | bytes 1228800 | tf_op jit(solution)/shard_map/pallas_call | solution.py:106
  15.5 15.4 %all_to_all.5 = f32[16,48,128]{2,1,0:T(8,128)S(1)} all-to-all(f32[16,48,128]{2,1,0:T(8,128)S(1)} %shard_map.38), channel_id=1, replica_groups=mesh['groups'=2,'tm'=8,'cells'=2] {'tm'}, dimensions={0} | all-to-all | bytes 786432 | tf_op jit(solution)/shard_map/all_to_all | solution.py:120
  30.9 0.6 %reduce_sum.9 = f32[2,48,128]{2,1,0:T(8,128)} reduce(f32[8,2,48,128]{3,2,1,0:T(8,128)S(1)} %bitcast.10, f32[]{:T(128)} %constant.10.clone.1), dimensions={0}, to_apply=%region_0.1 | reduce | flops 86016 | bytes 442372 | tf_op jit(solution)/shard_map/reduce_sum | solution.py:121
  (2 shorter events, 0.0 us)
Async XLA Ops:
  0.0 9.2 %copy-start.2 = (bf16[2,12,48]{2,0,1:T(2,128)(2,1)S(1)}, bf16[2,12,48]{2,0,1:T(2,128)(2,1)}, u32[]{:S(2)}) copy-start(bf16[2,12,48]{2,0,1:T(2,128)(2,1)} %param.5) | copy-start | bytes 6916
  0.0 4.8 %collective-permute-start = (bf16[1,24,48]{2,1,0:T(8,128)(2,1)}, bf16[1,24,48]{2,1,0:T(8,128)(2,1)S(1)}, u32[]{:S(2)}, u32[]{:S(2)}) collective-permute-start(bf16[1,24,48]{2,1,0:T(8,128)(2,1)} %bitcast.11), channel_id=1, source_target_pairs={{0,2},{2,0},{4,6},{6,4},{8,10},{10,8},{12,14},{14,12},{1,3},{3,1},... | collective-permute-start | bytes 6920 | tf_op jit(solution)/shard_map/ppermute | solution.py:68
  5.5 3.7 %collective-permute-start.1 = (bf16[2,24,48]{2,1,0:T(8,128)(2,1)S(1)}, bf16[2,24,48]{2,1,0:T(8,128)(2,1)S(1)}, u32[]{:S(2)}, u32[]{:S(2)}) collective-permute-start(bf16[2,24,48]{2,1,0:T(8,128)(2,1)S(1)} %pad_maximum_fusion.1), channel_id=1, source_target_pairs={{0,4},{2,6},{4,0},{6,2},{8,12},{10,14},{12,8},{14,10},{1,5},{3,7},... | collective-permute-start | bytes 13832 | tf_op jit(solution)/shard_map/ppermute | solution.py:68
  9.3 5.1 %collective-permute-start.2 = (bf16[4,24,48]{2,1,0:T(8,128)(2,1)S(1)}, bf16[4,24,48]{2,1,0:T(8,128)(2,1)S(1)}, u32[]{:S(2)}, u32[]{:S(2)}) collective-permute-start(bf16[4,24,48]{2,1,0:T(8,128)(2,1)S(1)} %pad_maximum_fusion), channel_id=1, source_target_pairs={{0,8},{2,10},{4,12},{6,14},{8,0},{10,2},{12,4},{14,6},{1,9},{3,11}... | collective-permute-start | bytes 27656 | tf_op jit(solution)/shard_map/ppermute | solution.py:68
  12.4 0.7 %copy-start.1 = (s32[17,2]{0,1:T(2,128)S(1)}, s32[17,2]{0,1:T(2,128)}, u32[]{:S(2)}) copy-start(s32[17,2]{0,1:T(2,128)} %param.4) | copy-start | bytes 412
  13.0 1.1 %copy-start = (bf16[17,48,4,128]{3,2,1,0:T(4,128)(2,1)S(1)}, bf16[17,48,4,128]{3,2,1,0:T(4,128)(2,1)}, u32[]{:S(2)}) copy-start(bf16[17,48,4,128]{3,2,1,0:T(4,128)(2,1)} %param.3) | copy-start | bytes 2506756

commit v3 on v2

--- a/solution.py
+++ b/solution.py
@@ -6,9 +6,8 @@
 from jax.sharding import PartitionSpec as P
 
 
-def tile_sums(months, me_ref, blocks_ref, histories_ref, tiles_ref, sums_ref, wide_ref):
+def tile_sums(months, blocks_ref, histories_ref, tiles_ref, sums_ref, wide_ref):
     size, packed_rows, packed_width = histories_ref.shape
-    me = me_ref[0]
     slot_count, tile_height, cell_count = tiles_ref.shape
     block_count, height, cell_count = sums_ref.shape
     own_blocks = block_count // size
@@ -25,7 +24,7 @@
     for which, source in enumerate((first, block_count - 1 - first)):
         repeat_rows = (row_of + source % own_blocks == packed_row).astype(jnp.bfloat16)
         tall = jnp.dot(
-            repeat_rows, histories_ref[(source // own_blocks) ^ me], preferred_element_type=jnp.float32
+            repeat_rows, histories_ref[source // own_blocks], preferred_element_type=jnp.float32
         )
         wide = jnp.dot(tall.astype(jnp.bfloat16), repeat_columns, preferred_element_type=jnp.float32)
         wide_ref[which] = jnp.where(same_month, wide, 0.0).astype(jnp.bfloat16)
@@ -64,10 +63,6 @@
         copy.wait()
 
 
-def swap(value, step, size):
-    return lax.ppermute(value, "tm", [(i, i ^ step) for i in range(size)])
-
-
 def shards(propagator, tile_blocks, histories):
     size = lax.axis_size("tm")
     own_blocks, tracer_count, source_width = histories.shape
@@ -76,14 +71,12 @@
     height = tracer_count * months
 
     used_rows = tracer_count * own_blocks
-    tail = ((0, 0), (0, -used_rows % 16), (0, -source_width % 128))
-    held = jnp.swapaxes(histories, 0, 1).reshape(1, used_rows, source_width)
-
-    step = 1
-    while step < size:
-        held = jnp.concatenate([held, swap(held, step, size)])
-        step *= 2
-    received = jnp.pad(held, tail)
+    packed = jnp.pad(
+        jnp.swapaxes(histories, 0, 1).reshape(used_rows, source_width),
+        ((0, -used_rows % 16), (0, -source_width % 128)),
+    )
+    copies = jnp.broadcast_to(packed[None], (size,) + packed.shape)
+    received = lax.all_to_all(copies, "tm", 0, 0, tiled=True)
 
     tiles = propagator.reshape(slot_count, source_width * months, cell_count)
     blocks = tile_blocks.T
@@ -102,11 +95,10 @@
         compiler_params=pltpu.CompilerParams(vmem_limit_bytes=16 * 1024 * 1024),
         cost_estimate=pl.CostEstimate(flops=0, bytes_accessed=propagator.size * 4, transcendentals=0),
     )(blocks, tiles)
-    me = lax.axis_index("tm").astype(jnp.int32)[None]
     partial_sums = pl.pallas_call(
         lambda *refs: tile_sums(months, *refs),
         out_shape=jax.ShapeDtypeStruct((block_count, height, cell_count), jnp.float32),
-        in_specs=[smem, smem, vmem, vmem],
+        in_specs=[smem, vmem, vmem],
         out_specs=vmem,
         scratch_shapes=[pltpu.VMEM((2, height, source_width * months), jnp.bfloat16)],
         compiler_params=pltpu.CompilerParams(vmem_limit_bytes=32 * 1024 * 1024),
@@ -115,7 +107,7 @@
             bytes_accessed=propagator.size * 2 + block_count * height * cell_count * 4,
             transcendentals=0,
         ),
-    )(me, blocks, received, tiles)
+    )(blocks, received, tiles)
 
     exchanged = lax.all_to_all(partial_sums, "tm", 0, 0, tiled=True)
     owned = exchanged.reshape(size, own_blocks, height, cell_count).sum(0)

time: 31.8 us -> 30.9 us (0.972)
  blocking collectives: 15.4 us -> 13.3 us
  waiting for transfers between devices: 3.56 us -> 4.93 us
  local copies, waits for them, and re-layouts: 1.83 us -> 3.15 us
  starting transfers between devices: 8.08 us -> 7.25 us
  other arithmetic: 1.38 us -> 0.64 us
    ppermute x3 -> x0, starting transfers between devices: 8.08 us -> none  [swap(): return lax.ppermute(value, 'tm', [(i, i ^ step) for i in range(size)])]
    all_to_all x0 -> x1, starting transfers between devices: none -> 7.25 us  [shards(): received = lax.all_to_all(copies, 'tm', 0, 0, tiled=True)]
    all_to_all x0 -> x1, waiting for transfers between devices: none -> 4.93 us  [shards(): received = lax.all_to_all(copies, 'tm', 0, 0, tiled=True)]
    ppermute x3 -> x0, waiting for transfers between devices: 3.56 us -> none  [swap(): return lax.ppermute(value, 'tm', [(i, i ^ step) for i in range(size)])]
    all_to_all x1, blocking collectives: 15.4 us -> 13.3 us  [shards(): exchanged = lax.all_to_all(partial_sums, 'tm', 0, 0, tiled=True)]
    concatenate x3 -> x0, other arithmetic: 0.73 us -> none  [shards(): held = jnp.concatenate([held, swap(held, step, size)])]
    pad x0 -> x1, local copies, waits for them, and re-layouts: none -> 0.7 us  [shards(): jnp.pad(jnp.swapaxes(histories, 0, 1).reshape(used_rows, source_width), (...]
    broadcast_in_dim x0 -> x1, local copies, waits for them, and re-layouts: none -> 0.62 us  [shards(): copies = jnp.broadcast_to(packed[None], (size,) + packed.shape)]
  transfers between devices with their start and end apart: 3 -> 1, of which waited for: 2 -> 1; matrix products, arithmetic and copies ran while one was open for 0% -> 0% of each run, Pallas kernels for 0% -> 0%
where the time goes in v3:
time: 30.9 us; the launch traced here: 30.6 us
  blocking collectives  13.3 us (43%)
  starting transfers between devices  7.25 us (23%)
  waiting for transfers between devices  4.93 us (16%)
  local copies, waits for them, and re-layouts  3.15 us (10%)
  Pallas kernels  1.28 us (4%)
  other arithmetic  0.64 us (2%)
    all_to_all x1, blocking collectives, shards(): exchanged = lax.all_to_all(partial_sums, 'tm', 0, 0, tiled=True)  13.3 us
    all_to_all x1, starting transfers between devices, shards(): received = lax.all_to_all(copies, 'tm', 0, 0, tiled=True)  7.25 us
    all_to_all x1, waiting for transfers between devices, shards(): received = lax.all_to_all(copies, 'tm', 0, 0, tiled=True)  4.93 us
    unnamed x4, local copies, waits for them, and re-layouts  1.83 us
    pallas_call x1, Pallas kernels, shards(): pl.pallas_call(lambda *refs: tile_sums(months, *refs), out_shape=jax.Shap...  1.15 us
    pad x1, local copies, waits for them, and re-layouts, shards(): jnp.pad(jnp.swapaxes(histories, 0, 1).reshape(used_rows, source_width), (...  0.7 us
    reduce_sum x1, other arithmetic, shards(): owned = exchanged.reshape(size, own_blocks, height, cell_count).sum(0)  0.64 us
    broadcast_in_dim x1, local copies, waits for them, and re-layouts, shards(): copies = jnp.broadcast_to(packed[None], (size,) + packed.shape)  0.62 us
  transfers between devices with their start and end apart: 1, of which 1 were waited for; matrix products, arithmetic and copies ran while one was open for 0% of the time, Pallas kernels for 0%

profile of v3, /device:TPU:0, one launch (start us, length us, event | category | flops | bytes accessed | tf_op | source)
XLA Modules:
  0.0 30.6 jit_solution(8864319020636421756)
XLA Ops:
  0.0 0.7 %pad.4 = bf16[32,128]{1,0:T(8,128)(2,1)S(1)} pad(bf16[24,48]{1,0:T(8,128)(2,1)} %bitcast.10, bf16[]{:T(256)} %constant.1.clone.1), padding=0_8x0_80 | pad | bytes 10498 | tf_op jit(solution)/shard_map/jit(_pad)/pad | solution.py:74
  0.7 0.6 %broadcast_in_dim.2 = bf16[8,32,128]{2,1,0:T(8,128)(2,1)} broadcast(bf16[32,128]{1,0:T(8,128)(2,1)S(1)} %pad.4), dimensions={1,2} | broadcast | bytes 73728 | tf_op jit(solution)/shard_map/broadcast_in_dim | solution.py:78
  1.3 7.3 %all-to-all-start = ((bf16[8,32,128]{2,1,0:T(8,128)(2,1)}), bf16[8,32,128]{2,1,0:T(8,128)(2,1)S(1)}, u32[]{:S(2)}, u32[]{:S(2)}) async-start(bf16[8,32,128]{2,1,0:T(8,128)(2,1)} %broadcast_in_dim.2), calls=%async_computation | async-start | bytes 131072 | tf_op jit(solution)/shard_map/all_to_all | solution.py:79
  8.6 0.0 copy-start.1
  8.6 0.7 %copy-done.1 = s32[17,2]{0,1:T(2,128)S(1)} copy-done((s32[17,2]{0,1:T(2,128)S(1)}, s32[17,2]{0,1:T(2,128)}, u32[]{:S(2)}) %copy-start.1) | copy-done | bytes 160
  9.3 0.0 copy-start
  9.3 1.1 %copy-done = bf16[17,48,4,128]{3,2,1,0:T(4,128)(2,1)S(1)} copy-done((bf16[17,48,4,128]{3,2,1,0:T(4,128)(2,1)S(1)}, bf16[17,48,4,128]{3,2,1,0:T(4,128)(2,1)}, u32[]{:S(2)}) %copy-start) | copy-done | bytes 835608
  10.4 0.1 shard_map.37
  10.5 4.9 %all-to-all-done.refs_1_ = bf16[8,32,128]{2,1,0:T(8,128)(2,1)S(1)} async-done(((bf16[8,32,128]{2,1,0:T(8,128)(2,1)}), bf16[8,32,128]{2,1,0:T(8,128)(2,1)S(1)}, u32[]{:S(2)}, u32[]{:S(2)}) %all-to-all-start) | async-done | bytes 65568 | tf_op jit(solution)/shard_map/all_to_all | solution.py:79
  15.5 1.1 %shard_map.38 = f32[16,48,128]{2,1,0:T(8,128)S(1)} custom-call(s32[2,17]{1,0:T(2,128)S(1)} %get-tuple-element.7.refs_0_, bf16[8,32,128]{2,1,0:T(8,128)(2,1)S(1)} %all-to-all-done.refs_1_, bf16[17,192,128]{2,1,0:T(8,128)(2,1)S(1)} %get-tuple-element.8.refs_2_), custom_call_target="tpu_custom_call" | custom-call | flops 40108032 | bytes 1228800 | tf_op jit(solution)/shard_map/pallas_call | solution.py:98
  16.6 13.3 %all_to_all.10 = f32[16,48,128]{2,1,0:T(8,128)S(1)} all-to-all(f32[16,48,128]{2,1,0:T(8,128)S(1)} %shard_map.38), channel_id=1, replica_groups=mesh['groups'=2,'tm'=8,'cells'=2] {'tm'}, dimensions={0} | all-to-all | bytes 786432 | tf_op jit(solution)/shard_map/all_to_all | solution.py:112
  29.9 0.6 %reduce_sum.9 = f32[2,48,128]{2,1,0:T(8,128)} reduce(f32[8,2,48,128]{3,2,1,0:T(8,128)S(1)} %bitcast.9, f32[]{:T(128)} %constant.4.clone.1), dimensions={0}, to_apply=%region_0.1 | reduce | flops 86016 | bytes 442372 | tf_op jit(solution)/shard_map/reduce_sum | solution.py:113
Async XLA Ops:
  1.3 14.2 %all-to-all-start = ((bf16[8,32,128]{2,1,0:T(8,128)(2,1)}), bf16[8,32,128]{2,1,0:T(8,128)(2,1)S(1)}, u32[]{:S(2)}, u32[]{:S(2)}) async-start(bf16[8,32,128]{2,1,0:T(8,128)(2,1)} %broadcast_in_dim.2), calls=%async_computation | async-start | bytes 131072 | tf_op jit(solution)/shard_map/all_to_all | solution.py:79
  8.6 0.7 %copy-start.1 = (s32[17,2]{0,1:T(2,128)S(1)}, s32[17,2]{0,1:T(2,128)}, u32[]{:S(2)}) copy-start(s32[17,2]{0,1:T(2,128)} %param.4) | copy-start | bytes 412
  9.3 1.1 %copy-start = (bf16[17,48,4,128]{3,2,1,0:T(4,128)(2,1)S(1)}, bf16[17,48,4,128]{3,2,1,0:T(4,128)(2,1)}, u32[]{:S(2)}) copy-start(bf16[17,48,4,128]{3,2,1,0:T(4,128)(2,1)} %param.3) | copy-start | bytes 2506756

commit v4 on v3

--- a/solution.py
+++ b/solution.py
@@ -24,7 +24,7 @@
     for which, source in enumerate((first, block_count - 1 - first)):
         repeat_rows = (row_of + source % own_blocks == packed_row).astype(jnp.bfloat16)
         tall = jnp.dot(
-            repeat_rows, histories_ref[source // own_blocks], preferred_element_type=jnp.float32
+            repeat_rows, histories_ref[size - 1 - source // own_blocks], preferred_element_type=jnp.float32
         )
         wide = jnp.dot(tall.astype(jnp.bfloat16), repeat_columns, preferred_element_type=jnp.float32)
         wide_ref[which] = jnp.where(same_month, wide, 0.0).astype(jnp.bfloat16)
@@ -34,7 +34,8 @@
     def add_tile(slot):
         which = (blocks_ref[0, slot] != first).astype(jnp.int32)
         arrival = blocks_ref[1, slot]
-        sums_ref[arrival] += jnp.dot(wide_ref[which], tiles_ref[slot], preferred_element_type=jnp.float32)
+        place = (size - 1 - arrival // own_blocks) * own_blocks + arrival % own_blocks
+        sums_ref[place] += jnp.dot(wide_ref[which], tiles_ref[slot], preferred_element_type=jnp.float32)
 
     unrolled = 17
     rounds = slot_count // unrolled
@@ -63,6 +64,12 @@
         copy.wait()
 
 
+def exchange(value, size):
+    return lax.all_to_all(
+        value, "tm", 0, 0, axis_index_groups=[list(range(size - 1, -1, -1))], tiled=True
+    )
+
+
 def shards(propagator, tile_blocks, histories):
     size = lax.axis_size("tm")
     own_blocks, tracer_count, source_width = histories.shape
@@ -71,12 +78,12 @@
     height = tracer_count * months
 
     used_rows = tracer_count * own_blocks
-    packed = jnp.pad(
-        jnp.swapaxes(histories, 0, 1).reshape(used_rows, source_width),
-        ((0, -used_rows % 16), (0, -source_width % 128)),
+    rows = jnp.swapaxes(histories, 0, 1).reshape(1, used_rows, source_width)
+    copies = jnp.pad(
+        jnp.broadcast_to(rows, (size, used_rows, source_width)),
+        ((0, 0), (0, -used_rows % 16), (0, -source_width % 128)),
     )
-    copies = jnp.broadcast_to(packed[None], (size,) + packed.shape)
-    received = lax.all_to_all(copies, "tm", 0, 0, tiled=True)
+    received = exchange(copies, size)
 
     tiles = propagator.reshape(slot_count, source_width * months, cell_count)
     blocks = tile_blocks.T
@@ -109,7 +116,7 @@
         ),
     )(blocks, received, tiles)
 
-    exchanged = lax.all_to_all(partial_sums, "tm", 0, 0, tiled=True)
+    exchanged = exchange(partial_sums, size)
     owned = exchanged.reshape(size, own_blocks, height, cell_count).sum(0)
     return owned.reshape(own_blocks, tracer_count, months, cell_count)
 

time: 30.9 us -> 30.4 us (0.984)
  waiting for transfers between devices: 4.93 us -> 1 us
  starting transfers between devices: 7.25 us -> 9.27 us
  blocking collectives: 13.3 us -> 14.8 us
    all_to_all x1, waiting for transfers between devices: 4.93 us -> 1 us  [exchange(): lax.all_to_all(value, 'tm', 0, 0, axis_index_groups=[list(range(size - 1,...]
    all_to_all x1, starting transfers between devices: 7.25 us -> 9.27 us  [exchange(): lax.all_to_all(value, 'tm', 0, 0, axis_index_groups=[list(range(size - 1,...]
    all_to_all x1, blocking collectives: 13.3 us -> 14.8 us  [exchange(): lax.all_to_all(value, 'tm', 0, 0, axis_index_groups=[list(range(size - 1,...]
    broadcast_in_dim x1 -> x0, local copies, waits for them, and re-layouts: 0.62 us -> none  [shards(): copies = jnp.broadcast_to(packed[None], (size,) + packed.shape)]
    pad x1 -> x2, local copies, waits for them, and re-layouts: 0.7 us -> 1.32 us  [shards(): jnp.pad(jnp.broadcast_to(rows, (size, used_rows, source_width)), ((0, 0),...]
where the time goes in v4:
time: 30.4 us; the launch traced here: 30.1 us
  blocking collectives  14.8 us (49%)
  starting transfers between devices  9.27 us (30%)
  local copies, waits for them, and re-layouts  3.15 us (10%)
  Pallas kernels  1.28 us (4%)
  waiting for transfers between devices  1 us (3%)
  other arithmetic  0.64 us (2%)
    all_to_all x1, blocking collectives, exchange(): lax.all_to_all(value, 'tm', 0, 0, axis_index_groups=[list(range(size - 1,...  14.8 us
    all_to_all x1, starting transfers between devices, exchange(): lax.all_to_all(value, 'tm', 0, 0, axis_index_groups=[list(range(size - 1,...  9.27 us
    unnamed x4, local copies, waits for them, and re-layouts  1.83 us
    pad x2, local copies, waits for them, and re-layouts, shards(): jnp.pad(jnp.broadcast_to(rows, (size, used_rows, source_width)), ((0, 0),...  1.32 us
    pallas_call x1, Pallas kernels, shards(): pl.pallas_call(lambda *refs: tile_sums(months, *refs), out_shape=jax.Shap...  1.15 us
    all_to_all x1, waiting for transfers between devices, exchange(): lax.all_to_all(value, 'tm', 0, 0, axis_index_groups=[list(range(size - 1,...  1 us
    reduce_sum x1, other arithmetic, shards(): owned = exchanged.reshape(size, own_blocks, height, cell_count).sum(0)  0.64 us
  transfers between devices with their start and end apart: 1, of which 1 were waited for; matrix products, arithmetic and copies ran while one was open for 0% of the time, Pallas kernels for 0%

profile of v4, /device:TPU:0, one launch (start us, length us, event | category | flops | bytes accessed | tf_op | source)
XLA Modules:
  0.0 30.1 jit_solution(6291902991550359650)
XLA Ops:
  0.0 0.7 %pad.6 = bf16[32,128]{1,0:T(8,128)(2,1)S(1)} pad(bf16[24,48]{1,0:T(8,128)(2,1)} %bitcast.10, bf16[]{:T(256)} %constant.1.clone.1), padding=0_8x0_80 | pad | bytes 10498 | tf_op jit(solution)/shard_map/jit(_pad)/pad | solution.py:82
  0.7 0.6 %pad.7 = bf16[8,32,128]{2,1,0:T(8,128)(2,1)} broadcast(bf16[32,128]{1,0:T(8,128)(2,1)S(1)} %pad.6), dimensions={1,2} | broadcast | bytes 73728 | tf_op jit(solution)/shard_map/jit(_pad)/pad | solution.py:82
  1.3 9.3 %all-to-all-start = ((bf16[8,32,128]{2,1,0:T(8,128)(2,1)}), bf16[8,32,128]{2,1,0:T(8,128)(2,1)S(1)}, u32[]{:S(2)}, u32[]{:S(2)}) async-start(bf16[8,32,128]{2,1,0:T(8,128)(2,1)} %pad.7), calls=%async_computation | async-start | bytes 131072 | tf_op jit(solution)/shard_map/all_to_all | solution.py:68
  10.6 0.0 copy-start.1
  10.6 0.7 %copy-done.1 = s32[17,2]{0,1:T(2,128)S(1)} copy-done((s32[17,2]{0,1:T(2,128)S(1)}, s32[17,2]{0,1:T(2,128)}, u32[]{:S(2)}) %copy-start.1) | copy-done | bytes 160
  11.3 0.0 copy-start
  11.3 1.1 %copy-done = bf16[17,48,4,128]{3,2,1,0:T(4,128)(2,1)S(1)} copy-done((bf16[17,48,4,128]{3,2,1,0:T(4,128)(2,1)S(1)}, bf16[17,48,4,128]{3,2,1,0:T(4,128)(2,1)}, u32[]{:S(2)}) %copy-start) | copy-done | bytes 835608
  12.4 0.1 shard_map.37
  12.6 1.0 %all-to-all-done.refs_1_ = bf16[8,32,128]{2,1,0:T(8,128)(2,1)S(1)} async-done(((bf16[8,32,128]{2,1,0:T(8,128)(2,1)}), bf16[8,32,128]{2,1,0:T(8,128)(2,1)S(1)}, u32[]{:S(2)}, u32[]{:S(2)}) %all-to-all-start) | async-done | bytes 65568 | tf_op jit(solution)/shard_map/all_to_all | solution.py:68
  13.6 1.1 %shard_map.38 = f32[16,48,128]{2,1,0:T(8,128)S(1)} custom-call(s32[2,17]{1,0:T(2,128)S(1)} %get-tuple-element.7.refs_0_, bf16[8,32,128]{2,1,0:T(8,128)(2,1)S(1)} %all-to-all-done.refs_1_, bf16[17,192,128]{2,1,0:T(8,128)(2,1)S(1)} %get-tuple-element.8.refs_2_), custom_call_target="tpu_custom_call" | custom-call | flops 40108032 | bytes 1228800 | tf_op jit(solution)/shard_map/pallas_call | solution.py:105
  14.7 14.8 %all_to_all.10 = f32[16,48,128]{2,1,0:T(8,128)S(1)} all-to-all(f32[16,48,128]{2,1,0:T(8,128)S(1)} %shard_map.38), channel_id=1, replica_groups={{14,12,10,8,6,4,2,0},{15,13,11,9,7,5,3,1},{30,28,26,24,22,20,18,16},{31..., dimensions={0} | all-to-all | bytes 786432 | tf_op jit(solution)/shard_map/all_to_all | solution.py:68
  29.5 0.6 %reduce_sum.9 = f32[2,48,128]{2,1,0:T(8,128)} reduce(f32[8,2,48,128]{3,2,1,0:T(8,128)S(1)} %bitcast.9, f32[]{:T(128)} %constant.4.clone.1), dimensions={0}, to_apply=%region_0.1 | reduce | flops 86016 | bytes 442372 | tf_op jit(solution)/shard_map/reduce_sum | solution.py:120
Async XLA Ops:
  1.3 12.2 %all-to-all-start = ((bf16[8,32,128]{2,1,0:T(8,128)(2,1)}), bf16[8,32,128]{2,1,0:T(8,128)(2,1)S(1)}, u32[]{:S(2)}, u32[]{:S(2)}) async-start(bf16[8,32,128]{2,1,0:T(8,128)(2,1)} %pad.7), calls=%async_computation | async-start | bytes 131072 | tf_op jit(solution)/shard_map/all_to_all | solution.py:68
  10.6 0.7 %copy-start.1 = (s32[17,2]{0,1:T(2,128)S(1)}, s32[17,2]{0,1:T(2,128)}, u32[]{:S(2)}) copy-start(s32[17,2]{0,1:T(2,128)} %param.4) | copy-start | bytes 412
  11.3 1.1 %copy-start = (bf16[17,48,4,128]{3,2,1,0:T(4,128)(2,1)S(1)}, bf16[17,48,4,128]{3,2,1,0:T(4,128)(2,1)}, u32[]{:S(2)}) copy-start(bf16[17,48,4,128]{3,2,1,0:T(4,128)(2,1)} %param.3) | copy-start | bytes 2506756

commit v5 on v4

--- a/solution.py
+++ b/solution.py
@@ -1,3 +1,5 @@
+import functools
+
 import jax
 import jax.numpy as jnp
 from jax import lax
@@ -5,11 +7,16 @@
 from jax.experimental.pallas import tpu as pltpu
 from jax.sharding import PartitionSpec as P
 
+STEPS = 32700.0
+LEVELS = 128
+SMALLEST = 2.0**-126
 
-def tile_sums(months, blocks_ref, histories_ref, tiles_ref, sums_ref, wide_ref):
-    size, packed_rows, packed_width = histories_ref.shape
+
+def tile_sums(months, blocks_ref, histories_ref, tiles_ref, coded_ref, wide_ref, sums_ref):
+    packed_rows, packed_width = histories_ref.shape[1:]
     slot_count, tile_height, cell_count = tiles_ref.shape
     block_count, height, cell_count = sums_ref.shape
+    size = coded_ref.shape[0]
     own_blocks = block_count // size
 
     first = blocks_ref[0, 0]
@@ -51,6 +58,39 @@
         lax.fori_loop(0, rounds, add_round, 0)
     for slot in range(rounds * unrolled, slot_count):
         add_tile(slot)
+
+    coded_rows = own_blocks * height
+
+    def code(slot, carry):
+        blocks = [sums_ref[slot * own_blocks + block] for block in range(own_blocks)]
+        top = jnp.max(functools.reduce(jnp.maximum, map(jnp.abs, blocks)), axis=0, keepdims=True)
+        level = jnp.ceil(jnp.log2(jnp.maximum(top, SMALLEST)) * LEVELS)
+        half = jnp.exp2(level * (-0.5 / LEVELS))
+        for block, value in enumerate(blocks):
+            steps = jnp.round(value * half * (half * STEPS))
+            coded_ref[slot, pl.ds(block * height, height)] = steps.astype(jnp.int32).astype(jnp.int16)
+        spread = jnp.broadcast_to(level.astype(jnp.int32), (16, cell_count))
+        coded_ref[slot, pl.ds(coded_rows, 16)] = spread.astype(jnp.int16)
+        return carry
+
+    lax.fori_loop(0, size, code, 0, unroll=size <= 8)
+
+
+def add_parts(coded_ref, total_ref):
+    size = coded_ref.shape[0]
+    own_blocks, height, cell_count = total_ref.shape
+    coded_rows = own_blocks * height
+    total_ref[...] = jnp.zeros(total_ref.shape, total_ref.dtype)
+
+    def add(slot, carry):
+        level = coded_ref[slot, pl.ds(coded_rows, 16)].astype(jnp.int32).astype(jnp.float32)[:1]
+        half = jnp.exp2(level * (0.5 / LEVELS))
+        for block in range(own_blocks):
+            steps = coded_ref[slot, pl.ds(block * height, height)].astype(jnp.int32)
+            total_ref[block] += steps.astype(jnp.float32) * (half * (1.0 / STEPS)) * half
+        return carry
+
+    lax.fori_loop(0, size, add, 0, unroll=size <= 8)
 
 
 def stage(blocks_in, tiles_in, blocks_out, tiles_out, semaphores):
@@ -102,12 +142,15 @@
         compiler_params=pltpu.CompilerParams(vmem_limit_bytes=16 * 1024 * 1024),
         cost_estimate=pl.CostEstimate(flops=0, bytes_accessed=propagator.size * 4, transcendentals=0),
     )(blocks, tiles)
-    partial_sums = pl.pallas_call(
+    coded = pl.pallas_call(
         lambda *refs: tile_sums(months, *refs),
-        out_shape=jax.ShapeDtypeStruct((block_count, height, cell_count), jnp.float32),
+        out_shape=jax.ShapeDtypeStruct((size, own_blocks * height + 16, cell_count), jnp.int16),
         in_specs=[smem, vmem, vmem],
         out_specs=vmem,
-        scratch_shapes=[pltpu.VMEM((2, height, source_width * months), jnp.bfloat16)],
+        scratch_shapes=[
+            pltpu.VMEM((2, height, source_width * months), jnp.bfloat16),
+            pltpu.VMEM((block_count, height, cell_count), jnp.float32),
+        ],
         compiler_params=pltpu.CompilerParams(vmem_limit_bytes=32 * 1024 * 1024),
         cost_estimate=pl.CostEstimate(
             flops=2 * slot_count * height * source_width * months * cell_count,
@@ -116,8 +159,13 @@
         ),
     )(blocks, received, tiles)
 
-    exchanged = exchange(partial_sums, size)
-    owned = exchanged.reshape(size, own_blocks, height, cell_count).sum(0)
+    owned = pl.pallas_call(
+        add_parts,
+        out_shape=jax.ShapeDtypeStruct((own_blocks, height, cell_count), jnp.float32),
+        in_specs=[vmem],
+        out_specs=vmem,
+        compiler_params=pltpu.CompilerParams(vmem_limit_bytes=16 * 1024 * 1024),
+    )(exchange(coded, size))
     return owned.reshape(own_blocks, tracer_count, months, cell_count)
 
 

time: 30.4 us -> 27.2 us (0.89)
  blocking collectives: 14.8 us -> 11.3 us
  Pallas kernels: 1.28 us -> 2.07 us
  other arithmetic: 0.64 us -> 0 us
    all_to_all x1, blocking collectives: 14.8 us -> 11.3 us  [exchange(): lax.all_to_all(value, 'tm', 0, 0, axis_index_groups=[list(range(size - 1,...]
    pallas_call x0 -> x1, Pallas kernels: none -> 0.69 us  [shards(): pl.pallas_call(add_parts, out_shape=jax.ShapeDtypeStruct((own_blocks, hei...]
    reduce_sum x1 -> x0, other arithmetic: 0.64 us -> none  [shards(): owned = exchanged.reshape(size, own_blocks, height, cell_count).sum(0)]
  transfers between devices with their start and end apart: 1 -> 1, of which waited for: 1 -> 1; matrix products, arithmetic and copies ran while one was open for 0% -> 0% of each run, Pallas kernels for 0% -> 1%
where the time goes in v5:
time: 27.2 us; the launch traced here: 26.8 us
  blocking collectives  11.3 us (42%)
  starting transfers between devices  9.27 us (34%)
  local copies, waits for them, and re-layouts  3.16 us (12%)
  Pallas kernels  2.07 us (8%)
  waiting for transfers between devices  1 us (4%)
    all_to_all x1, blocking collectives, exchange(): lax.all_to_all(value, 'tm', 0, 0, axis_index_groups=[list(range(size - 1,...  11.3 us
    all_to_all x1, starting transfers between devices, exchange(): lax.all_to_all(value, 'tm', 0, 0, axis_index_groups=[list(range(size - 1,...  9.27 us
    unnamed x4, local copies, waits for them, and re-layouts  1.83 us
    pad x2, local copies, waits for them, and re-layouts, shards(): jnp.pad(jnp.broadcast_to(rows, (size, used_rows, source_width)), ((0, 0),...  1.33 us
    pallas_call x1, Pallas kernels, shards(): pl.pallas_call(lambda *refs: tile_sums(months, *refs), out_shape=jax.Shap...  1.25 us
    all_to_all x1, waiting for transfers between devices, exchange(): lax.all_to_all(value, 'tm', 0, 0, axis_index_groups=[list(range(size - 1,...  1 us
    pallas_call x1, Pallas kernels, shards(): pl.pallas_call(add_parts, out_shape=jax.ShapeDtypeStruct((own_blocks, hei...  0.69 us
  transfers between devices with their start and end apart: 1, of which 1 were waited for; matrix products, arithmetic and copies ran while one was open for 0% of the time, Pallas kernels for 1%

profile of v5, /device:TPU:0, one launch (start us, length us, event | category | flops | bytes accessed | tf_op | source)
XLA Modules:
  0.0 26.8 jit_solution(10009578100571767841)
XLA Ops:
  0.0 0.7 %pad.6 = bf16[32,128]{1,0:T(8,128)(2,1)S(1)} pad(bf16[24,48]{1,0:T(8,128)(2,1)} %bitcast.8, bf16[]{:T(256)} %constant.2.clone.1), padding=0_8x0_80 | pad | bytes 10498 | tf_op jit(solution)/shard_map/jit(_pad)/pad | solution.py:122
  0.7 0.6 %pad.7 = bf16[8,32,128]{2,1,0:T(8,128)(2,1)} broadcast(bf16[32,128]{1,0:T(8,128)(2,1)S(1)} %pad.6), dimensions={1,2} | broadcast | bytes 73728 | tf_op jit(solution)/shard_map/jit(_pad)/pad | solution.py:122
  1.3 9.3 %all-to-all-start = ((bf16[8,32,128]{2,1,0:T(8,128)(2,1)}), bf16[8,32,128]{2,1,0:T(8,128)(2,1)S(1)}, u32[]{:S(2)}, u32[]{:S(2)}) async-start(bf16[8,32,128]{2,1,0:T(8,128)(2,1)} %pad.7), calls=%async_computation | async-start | bytes 131072 | tf_op jit(solution)/shard_map/all_to_all | solution.py:108
  10.6 0.0 copy-start.1
  10.6 0.7 %copy-done.1 = s32[17,2]{0,1:T(2,128)S(1)} copy-done((s32[17,2]{0,1:T(2,128)S(1)}, s32[17,2]{0,1:T(2,128)}, u32[]{:S(2)}) %copy-start.1) | copy-done | bytes 160
  11.3 0.0 copy-start
  11.3 1.1 %copy-done = bf16[17,48,4,128]{3,2,1,0:T(4,128)(2,1)S(1)} copy-done((bf16[17,48,4,128]{3,2,1,0:T(4,128)(2,1)S(1)}, bf16[17,48,4,128]{3,2,1,0:T(4,128)(2,1)}, u32[]{:S(2)}) %copy-start) | copy-done | bytes 835608
  12.4 0.1 shard_map.37
  12.6 1.0 %all-to-all-done.refs_1_ = bf16[8,32,128]{2,1,0:T(8,128)(2,1)S(1)} async-done(((bf16[8,32,128]{2,1,0:T(8,128)(2,1)}), bf16[8,32,128]{2,1,0:T(8,128)(2,1)S(1)}, u32[]{:S(2)}, u32[]{:S(2)}) %all-to-all-start) | async-done | bytes 65568 | tf_op jit(solution)/shard_map/all_to_all | solution.py:108
  13.6 1.2 %shard_map.38 = s16[8,112,128]{2,1,0:T(8,128)(2,1)S(1)} custom-call(s32[2,17]{1,0:T(2,128)S(1)} %get-tuple-element.7.refs_0_, bf16[8,32,128]{2,1,0:T(8,128)(2,1)S(1)} %all-to-all-done.refs_1_, bf16[17,192,128]{2,1,0:T(8,128)(2,1)S(1)} %get-tuple-element.8.refs_2_), custom_call_target="tpu_custom_call" | custom-call | flops 40108032 | bytes 1228800 | tf_op jit(solution)/shard_map/pallas_call | solution.py:145
  14.8 11.3 %all_to_all.10.coded_ref = s16[8,112,128]{2,1,0:T(8,128)(2,1)S(1)} all-to-all(s16[8,112,128]{2,1,0:T(8,128)(2,1)S(1)} %shard_map.38), channel_id=1, replica_groups={{14,12,10,8,6,4,2,0},{15,13,11,9,7,5,3,1},{30,28,26,24,22,20,18,16},{31..., dimensions={0} | all-to-all | bytes 458752 | tf_op jit(solution)/shard_map/all_to_all | solution.py:108
  26.1 0.7 %shard_map.39 = f32[2,48,128]{2,1,0:T(8,128)} custom-call(s16[8,112,128]{2,1,0:T(8,128)(2,1)S(1)} %all_to_all.10.coded_ref), custom_call_target="tpu_custom_call" | custom-call | tf_op jit(solution)/shard_map/pallas_call | solution.py:162
Async XLA Ops:
  1.3 12.2 %all-to-all-start = ((bf16[8,32,128]{2,1,0:T(8,128)(2,1)}), bf16[8,32,128]{2,1,0:T(8,128)(2,1)S(1)}, u32[]{:S(2)}, u32[]{:S(2)}) async-start(bf16[8,32,128]{2,1,0:T(8,128)(2,1)} %pad.7), calls=%async_computation | async-start | bytes 131072 | tf_op jit(solution)/shard_map/all_to_all | solution.py:108
  10.6 0.7 %copy-start.1 = (s32[17,2]{0,1:T(2,128)S(1)}, s32[17,2]{0,1:T(2,128)}, u32[]{:S(2)}) copy-start(s32[17,2]{0,1:T(2,128)} %param.4) | copy-start | bytes 412
  11.3 1.1 %copy-start = (bf16[17,48,4,128]{3,2,1,0:T(4,128)(2,1)S(1)}, bf16[17,48,4,128]{3,2,1,0:T(4,128)(2,1)}, u32[]{:S(2)}) copy-start(bf16[17,48,4,128]{3,2,1,0:T(4,128)(2,1)} %param.3) | copy-start | bytes 2506756

commit v6 on v5

--- a/solution.py
+++ b/solution.py
@@ -31,7 +31,7 @@
     for which, source in enumerate((first, block_count - 1 - first)):
         repeat_rows = (row_of + source % own_blocks == packed_row).astype(jnp.bfloat16)
         tall = jnp.dot(
-            repeat_rows, histories_ref[size - 1 - source // own_blocks], preferred_element_type=jnp.float32
+            repeat_rows, histories_ref[slot_of(source // own_blocks, size)], preferred_element_type=jnp.float32
         )
         wide = jnp.dot(tall.astype(jnp.bfloat16), repeat_columns, preferred_element_type=jnp.float32)
         wide_ref[which] = jnp.where(same_month, wide, 0.0).astype(jnp.bfloat16)
@@ -41,7 +41,7 @@
     def add_tile(slot):
         which = (blocks_ref[0, slot] != first).astype(jnp.int32)
         arrival = blocks_ref[1, slot]
-        place = (size - 1 - arrival // own_blocks) * own_blocks + arrival % own_blocks
+        place = slot_of(arrival // own_blocks, size) * own_blocks + arrival % own_blocks
         sums_ref[place] += jnp.dot(wide_ref[which], tiles_ref[slot], preferred_element_type=jnp.float32)
 
     unrolled = 17
@@ -104,10 +104,18 @@
         copy.wait()
 
 
+def centre(size):
+    return size * 5 // 8
+
+
+def slot_of(device, size):
+    return jnp.where(device == centre(size), 0, device + (device < centre(size)).astype(jnp.int32))
+
+
 def exchange(value, size):
-    return lax.all_to_all(
-        value, "tm", 0, 0, axis_index_groups=[list(range(size - 1, -1, -1))], tiled=True
-    )
+    first = centre(size)
+    order = [first] + [device for device in range(size) if device != first]
+    return lax.all_to_all(value, "tm", 0, 0, axis_index_groups=[order], tiled=True)
 
 
 def shards(propagator, tile_blocks, histories):

time: 27.2 us -> 25.6 us (0.941)
  starting transfers between devices: 9.27 us -> 8.21 us
  blocking collectives: 11.3 us -> 10.3 us
  waiting for transfers between devices: 1 us -> 1.54 us
    all_to_all x1, blocking collectives: 11.3 us -> 10.3 us  [exchange(): lax.all_to_all(value, 'tm', 0, 0, axis_index_groups=[order], tiled=True)]
    all_to_all x1, starting transfers between devices: 9.27 us -> 8.21 us  [exchange(): lax.all_to_all(value, 'tm', 0, 0, axis_index_groups=[order], tiled=True)]
    all_to_all x1, waiting for transfers between devices: 1 us -> 1.54 us  [exchange(): lax.all_to_all(value, 'tm', 0, 0, axis_index_groups=[order], tiled=True)]
where the time goes in v6:
time: 25.6 us; the launch traced here: 25.3 us
  blocking collectives  10.3 us (40%)
  starting transfers between devices  8.21 us (32%)
  local copies, waits for them, and re-layouts  3.16 us (12%)
  Pallas kernels  2.08 us (8%)
  waiting for transfers between devices  1.54 us (6%)
    all_to_all x1, blocking collectives, exchange(): lax.all_to_all(value, 'tm', 0, 0, axis_index_groups=[order], tiled=True)  10.3 us
    all_to_all x1, starting transfers between devices, exchange(): lax.all_to_all(value, 'tm', 0, 0, axis_index_groups=[order], tiled=True)  8.21 us
    unnamed x4, local copies, waits for them, and re-layouts  1.83 us
    all_to_all x1, waiting for transfers between devices, exchange(): lax.all_to_all(value, 'tm', 0, 0, axis_index_groups=[order], tiled=True)  1.54 us
    pad x2, local copies, waits for them, and re-layouts, shards(): jnp.pad(jnp.broadcast_to(rows, (size, used_rows, source_width)), ((0, 0),...  1.33 us
    pallas_call x1, Pallas kernels, shards(): pl.pallas_call(lambda *refs: tile_sums(months, *refs), out_shape=jax.Shap...  1.25 us
    pallas_call x1, Pallas kernels, shards(): pl.pallas_call(add_parts, out_shape=jax.ShapeDtypeStruct((own_blocks, hei...  0.69 us
  transfers between devices with their start and end apart: 1, of which 1 were waited for; matrix products, arithmetic and copies ran while one was open for 0% of the time, Pallas kernels for 1%

profile of v6, /device:TPU:0, one launch (start us, length us, event | category | flops | bytes accessed | tf_op | source)
XLA Modules:
  0.0 25.3 jit_solution(7764827488743537052)
XLA Ops:
  0.0 0.7 %pad.6 = bf16[32,128]{1,0:T(8,128)(2,1)S(1)} pad(bf16[24,48]{1,0:T(8,128)(2,1)} %bitcast.8, bf16[]{:T(256)} %constant.2.clone.1), padding=0_8x0_80 | pad | bytes 10498 | tf_op jit(solution)/shard_map/jit(_pad)/pad | solution.py:130
  0.7 0.6 %pad.7 = bf16[8,32,128]{2,1,0:T(8,128)(2,1)} broadcast(bf16[32,128]{1,0:T(8,128)(2,1)S(1)} %pad.6), dimensions={1,2} | broadcast | bytes 73728 | tf_op jit(solution)/shard_map/jit(_pad)/pad | solution.py:130
  1.3 8.2 %all-to-all-start = ((bf16[8,32,128]{2,1,0:T(8,128)(2,1)}), bf16[8,32,128]{2,1,0:T(8,128)(2,1)S(1)}, u32[]{:S(2)}, u32[]{:S(2)}) async-start(bf16[8,32,128]{2,1,0:T(8,128)(2,1)} %pad.7), calls=%async_computation | async-start | bytes 131072 | tf_op jit(solution)/shard_map/all_to_all | solution.py:118
  9.5 0.0 copy-start.1
  9.5 0.7 %copy-done.1 = s32[17,2]{0,1:T(2,128)S(1)} copy-done((s32[17,2]{0,1:T(2,128)S(1)}, s32[17,2]{0,1:T(2,128)}, u32[]{:S(2)}) %copy-start.1) | copy-done | bytes 160
  10.2 0.0 copy-start
  10.2 1.1 %copy-done = bf16[17,48,4,128]{3,2,1,0:T(4,128)(2,1)S(1)} copy-done((bf16[17,48,4,128]{3,2,1,0:T(4,128)(2,1)S(1)}, bf16[17,48,4,128]{3,2,1,0:T(4,128)(2,1)}, u32[]{:S(2)}) %copy-start) | copy-done | bytes 835608
  11.4 0.1 shard_map.37
  11.5 1.5 %all-to-all-done.refs_1_ = bf16[8,32,128]{2,1,0:T(8,128)(2,1)S(1)} async-done(((bf16[8,32,128]{2,1,0:T(8,128)(2,1)}), bf16[8,32,128]{2,1,0:T(8,128)(2,1)S(1)}, u32[]{:S(2)}, u32[]{:S(2)}) %all-to-all-start) | async-done | bytes 65568 | tf_op jit(solution)/shard_map/all_to_all | solution.py:118
  13.1 1.3 %shard_map.38 = s16[8,112,128]{2,1,0:T(8,128)(2,1)S(1)} custom-call(s32[2,17]{1,0:T(2,128)S(1)} %get-tuple-element.7.refs_0_, bf16[8,32,128]{2,1,0:T(8,128)(2,1)S(1)} %all-to-all-done.refs_1_, bf16[17,192,128]{2,1,0:T(8,128)(2,1)S(1)} %get-tuple-element.8.refs_2_), custom_call_target="tpu_custom_call" | custom-call | flops 40108032 | bytes 1228800 | tf_op jit(solution)/shard_map/pallas_call | solution.py:153
  14.3 10.3 %all_to_all.10.coded_ref = s16[8,112,128]{2,1,0:T(8,128)(2,1)S(1)} all-to-all(s16[8,112,128]{2,1,0:T(8,128)(2,1)S(1)} %shard_map.38), channel_id=1, replica_groups={{10,0,2,4,6,8,12,14},{11,1,3,5,7,9,13,15},{26,16,18,20,22,24,28,30},{27..., dimensions={0} | all-to-all | bytes 458752 | tf_op jit(solution)/shard_map/all_to_all | solution.py:118
  24.6 0.7 %shard_map.39 = f32[2,48,128]{2,1,0:T(8,128)} custom-call(s16[8,112,128]{2,1,0:T(8,128)(2,1)S(1)} %all_to_all.10.coded_ref), custom_call_target="tpu_custom_call" | custom-call | tf_op jit(solution)/shard_map/pallas_call | solution.py:170
Async XLA Ops:
  1.3 11.7 %all-to-all-start = ((bf16[8,32,128]{2,1,0:T(8,128)(2,1)}), bf16[8,32,128]{2,1,0:T(8,128)(2,1)S(1)}, u32[]{:S(2)}, u32[]{:S(2)}) async-start(bf16[8,32,128]{2,1,0:T(8,128)(2,1)} %pad.7), calls=%async_computation | async-start | bytes 131072 | tf_op jit(solution)/shard_map/all_to_all | solution.py:118
  9.5 0.7 %copy-start.1 = (s32[17,2]{0,1:T(2,128)S(1)}, s32[17,2]{0,1:T(2,128)}, u32[]{:S(2)}) copy-start(s32[17,2]{0,1:T(2,128)} %param.4) | copy-start | bytes 412
  10.2 1.1 %copy-start = (bf16[17,48,4,128]{3,2,1,0:T(4,128)(2,1)S(1)}, bf16[17,48,4,128]{3,2,1,0:T(4,128)(2,1)}, u32[]{:S(2)}) copy-start(bf16[17,48,4,128]{3,2,1,0:T(4,128)(2,1)} %param.3) | copy-start | bytes 2506756

commit v7 on v6

--- a/solution.py
+++ b/solution.py
@@ -93,17 +93,6 @@
     lax.fori_loop(0, size, add, 0, unroll=size <= 8)
 
 
-def stage(blocks_in, tiles_in, blocks_out, tiles_out, semaphores):
-    copies = [
-        pltpu.make_async_copy(blocks_in, blocks_out, semaphores.at[0]),
-        pltpu.make_async_copy(tiles_in, tiles_out, semaphores.at[1]),
-    ]
-    for copy in copies:
-        copy.start()
-    for copy in copies:
-        copy.wait()
-
-
 def centre(size):
     return size * 5 // 8
 
@@ -138,18 +127,8 @@
     vmem = pl.BlockSpec(memory_space=pltpu.VMEM)
     smem = pl.BlockSpec(memory_space=pltpu.SMEM)
     hbm = pl.BlockSpec(memory_space=pltpu.HBM)
-    blocks, tiles = pl.pallas_call(
-        stage,
-        out_shape=[
-            jax.ShapeDtypeStruct(blocks.shape, blocks.dtype),
-            jax.ShapeDtypeStruct(tiles.shape, tiles.dtype),
-        ],
-        in_specs=[hbm, hbm],
-        out_specs=[vmem, vmem],
-        scratch_shapes=[pltpu.SemaphoreType.DMA((2,))],
-        compiler_params=pltpu.CompilerParams(vmem_limit_bytes=16 * 1024 * 1024),
-        cost_estimate=pl.CostEstimate(flops=0, bytes_accessed=propagator.size * 4, transcendentals=0),
-    )(blocks, tiles)
+    tiles = lax.ppermute(tiles, "tm", [(i, i) for i in range(size)])
+    blocks = lax.ppermute(blocks, "tm", [(i, i) for i in range(size)])
     coded = pl.pallas_call(
         lambda *refs: tile_sums(months, *refs),
         out_shape=jax.ShapeDtypeStruct((size, own_blocks * height + 16, cell_count), jnp.int16),

time: 25.6 us -> 26.7 us (1.043)
  waiting for transfers between devices: 1.54 us -> 2.83 us
  starting transfers between devices: 8.21 us -> 9.37 us
  local copies, waits for them, and re-layouts: 3.16 us -> 2.01 us
    all_to_all x1, waiting for transfers between devices: 1.54 us -> 2.83 us  [exchange(): lax.all_to_all(value, 'tm', 0, 0, axis_index_groups=[order], tiled=True)]
    ppermute x0 -> x2, starting transfers between devices: none -> 1.15 us  [the longest x1 1.15 us: shards(): tiles = lax.ppermute(tiles, 'tm', [(i, i) for i in range(size)])]
    unnamed x4 -> x2, local copies, waits for them, and re-layouts: 1.83 us -> 0.68 us
  transfers between devices with their start and end apart: 1 -> 3, of which waited for: 1 -> 1; matrix products, arithmetic and copies ran while one was open for 0% -> 5% of each run, Pallas kernels for 1% -> 0%
where the time goes in v7:
time: 26.7 us; the launch traced here: 26.4 us
  blocking collectives  10.3 us (39%)
  starting transfers between devices  9.37 us (35%)
  waiting for transfers between devices  2.83 us (11%)
  local copies, waits for them, and re-layouts  2.01 us (8%)
  Pallas kernels  1.94 us (7%)
    all_to_all x1, blocking collectives, exchange(): lax.all_to_all(value, 'tm', 0, 0, axis_index_groups=[order], tiled=True)  10.3 us
    all_to_all x1, starting transfers between devices, exchange(): lax.all_to_all(value, 'tm', 0, 0, axis_index_groups=[order], tiled=True)  8.21 us
    all_to_all x1, waiting for transfers between devices, exchange(): lax.all_to_all(value, 'tm', 0, 0, axis_index_groups=[order], tiled=True)  2.83 us
    pad x2, local copies, waits for them, and re-layouts, shards(): jnp.pad(jnp.broadcast_to(rows, (size, used_rows, source_width)), ((0, 0),...  1.33 us
    pallas_call x1, Pallas kernels, shards(): pl.pallas_call(lambda *refs: tile_sums(months, *refs), out_shape=jax.Shap...  1.25 us
    ppermute x1, starting transfers between devices, shards(): tiles = lax.ppermute(tiles, 'tm', [(i, i) for i in range(size)])  1.15 us
    pallas_call x1, Pallas kernels, shards(): pl.pallas_call(add_parts, out_shape=jax.ShapeDtypeStruct((own_blocks, hei...  0.69 us
    unnamed x2, local copies, waits for them, and re-layouts  0.68 us
  transfers between devices with their start and end apart: 3, of which 1 were waited for; matrix products, arithmetic and copies ran while one was open for 5% of the time, Pallas kernels for 0%

profile of v7, /device:TPU:0, one launch (start us, length us, event | category | flops | bytes accessed | tf_op | source)
XLA Modules:
  0.0 26.4 jit_solution(8350346108251265901)
XLA Ops:
  0.0 1.2 %collective-permute-start.1 = (bf16[17,192,128]{2,1,0:T(8,128)(2,1)}, bf16[17,192,128]{2,1,0:T(8,128)(2,1)S(1)}, u32[]{:S(2)}, u32[]{:S(2)}) collective-permute-start(bf16[17,192,128]{2,1,0:T(8,128)(2,1)} %bitcast.7), channel_id=1, source_target_pairs={{0,0},{2,2},{4,4},{6,6},{8,8},{10,10},{12,12},{14,14},{1,1},{3,3},... | collective-permute-start | bytes 2506760 | tf_op jit(solution)/shard_map/ppermute | solution.py:130
  1.2 0.7 %pad.6 = bf16[32,128]{1,0:T(8,128)(2,1)S(1)} pad(bf16[24,48]{1,0:T(8,128)(2,1)} %bitcast.6, bf16[]{:T(256)} %constant.2.clone.1), padding=0_8x0_80 | pad | bytes 10498 | tf_op jit(solution)/shard_map/jit(_pad)/pad | solution.py:119
  1.9 0.6 %pad.7 = bf16[8,32,128]{2,1,0:T(8,128)(2,1)} broadcast(bf16[32,128]{1,0:T(8,128)(2,1)S(1)} %pad.6), dimensions={1,2} | broadcast | bytes 73728 | tf_op jit(solution)/shard_map/jit(_pad)/pad | solution.py:119
  2.5 8.2 %all-to-all-start = ((bf16[8,32,128]{2,1,0:T(8,128)(2,1)}), bf16[8,32,128]{2,1,0:T(8,128)(2,1)S(1)}, u32[]{:S(2)}, u32[]{:S(2)}) async-start(bf16[8,32,128]{2,1,0:T(8,128)(2,1)} %pad.7), calls=%async_computation | async-start | bytes 131072 | tf_op jit(solution)/shard_map/all_to_all | solution.py:107
  10.7 0.0 copy-start
  10.7 0.7 %copy-done = s32[17,2]{0,1:T(2,128)S(1)} copy-done((s32[17,2]{0,1:T(2,128)S(1)}, s32[17,2]{0,1:T(2,128)}, u32[]{:S(2)}) %copy-start) | copy-done | bytes 160
  11.4 0.0 collective-permute-start
  11.4 0.0 collective-permute-done.refs_0_
  11.4 2.8 %all-to-all-done.refs_1_ = bf16[8,32,128]{2,1,0:T(8,128)(2,1)S(1)} async-done(((bf16[8,32,128]{2,1,0:T(8,128)(2,1)}), bf16[8,32,128]{2,1,0:T(8,128)(2,1)S(1)}, u32[]{:S(2)}, u32[]{:S(2)}) %all-to-all-start) | async-done | bytes 65568 | tf_op jit(solution)/shard_map/all_to_all | solution.py:107
  14.2 0.0 collective-permute-done.1.refs_2_
  14.2 1.2 %shard_map.37 = s16[8,112,128]{2,1,0:T(8,128)(2,1)S(1)} custom-call(s32[2,17]{1,0:T(2,128)S(1)} %collective-permute-done.refs_0_, bf16[8,32,128]{2,1,0:T(8,128)(2,1)S(1)} %all-to-all-done.refs_1_, bf16[17,192,128]{2,1,0:T(8,128)(2,1)S(1)} %collective-permute-done.1.refs_2_), custom_call_target="tpu_custom_call" | custom-call | flops 40108032 | bytes 1228800 | tf_op jit(solution)/shard_map/pallas_call | solution.py:132
  15.5 10.3 %all_to_all.10.coded_ref = s16[8,112,128]{2,1,0:T(8,128)(2,1)S(1)} all-to-all(s16[8,112,128]{2,1,0:T(8,128)(2,1)S(1)} %shard_map.37), channel_id=1, replica_groups={{10,0,2,4,6,8,12,14},{11,1,3,5,7,9,13,15},{26,16,18,20,22,24,28,30},{27..., dimensions={0} | all-to-all | bytes 458752 | tf_op jit(solution)/shard_map/all_to_all | solution.py:107
  25.7 0.7 %shard_map.38 = f32[2,48,128]{2,1,0:T(8,128)} custom-call(s16[8,112,128]{2,1,0:T(8,128)(2,1)S(1)} %all_to_all.10.coded_ref), custom_call_target="tpu_custom_call" | custom-call | tf_op jit(solution)/shard_map/pallas_call | solution.py:149
Async XLA Ops:
  0.0 14.2 %collective-permute-start.1 = (bf16[17,192,128]{2,1,0:T(8,128)(2,1)}, bf16[17,192,128]{2,1,0:T(8,128)(2,1)S(1)}, u32[]{:S(2)}, u32[]{:S(2)}) collective-permute-start(bf16[17,192,128]{2,1,0:T(8,128)(2,1)} %bitcast.7), channel_id=1, source_target_pairs={{0,0},{2,2},{4,4},{6,6},{8,8},{10,10},{12,12},{14,14},{1,1},{3,3},... | collective-permute-start | bytes 2506760 | tf_op jit(solution)/shard_map/ppermute | solution.py:130
  2.5 11.7 %all-to-all-start = ((bf16[8,32,128]{2,1,0:T(8,128)(2,1)}), bf16[8,32,128]{2,1,0:T(8,128)(2,1)S(1)}, u32[]{:S(2)}, u32[]{:S(2)}) async-start(bf16[8,32,128]{2,1,0:T(8,128)(2,1)} %pad.7), calls=%async_computation | async-start | bytes 131072 | tf_op jit(solution)/shard_map/all_to_all | solution.py:107
  10.7 0.7 %copy-start = (s32[17,2]{0,1:T(2,128)S(1)}, s32[17,2]{0,1:T(2,128)}, u32[]{:S(2)}) copy-start(s32[17,2]{0,1:T(2,128)} %param.4) | copy-start | bytes 412
  (1 other events, 0.0 us)

commit v8 on v7

v8 whole, which is shorter than its diff:
```python
import jax
import jax.numpy as jnp
from jax import lax
from jax.experimental import pallas as pl
from jax.experimental.pallas import tpu as pltpu
from jax.sharding import PartitionSpec as P

STEPS = 32700.0
LEVELS = 128
SMALLEST = 2.0**-126


def centre(size):
    return size * 5 // 8


def slot_of(device, size):
    return jnp.where(device == centre(size), 0, device + (device < centre(size)).astype(jnp.int32))


def device_of(slot, size):
    if isinstance(slot, int):
        return centre(size) if slot == 0 else slot - (slot <= centre(size))
    return jnp.where(slot == 0, centre(size), slot - (slot <= centre(size)).astype(jnp.int32))


def exchange(value, size):
    order = [device_of(slot, size) for slot in range(size)]
    return lax.all_to_all(value, "tm", 0, 0, axis_index_groups=[order], tiled=True)


def each(count, body):
    if count <= 17:
        for index in range(count):
            body(index)
    else:
        lax.fori_loop(0, count, lambda index, carry: (body(index), carry)[1], 0)


def stage(size, months, own_blocks, blocks_ref, tiles_ref, sorted_ref, pick_ref, semaphores):
    block_count = sorted_ref.shape[0]
    slot_count = tiles_ref.shape[0]
    height = pick_ref.shape[0] // 2
    packed_rows = pick_ref.shape[1] // size
    first = blocks_ref[0, 0]

    def clear(block):
        sorted_ref[block] = jnp.zeros(sorted_ref.shape[1:], sorted_ref.dtype)

    def load(slot):
        which = (blocks_ref[0, slot] != first).astype(jnp.int32)
        place = sorted_ref.at[blocks_ref[1, slot], which]
        return pltpu.make_async_copy(tiles_ref.at[slot], place, semaphores.at[slot])

    each(block_count, clear)
    each(slot_count, lambda slot: load(slot).start())
    row = lax.broadcasted_iota(jnp.int32, (height, pick_ref.shape[1]), 0)
    column = lax.broadcasted_iota(jnp.int32, (height, pick_ref.shape[1]), 1)
    for which, source in enumerate((first, block_count - 1 - first)):
        start = slot_of(source // own_blocks, size) * packed_rows + source % own_blocks
        picked = column == start + row // months * own_blocks
        pick_ref[pl.ds(which * height, height)] = picked.astype(jnp.bfloat16)
    each(slot_count, lambda slot: load(slot).wait())


def tile_sums(months, histories_ref, pick_ref, sorted_ref, coded_ref):
    size, packed_rows, packed_width = histories_ref.shape
    block_count, sources, tile_height, cell_count = sorted_ref.shape
    own_blocks = block_count // size
    height = pick_ref.shape[0] // sources

    column_of = lax.broadcasted_iota(jnp.int32, (packed_width, tile_height), 1) // months
    packed_column = lax.broadcasted_iota(jnp.int32, (packed_width, tile_height), 0)
    repeat_columns = (column_of == packed_column).astype(jnp.bfloat16)
    month_of_row = lax.broadcasted_iota(jnp.int32, (sources * height, tile_height), 0) % months
    month_of_column = lax.broadcasted_iota(jnp.int32, (sources * height, tile_height), 1) % months
    histories = histories_ref[...].reshape(size * packed_rows, packed_width)
    tall = jnp.dot(pick_ref[...], histories, preferred_element_type=jnp.float32)
    wide = jnp.dot(tall.astype(jnp.bfloat16), repeat_columns, preferred_element_type=jnp.float32)
    wide = jnp.where(month_of_row == month_of_column, wide, 0.0).astype(jnp.bfloat16)

    coded_rows = own_blocks * height

    def code(slot):
        values = []
        for block in range(own_blocks):
            place = device_of(slot, size) * own_blocks + block
            parts = [
                jnp.dot(
                    wide[which * height : (which + 1) * height],
                    sorted_ref[place, which],
                    preferred_element_type=jnp.float32,
                )
                for which in range(sources)
            ]
            values.append(sum(parts[1:], parts[0]))
        top = jnp.abs(values[0])
        for value in values[1:]:
            top = jnp.maximum(top, jnp.abs(value))
        top = jnp.max(top, axis=0, keepdims=True)
        level = jnp.ceil(jnp.log2(jnp.maximum(top, SMALLEST)) * LEVELS)
        half = jnp.exp2(level * (-0.5 / LEVELS))
        for block, value in enumerate(values):
            steps = jnp.round(value * half * (half * STEPS))
            coded_ref[slot, pl.ds(block * height, height)] = steps.astype(jnp.int32).astype(jnp.int16)
        spread = jnp.broadcast_to(level.astype(jnp.int32), (16, cell_count))
        coded_ref[slot, pl.ds(coded_rows, 16)] = spread.astype(jnp.int16)

    each(size, code)


def add_parts(coded_ref, total_ref):
    size = coded_ref.shape[0]
    own_blocks, height, cell_count = total_ref.shape
    coded_rows = own_blocks * height
    total_ref[...] = jnp.zeros(total_ref.shape, total_ref.dtype)

    def add(slot):
        level = coded_ref[slot, pl.ds(coded_rows, 16)].astype(jnp.int32).astype(jnp.float32)[:1]
        half = jnp.exp2(level * (0.5 / LEVELS))
        for block in range(own_blocks):
            steps = coded_ref[slot, pl.ds(block * height, height)].astype(jnp.int32)
            total_ref[block] += steps.astype(jnp.float32) * (half * (1.0 / STEPS)) * half

    each(size, add)


def shards(propagator, tile_blocks, histories):
    size = lax.axis_size("tm")
    own_blocks, tracer_count, source_width = histories.shape
    slot_count, source_width, months, cell_count = propagator.shape
    block_count = size * own_blocks
    height = tracer_count * months
    tile_height = source_width * months

    used_rows = tracer_count * own_blocks
    rows = jnp.swapaxes(histories, 0, 1).reshape(1, used_rows, source_width)
    copies = jnp.pad(
        jnp.broadcast_to(rows, (size, used_rows, source_width)),
        ((0, 0), (0, -used_rows % 16), (0, -source_width % 128)),
    )
    received = exchange(copies, size)

    vmem = pl.BlockSpec(memory_space=pltpu.VMEM)
    smem = pl.BlockSpec(memory_space=pltpu.SMEM)
    anywhere = pl.BlockSpec(memory_space=pl.ANY)
    sorted_tiles, pick = pl.pallas_call(
        lambda *refs: stage(size, months, own_blocks, *refs),
        out_shape=[
            jax.ShapeDtypeStruct((block_count, 2, tile_height, cell_count), propagator.dtype),
            jax.ShapeDtypeStruct((2 * height, size * copies.shape[1]), jnp.bfloat16),
        ],
        in_specs=[smem, anywhere],
        out_specs=[vmem, vmem],
        scratch_shapes=[pltpu.SemaphoreType.DMA((slot_count,))],
        compiler_params=pltpu.CompilerParams(vmem_limit_bytes=20 * 1024 * 1024),
        cost_estimate=pl.CostEstimate(flops=0, bytes_accessed=propagator.size * 4, transcendentals=0),
    )(tile_blocks.T, propagator.reshape(slot_count, tile_height, cell_count))

    coded = pl.pallas_call(
        lambda *refs: tile_sums(months, *refs),
        out_shape=jax.ShapeDtypeStruct((size, own_blocks * height + 16, cell_count), jnp.int16),
        in_specs=[vmem, vmem, vmem],
        out_specs=vmem,
        compiler_params=pltpu.CompilerParams(vmem_limit_bytes=20 * 1024 * 1024),
        cost_estimate=pl.CostEstimate(
            flops=2 * slot_count * height * tile_height * cell_count,
            bytes_accessed=propagator.size * 4,
            transcendentals=0,
        ),
    )(received, pick, sorted_tiles)

    owned = pl.pallas_call(
        add_parts,
        out_shape=jax.ShapeDtypeStruct((own_blocks, height, cell_count), jnp.float32),
        in_specs=[vmem],
        out_specs=vmem,
        compiler_params=pltpu.CompilerParams(vmem_limit_bytes=16 * 1024 * 1024),
    )(exchange(coded, size))
    return owned.reshape(own_blocks, tracer_count, months, cell_count)


def solution(mesh):
    in_specs = (
        P(("groups", "tm"), None, None, "cells"),
        P(("groups", "tm"), None),
        P("tm", None, None),
    )
    out_specs = P(("groups", "tm"), None, None, "cells")
    return jax.shard_map(shards, mesh=mesh, in_specs=in_specs, out_specs=out_specs, check_vma=False)
```

time: 26.7 us -> 25.9 us (0.970)
  waiting for transfers between devices: 2.83 us -> 0.01 us
  Pallas kernels: 1.94 us -> 3.75 us
  starting transfers between devices: 9.37 us -> 8.21 us
  local copies, waits for them, and re-layouts: 2.01 us -> 3.16 us
    all_to_all x1, waiting for transfers between devices: 2.83 us -> 0.01 us  [exchange(): lax.all_to_all(value, 'tm', 0, 0, axis_index_groups=[order], tiled=True)]
    pallas_call x0 -> x1, Pallas kernels: none -> 2.14 us  [shards(): pl.pallas_call(lambda *refs: stage(size, months, own_blocks, *refs), out_...]
    ppermute x2 -> x0, starting transfers between devices: 1.15 us -> none  [the longest x1 1.15 us: shards(): tiles = lax.ppermute(tiles, 'tm', [(i, i) for i in range(size)])]
    unnamed x2 -> x4, local copies, waits for them, and re-layouts: 0.68 us -> 1.83 us
    pallas_call x1, Pallas kernels: 1.25 us -> 0.92 us  [shards(): pl.pallas_call(lambda *refs: tile_sums(months, *refs), out_shape=jax.Shap...]
  transfers between devices with their start and end apart: 3 -> 1, of which waited for: 1 -> 0; matrix products, arithmetic and copies ran while one was open for 5% -> 0% of each run, Pallas kernels for 0% -> 8%
where the time goes in v8:
time: 25.9 us; the launch traced here: 25.6 us
  blocking collectives  10.4 us (40%)
  starting transfers between devices  8.21 us (32%)
  Pallas kernels  3.75 us (14%)
  local copies, waits for them, and re-layouts  3.16 us (12%)
    all_to_all x1, blocking collectives, exchange(): lax.all_to_all(value, 'tm', 0, 0, axis_index_groups=[order], tiled=True)  10.4 us
    all_to_all x1, starting transfers between devices, exchange(): lax.all_to_all(value, 'tm', 0, 0, axis_index_groups=[order], tiled=True)  8.21 us
    pallas_call x1, Pallas kernels, shards(): pl.pallas_call(lambda *refs: stage(size, months, own_blocks, *refs), out_...  2.14 us
    unnamed x4, local copies, waits for them, and re-layouts  1.83 us
    pad x2, local copies, waits for them, and re-layouts, shards(): jnp.pad(jnp.broadcast_to(rows, (size, used_rows, source_width)), ((0, 0),...  1.33 us
    pallas_call x1, Pallas kernels, shards(): pl.pallas_call(lambda *refs: tile_sums(months, *refs), out_shape=jax.Shap...  0.92 us
    pallas_call x1, Pallas kernels, shards(): pl.pallas_call(add_parts, out_shape=jax.ShapeDtypeStruct((own_blocks, hei...  0.69 us
  transfers between devices with their start and end apart: 1, of which 0 were waited for; matrix products, arithmetic and copies ran while one was open for 0% of the time, Pallas kernels for 8%

profile of v8, /device:TPU:0, one launch (start us, length us, event | category | flops | bytes accessed | tf_op | source)
XLA Modules:
  0.0 25.6 jit_solution(3226258815449421902)
XLA Ops:
  0.0 0.7 %pad.6 = bf16[32,128]{1,0:T(8,128)(2,1)S(1)} pad(bf16[24,48]{1,0:T(8,128)(2,1)} %bitcast.8, bf16[]{:T(256)} %constant.2.clone.1), padding=0_8x0_80 | pad | bytes 10498 | tf_op jit(solution)/shard_map/jit(_pad)/pad | solution.py:138
  0.7 0.6 %pad.7 = bf16[8,32,128]{2,1,0:T(8,128)(2,1)} broadcast(bf16[32,128]{1,0:T(8,128)(2,1)S(1)} %pad.6), dimensions={1,2} | broadcast | bytes 73728 | tf_op jit(solution)/shard_map/jit(_pad)/pad | solution.py:138
  1.3 8.2 %all-to-all-start = ((bf16[8,32,128]{2,1,0:T(8,128)(2,1)}), bf16[8,32,128]{2,1,0:T(8,128)(2,1)S(1)}, u32[]{:S(2)}, u32[]{:S(2)}) async-start(bf16[8,32,128]{2,1,0:T(8,128)(2,1)} %pad.7), calls=%async_computation | async-start | bytes 131072 | tf_op jit(solution)/shard_map/all_to_all | solution.py:29
  9.5 0.0 copy-start
  9.5 1.1 %copy-done = bf16[17,48,4,128]{3,2,1,0:T(4,128)(2,1)S(1)} copy-done((bf16[17,48,4,128]{3,2,1,0:T(4,128)(2,1)S(1)}, bf16[17,48,4,128]{3,2,1,0:T(4,128)(2,1)}, u32[]{:S(2)}) %copy-start) | copy-done | bytes 835608
  10.7 0.0 copy-start.1
  10.7 0.7 %copy-done.1 = s32[17,2]{0,1:T(2,128)S(1)} copy-done((s32[17,2]{0,1:T(2,128)S(1)}, s32[17,2]{0,1:T(2,128)}, u32[]{:S(2)}) %copy-start.1) | copy-done | bytes 160
  11.4 2.1 %shard_map.37 = (bf16[16,2,192,128]{3,2,1,0:T(8,128)(2,1)S(1)}, bf16[96,256]{1,0:T(8,128)(2,1)S(1)}) custom-call(s32[2,17]{1,0:T(2,128)S(1)} %bitcast.7, bf16[17,192,128]{2,1,0:T(8,128)(2,1)S(1)} %bitcast.6), custom_call_target="tpu_custom_call" | custom-call | bytes 1671168 | tf_op jit(solution)/shard_map/pallas_call | solution.py:147
  13.5 0.0 all-to-all-done.refs_0_
  13.5 0.9 %shard_map.38 = s16[8,112,128]{2,1,0:T(8,128)(2,1)S(1)} custom-call(bf16[8,32,128]{2,1,0:T(8,128)(2,1)S(1)} %all-to-all-done.refs_0_, bf16[96,256]{1,0:T(8,128)(2,1)S(1)} %get-tuple-element.7.refs_1_, bf16[16,2,192,128]{3,2,1,0:T(8,128)(2,1)S(1)} %get-tuple-element.8.refs_2_), custom_call_target="tpu_custom_call" | custom-call | flops 40108032 | bytes 1671168 | tf_op jit(solution)/shard_map/pallas_call | solution.py:160
  14.5 10.4 %all_to_all.10.coded_ref = s16[8,112,128]{2,1,0:T(8,128)(2,1)S(1)} all-to-all(s16[8,112,128]{2,1,0:T(8,128)(2,1)S(1)} %shard_map.38), channel_id=1, replica_groups={{10,0,2,4,6,8,12,14},{11,1,3,5,7,9,13,15},{26,16,18,20,22,24,28,30},{27..., dimensions={0} | all-to-all | bytes 458752 | tf_op jit(solution)/shard_map/all_to_all | solution.py:29
  24.9 0.7 %shard_map.39 = f32[2,48,128]{2,1,0:T(8,128)} custom-call(s16[8,112,128]{2,1,0:T(8,128)(2,1)S(1)} %all_to_all.10.coded_ref), custom_call_target="tpu_custom_call" | custom-call | tf_op jit(solution)/shard_map/pallas_call | solution.py:173
Async XLA Ops:
  1.3 12.2 %all-to-all-start = ((bf16[8,32,128]{2,1,0:T(8,128)(2,1)}), bf16[8,32,128]{2,1,0:T(8,128)(2,1)S(1)}, u32[]{:S(2)}, u32[]{:S(2)}) async-start(bf16[8,32,128]{2,1,0:T(8,128)(2,1)} %pad.7), calls=%async_computation | async-start | bytes 131072 | tf_op jit(solution)/shard_map/all_to_all | solution.py:29
  9.5 1.1 %copy-start = (bf16[17,48,4,128]{3,2,1,0:T(4,128)(2,1)S(1)}, bf16[17,48,4,128]{3,2,1,0:T(4,128)(2,1)}, u32[]{:S(2)}) copy-start(bf16[17,48,4,128]{3,2,1,0:T(4,128)(2,1)} %param.3) | copy-start | bytes 2506756
  10.7 0.7 %copy-start.1 = (s32[17,2]{0,1:T(2,128)S(1)}, s32[17,2]{0,1:T(2,128)}, u32[]{:S(2)}) copy-start(s32[17,2]{0,1:T(2,128)} %param.4) | copy-start | bytes 412

commit v9 on v8

--- a/solution.py
+++ b/solution.py
@@ -15,13 +15,15 @@
 
 
 def slot_of(device, size):
-    return jnp.where(device == centre(size), 0, device + (device < centre(size)).astype(jnp.int32))
+    after = device - (device > centre(size)).astype(jnp.int32)
+    return jnp.where(device == centre(size), 0, jnp.where(device == 0, size - 1, after))
 
 
 def device_of(slot, size):
     if isinstance(slot, int):
-        return centre(size) if slot == 0 else slot - (slot <= centre(size))
-    return jnp.where(slot == 0, centre(size), slot - (slot <= centre(size)).astype(jnp.int32))
+        return centre(size) if slot == 0 else 0 if slot == size - 1 else slot + (slot >= centre(size))
+    after = slot + (slot >= centre(size)).astype(jnp.int32)
+    return jnp.where(slot == 0, centre(size), jnp.where(slot == size - 1, 0, after))
 
 
 def exchange(value, size):
@@ -37,7 +39,7 @@
         lax.fori_loop(0, count, lambda index, carry: (body(index), carry)[1], 0)
 
 
-def stage(size, months, own_blocks, blocks_ref, tiles_ref, sorted_ref, pick_ref, semaphores):
+def stage(size, months, own_blocks, blocks_ref, tiles_ref, sorted_ref, pick_ref):
     block_count = sorted_ref.shape[0]
     slot_count = tiles_ref.shape[0]
     height = pick_ref.shape[0] // 2
@@ -47,20 +49,18 @@
     def clear(block):
         sorted_ref[block] = jnp.zeros(sorted_ref.shape[1:], sorted_ref.dtype)
 
-    def load(slot):
+    def place(slot):
         which = (blocks_ref[0, slot] != first).astype(jnp.int32)
-        place = sorted_ref.at[blocks_ref[1, slot], which]
-        return pltpu.make_async_copy(tiles_ref.at[slot], place, semaphores.at[slot])
+        sorted_ref[blocks_ref[1, slot], which] = tiles_ref[slot]
 
     each(block_count, clear)
-    each(slot_count, lambda slot: load(slot).start())
+    each(slot_count, place)
     row = lax.broadcasted_iota(jnp.int32, (height, pick_ref.shape[1]), 0)
     column = lax.broadcasted_iota(jnp.int32, (height, pick_ref.shape[1]), 1)
     for which, source in enumerate((first, block_count - 1 - first)):
         start = slot_of(source // own_blocks, size) * packed_rows + source % own_blocks
         picked = column == start + row // months * own_blocks
         pick_ref[pl.ds(which * height, height)] = picked.astype(jnp.bfloat16)
-    each(slot_count, lambda slot: load(slot).wait())
 
 
 def tile_sums(months, histories_ref, pick_ref, sorted_ref, coded_ref):
@@ -143,16 +143,14 @@
 
     vmem = pl.BlockSpec(memory_space=pltpu.VMEM)
     smem = pl.BlockSpec(memory_space=pltpu.SMEM)
-    anywhere = pl.BlockSpec(memory_space=pl.ANY)
     sorted_tiles, pick = pl.pallas_call(
         lambda *refs: stage(size, months, own_blocks, *refs),
         out_shape=[
             jax.ShapeDtypeStruct((block_count, 2, tile_height, cell_count), propagator.dtype),
             jax.ShapeDtypeStruct((2 * height, size * copies.shape[1]), jnp.bfloat16),
         ],
-        in_specs=[smem, anywhere],
+        in_specs=[smem, vmem],
         out_specs=[vmem, vmem],
-        scratch_shapes=[pltpu.SemaphoreType.DMA((slot_count,))],
         compiler_params=pltpu.CompilerParams(vmem_limit_bytes=20 * 1024 * 1024),
         cost_estimate=pl.CostEstimate(flops=0, bytes_accessed=propagator.size * 4, transcendentals=0),
     )(tile_blocks.T, propagator.reshape(slot_count, tile_height, cell_count))

time: 25.9 us -> 24.9 us (0.961)
  Pallas kernels: 3.75 us -> 2.43 us
  waiting for transfers between devices: 0.01 us -> 0.98 us
  blocking collectives: 10.4 us -> 9.74 us
    pallas_call x1, Pallas kernels: 2.14 us -> 0.82 us  [shards(): pl.pallas_call(lambda *refs: stage(size, months, own_blocks, *refs), out_...]
    all_to_all x1, waiting for transfers between devices: 0.01 us -> 0.98 us  [exchange(): lax.all_to_all(value, 'tm', 0, 0, axis_index_groups=[order], tiled=True)]
    all_to_all x1, blocking collectives: 10.4 us -> 9.74 us  [exchange(): lax.all_to_all(value, 'tm', 0, 0, axis_index_groups=[order], tiled=True)]
  transfers between devices with their start and end apart: 1 -> 1, of which waited for: 0 -> 1; matrix products, arithmetic and copies ran while one was open for 0% -> 0% of each run, Pallas kernels for 8% -> 3%
where the time goes in v9:
time: 24.9 us; the launch traced here: 24.6 us
  blocking collectives  9.74 us (39%)
  starting transfers between devices  8.26 us (33%)
  local copies, waits for them, and re-layouts  3.16 us (13%)
  Pallas kernels  2.43 us (10%)
  waiting for transfers between devices  0.98 us (4%)
    all_to_all x1, blocking collectives, exchange(): lax.all_to_all(value, 'tm', 0, 0, axis_index_groups=[order], tiled=True)  9.74 us
    all_to_all x1, starting transfers between devices, exchange(): lax.all_to_all(value, 'tm', 0, 0, axis_index_groups=[order], tiled=True)  8.26 us
    unnamed x4, local copies, waits for them, and re-layouts  1.83 us
    pad x2, local copies, waits for them, and re-layouts, shards(): jnp.pad(jnp.broadcast_to(rows, (size, used_rows, source_width)), ((0, 0),...  1.33 us
    all_to_all x1, waiting for transfers between devices, exchange(): lax.all_to_all(value, 'tm', 0, 0, axis_index_groups=[order], tiled=True)  0.98 us
    pallas_call x1, Pallas kernels, shards(): pl.pallas_call(lambda *refs: tile_sums(months, *refs), out_shape=jax.Shap...  0.92 us
    pallas_call x1, Pallas kernels, shards(): pl.pallas_call(lambda *refs: stage(size, months, own_blocks, *refs), out_...  0.82 us
    pallas_call x1, Pallas kernels, shards(): pl.pallas_call(add_parts, out_shape=jax.ShapeDtypeStruct((own_blocks, hei...  0.69 us
  transfers between devices with their start and end apart: 1, of which 1 were waited for; matrix products, arithmetic and copies ran while one was open for 0% of the time, Pallas kernels for 3%

profile of v9, /device:TPU:0, one launch (start us, length us, event | category | flops | bytes accessed | tf_op | source)
XLA Modules:
  0.0 24.6 jit_solution(723055317488813715)
XLA Ops:
  0.0 0.7 %pad.6 = bf16[32,128]{1,0:T(8,128)(2,1)S(1)} pad(bf16[24,48]{1,0:T(8,128)(2,1)} %bitcast.8, bf16[]{:T(256)} %constant.2.clone.1), padding=0_8x0_80 | pad | bytes 10498 | tf_op jit(solution)/shard_map/jit(_pad)/pad | solution.py:138
  0.7 0.6 %pad.7 = bf16[8,32,128]{2,1,0:T(8,128)(2,1)} broadcast(bf16[32,128]{1,0:T(8,128)(2,1)S(1)} %pad.6), dimensions={1,2} | broadcast | bytes 73728 | tf_op jit(solution)/shard_map/jit(_pad)/pad | solution.py:138
  1.3 8.3 %all-to-all-start = ((bf16[8,32,128]{2,1,0:T(8,128)(2,1)}), bf16[8,32,128]{2,1,0:T(8,128)(2,1)S(1)}, u32[]{:S(2)}, u32[]{:S(2)}) async-start(bf16[8,32,128]{2,1,0:T(8,128)(2,1)} %pad.7), calls=%async_computation | async-start | bytes 131072 | tf_op jit(solution)/shard_map/all_to_all | solution.py:31
  9.6 0.0 copy-start
  9.6 1.1 %copy-done = bf16[17,48,4,128]{3,2,1,0:T(4,128)(2,1)S(1)} copy-done((bf16[17,48,4,128]{3,2,1,0:T(4,128)(2,1)S(1)}, bf16[17,48,4,128]{3,2,1,0:T(4,128)(2,1)}, u32[]{:S(2)}) %copy-start) | copy-done | bytes 835608
  10.7 0.0 copy-start.1
  10.7 0.7 %copy-done.1 = s32[17,2]{0,1:T(2,128)S(1)} copy-done((s32[17,2]{0,1:T(2,128)S(1)}, s32[17,2]{0,1:T(2,128)}, u32[]{:S(2)}) %copy-start.1) | copy-done | bytes 160
  11.4 0.8 %shard_map.37 = (bf16[16,2,192,128]{3,2,1,0:T(8,128)(2,1)S(1)}, bf16[96,256]{1,0:T(8,128)(2,1)S(1)}) custom-call(s32[2,17]{1,0:T(2,128)S(1)} %bitcast.7, bf16[17,192,128]{2,1,0:T(8,128)(2,1)S(1)} %bitcast.6), custom_call_target="tpu_custom_call" | custom-call | bytes 1671168 | tf_op jit(solution)/shard_map/pallas_call | solution.py:146
  12.2 1.0 %all-to-all-done.refs_0_ = bf16[8,32,128]{2,1,0:T(8,128)(2,1)S(1)} async-done(((bf16[8,32,128]{2,1,0:T(8,128)(2,1)}), bf16[8,32,128]{2,1,0:T(8,128)(2,1)S(1)}, u32[]{:S(2)}, u32[]{:S(2)}) %all-to-all-start) | async-done | bytes 65568 | tf_op jit(solution)/shard_map/all_to_all | solution.py:31
  13.2 0.9 %shard_map.38 = s16[8,112,128]{2,1,0:T(8,128)(2,1)S(1)} custom-call(bf16[8,32,128]{2,1,0:T(8,128)(2,1)S(1)} %all-to-all-done.refs_0_, bf16[96,256]{1,0:T(8,128)(2,1)S(1)} %get-tuple-element.7.refs_1_, bf16[16,2,192,128]{3,2,1,0:T(8,128)(2,1)S(1)} %get-tuple-element.8.refs_2_), custom_call_target="tpu_custom_call" | custom-call | flops 40108032 | bytes 1671168 | tf_op jit(solution)/shard_map/pallas_call | solution.py:158
  14.2 9.7 %all_to_all.10.coded_ref = s16[8,112,128]{2,1,0:T(8,128)(2,1)S(1)} all-to-all(s16[8,112,128]{2,1,0:T(8,128)(2,1)S(1)} %shard_map.38), channel_id=1, replica_groups={{10,2,4,6,8,12,14,0},{11,3,5,7,9,13,15,1},{26,18,20,22,24,28,30,16},{27..., dimensions={0} | all-to-all | bytes 458752 | tf_op jit(solution)/shard_map/all_to_all | solution.py:31
  23.9 0.7 %shard_map.39 = f32[2,48,128]{2,1,0:T(8,128)} custom-call(s16[8,112,128]{2,1,0:T(8,128)(2,1)S(1)} %all_to_all.10.coded_ref), custom_call_target="tpu_custom_call" | custom-call | tf_op jit(solution)/shard_map/pallas_call | solution.py:171
Async XLA Ops:
  1.3 11.9 %all-to-all-start = ((bf16[8,32,128]{2,1,0:T(8,128)(2,1)}), bf16[8,32,128]{2,1,0:T(8,128)(2,1)S(1)}, u32[]{:S(2)}, u32[]{:S(2)}) async-start(bf16[8,32,128]{2,1,0:T(8,128)(2,1)} %pad.7), calls=%async_computation | async-start | bytes 131072 | tf_op jit(solution)/shard_map/all_to_all | solution.py:31
  9.6 1.1 %copy-start = (bf16[17,48,4,128]{3,2,1,0:T(4,128)(2,1)S(1)}, bf16[17,48,4,128]{3,2,1,0:T(4,128)(2,1)}, u32[]{:S(2)}) copy-start(bf16[17,48,4,128]{3,2,1,0:T(4,128)(2,1)} %param.3) | copy-start | bytes 2506756
  10.7 0.7 %copy-start.1 = (s32[17,2]{0,1:T(2,128)S(1)}, s32[17,2]{0,1:T(2,128)}, u32[]{:S(2)}) copy-start(s32[17,2]{0,1:T(2,128)} %param.4) | copy-start | bytes 412

commit v10 on v9

--- a/solution.py
+++ b/solution.py
@@ -29,6 +29,16 @@
 def exchange(value, size):
     order = [device_of(slot, size) for slot in range(size)]
     return lax.all_to_all(value, "tm", 0, 0, axis_index_groups=[order], tiled=True)
+
+
+def exchange_across(value, size):
+    cells = lax.axis_size("cells")
+    order = [device_of(slot, size) for slot in range(size)]
+    groups = [
+        [device * cells + (cell + (device >= size // 2)) % cells for device in order]
+        for cell in range(cells)
+    ]
+    return lax.all_to_all(value, ("tm", "cells"), 0, 0, axis_index_groups=groups, tiled=True)
 
 
 def each(count, body):
@@ -139,7 +149,7 @@
         jnp.broadcast_to(rows, (size, used_rows, source_width)),
         ((0, 0), (0, -used_rows % 16), (0, -source_width % 128)),
     )
-    received = exchange(copies, size)
+    received = exchange_across(copies, size)
 
     vmem = pl.BlockSpec(memory_space=pltpu.VMEM)
     smem = pl.BlockSpec(memory_space=pltpu.SMEM)

time: 24.9 us -> 25.5 us (1.024)
  blocking collectives: 9.74 us -> 11.5 us
  waiting for transfers between devices: 0.98 us -> 0.41 us
  starting transfers between devices: 8.26 us -> 7.69 us
    all_to_all x1, blocking collectives: 9.74 us -> 11.5 us  [exchange(): lax.all_to_all(value, 'tm', 0, 0, axis_index_groups=[order], tiled=True)]
    all_to_all x1, waiting for transfers between devices: 0.98 us -> 0.41 us  [exchange_across(): lax.all_to_all(value, ('tm', 'cells'), 0, 0, axis_index_groups=groups, ti...]
    all_to_all x1, starting transfers between devices: 8.26 us -> 7.69 us  [exchange_across(): lax.all_to_all(value, ('tm', 'cells'), 0, 0, axis_index_groups=groups, ti...]
where the time goes in v10:
time: 25.5 us; the launch traced here: 25.2 us
  blocking collectives  11.5 us (45%)
  starting transfers between devices  7.69 us (30%)
  local copies, waits for them, and re-layouts  3.16 us (12%)
  Pallas kernels  2.43 us (10%)
  waiting for transfers between devices  0.41 us (2%)
    all_to_all x1, blocking collectives, exchange(): lax.all_to_all(value, 'tm', 0, 0, axis_index_groups=[order], tiled=True)  11.5 us
    all_to_all x1, starting transfers between devices, exchange_across(): lax.all_to_all(value, ('tm', 'cells'), 0, 0, axis_index_groups=groups, ti...  7.69 us
    unnamed x4, local copies, waits for them, and re-layouts  1.83 us
    pad x2, local copies, waits for them, and re-layouts, shards(): jnp.pad(jnp.broadcast_to(rows, (size, used_rows, source_width)), ((0, 0),...  1.33 us
    pallas_call x1, Pallas kernels, shards(): pl.pallas_call(lambda *refs: tile_sums(months, *refs), out_shape=jax.Shap...  0.92 us
    pallas_call x1, Pallas kernels, shards(): pl.pallas_call(lambda *refs: stage(size, months, own_blocks, *refs), out_...  0.82 us
    pallas_call x1, Pallas kernels, shards(): pl.pallas_call(add_parts, out_shape=jax.ShapeDtypeStruct((own_blocks, hei...  0.69 us
  transfers between devices with their start and end apart: 1, of which 1 were waited for; matrix products, arithmetic and copies ran while one was open for 0% of the time, Pallas kernels for 3%

profile of v10, /device:TPU:0, one launch (start us, length us, event | category | flops | bytes accessed | tf_op | source)
XLA Modules:
  0.0 25.2 jit_solution(9878820349320095894)
XLA Ops:
  0.0 0.7 %pad.6 = bf16[32,128]{1,0:T(8,128)(2,1)S(1)} pad(bf16[24,48]{1,0:T(8,128)(2,1)} %bitcast.8, bf16[]{:T(256)} %constant.2.clone.1), padding=0_8x0_80 | pad | bytes 10498 | tf_op jit(solution)/shard_map/jit(_pad)/pad | solution.py:148
  0.7 0.6 %pad.7 = bf16[8,32,128]{2,1,0:T(8,128)(2,1)} broadcast(bf16[32,128]{1,0:T(8,128)(2,1)S(1)} %pad.6), dimensions={1,2} | broadcast | bytes 73728 | tf_op jit(solution)/shard_map/jit(_pad)/pad | solution.py:148
  1.3 7.7 %all-to-all-start = ((bf16[8,32,128]{2,1,0:T(8,128)(2,1)}), bf16[8,32,128]{2,1,0:T(8,128)(2,1)S(1)}, u32[]{:S(2)}, u32[]{:S(2)}) async-start(bf16[8,32,128]{2,1,0:T(8,128)(2,1)} %pad.7), calls=%async_computation | async-start | bytes 131072 | tf_op jit(solution)/shard_map/all_to_all | solution.py:41
  9.0 0.0 copy-start
  9.0 1.1 %copy-done = bf16[17,48,4,128]{3,2,1,0:T(4,128)(2,1)S(1)} copy-done((bf16[17,48,4,128]{3,2,1,0:T(4,128)(2,1)S(1)}, bf16[17,48,4,128]{3,2,1,0:T(4,128)(2,1)}, u32[]{:S(2)}) %copy-start) | copy-done | bytes 835608
  10.2 0.0 copy-start.1
  10.2 0.7 %copy-done.1 = s32[17,2]{0,1:T(2,128)S(1)} copy-done((s32[17,2]{0,1:T(2,128)S(1)}, s32[17,2]{0,1:T(2,128)}, u32[]{:S(2)}) %copy-start.1) | copy-done | bytes 160
  10.9 0.8 %shard_map.37 = (bf16[16,2,192,128]{3,2,1,0:T(8,128)(2,1)S(1)}, bf16[96,256]{1,0:T(8,128)(2,1)S(1)}) custom-call(s32[2,17]{1,0:T(2,128)S(1)} %bitcast.7, bf16[17,192,128]{2,1,0:T(8,128)(2,1)S(1)} %bitcast.6), custom_call_target="tpu_custom_call" | custom-call | bytes 1671168 | tf_op jit(solution)/shard_map/pallas_call | solution.py:156
  11.7 0.4 %all-to-all-done.refs_0_ = bf16[8,32,128]{2,1,0:T(8,128)(2,1)S(1)} async-done(((bf16[8,32,128]{2,1,0:T(8,128)(2,1)}), bf16[8,32,128]{2,1,0:T(8,128)(2,1)S(1)}, u32[]{:S(2)}, u32[]{:S(2)}) %all-to-all-start) | async-done | bytes 65568 | tf_op jit(solution)/shard_map/all_to_all | solution.py:41
  12.1 0.9 %shard_map.38 = s16[8,112,128]{2,1,0:T(8,128)(2,1)S(1)} custom-call(bf16[8,32,128]{2,1,0:T(8,128)(2,1)S(1)} %all-to-all-done.refs_0_, bf16[96,256]{1,0:T(8,128)(2,1)S(1)} %get-tuple-element.7.refs_1_, bf16[16,2,192,128]{3,2,1,0:T(8,128)(2,1)S(1)} %get-tuple-element.8.refs_2_), custom_call_target="tpu_custom_call" | custom-call | flops 40108032 | bytes 1671168 | tf_op jit(solution)/shard_map/pallas_call | solution.py:168
  13.0 11.5 %all_to_all.10.coded_ref = s16[8,112,128]{2,1,0:T(8,128)(2,1)S(1)} all-to-all(s16[8,112,128]{2,1,0:T(8,128)(2,1)S(1)} %shard_map.38), channel_id=1, replica_groups={{10,2,4,6,8,12,14,0},{11,3,5,7,9,13,15,1},{26,18,20,22,24,28,30,16},{27..., dimensions={0} | all-to-all | bytes 458752 | tf_op jit(solution)/shard_map/all_to_all | solution.py:31
  24.5 0.7 %shard_map.39 = f32[2,48,128]{2,1,0:T(8,128)} custom-call(s16[8,112,128]{2,1,0:T(8,128)(2,1)S(1)} %all_to_all.10.coded_ref), custom_call_target="tpu_custom_call" | custom-call | tf_op jit(solution)/shard_map/pallas_call | solution.py:181
Async XLA Ops:
  1.3 10.8 %all-to-all-start = ((bf16[8,32,128]{2,1,0:T(8,128)(2,1)}), bf16[8,32,128]{2,1,0:T(8,128)(2,1)S(1)}, u32[]{:S(2)}, u32[]{:S(2)}) async-start(bf16[8,32,128]{2,1,0:T(8,128)(2,1)} %pad.7), calls=%async_computation | async-start | bytes 131072 | tf_op jit(solution)/shard_map/all_to_all | solution.py:41
  9.0 1.1 %copy-start = (bf16[17,48,4,128]{3,2,1,0:T(4,128)(2,1)S(1)}, bf16[17,48,4,128]{3,2,1,0:T(4,128)(2,1)}, u32[]{:S(2)}) copy-start(bf16[17,48,4,128]{3,2,1,0:T(4,128)(2,1)} %param.3) | copy-start | bytes 2506756
  10.2 0.7 %copy-start.1 = (s32[17,2]{0,1:T(2,128)S(1)}, s32[17,2]{0,1:T(2,128)}, u32[]{:S(2)}) copy-start(s32[17,2]{0,1:T(2,128)} %param.4) | copy-start | bytes 412

commit v11 on v9

--- a/solution.py
+++ b/solution.py
@@ -8,6 +8,7 @@
 STEPS = 32700.0
 LEVELS = 128
 SMALLEST = 2.0**-126
+SCALE_ROWS = 8
 
 
 def centre(size):
@@ -40,20 +41,22 @@
 
 
 def stage(size, months, own_blocks, blocks_ref, tiles_ref, sorted_ref, pick_ref):
-    block_count = sorted_ref.shape[0]
-    slot_count = tiles_ref.shape[0]
+    block_count = sorted_ref.shape[0] * own_blocks
+    slot_count, tile_height, cell_count = tiles_ref.shape
     height = pick_ref.shape[0] // 2
     packed_rows = pick_ref.shape[1] // size
     first = blocks_ref[0, 0]
 
-    def clear(block):
-        sorted_ref[block] = jnp.zeros(sorted_ref.shape[1:], sorted_ref.dtype)
+    def clear(owner):
+        sorted_ref[owner] = jnp.zeros(sorted_ref.shape[1:], sorted_ref.dtype)
 
     def place(slot):
         which = (blocks_ref[0, slot] != first).astype(jnp.int32)
-        sorted_ref[blocks_ref[1, slot], which] = tiles_ref[slot]
+        arrival = blocks_ref[1, slot]
+        start = pl.multiple_of(arrival % own_blocks * cell_count, cell_count)
+        sorted_ref[arrival // own_blocks, which, :, pl.ds(start, cell_count)] = tiles_ref[slot]
 
-    each(block_count, clear)
+    each(size, clear)
     each(slot_count, place)
     row = lax.broadcasted_iota(jnp.int32, (height, pick_ref.shape[1]), 0)
     column = lax.broadcasted_iota(jnp.int32, (height, pick_ref.shape[1]), 1)
@@ -65,8 +68,9 @@
 
 def tile_sums(months, histories_ref, pick_ref, sorted_ref, coded_ref):
     size, packed_rows, packed_width = histories_ref.shape
-    block_count, sources, tile_height, cell_count = sorted_ref.shape
-    own_blocks = block_count // size
+    sources, tile_height, row_length = sorted_ref.shape[1:]
+    cell_count = coded_ref.shape[2]
+    own_blocks = row_length // cell_count
     height = pick_ref.shape[0] // sources
 
     column_of = lax.broadcasted_iota(jnp.int32, (packed_width, tile_height), 1) // months
@@ -82,18 +86,16 @@
     coded_rows = own_blocks * height
 
     def code(slot):
-        values = []
-        for block in range(own_blocks):
-            place = device_of(slot, size) * own_blocks + block
-            parts = [
-                jnp.dot(
-                    wide[which * height : (which + 1) * height],
-                    sorted_ref[place, which],
-                    preferred_element_type=jnp.float32,
-                )
-                for which in range(sources)
-            ]
-            values.append(sum(parts[1:], parts[0]))
+        parts = [
+            jnp.dot(
+                wide[which * height : (which + 1) * height],
+                sorted_ref[device_of(slot, size), which],
+                preferred_element_type=jnp.float32,
+            )
+            for which in range(sources)
+        ]
+        total = sum(parts[1:], parts[0])
+        values = [total[:, block * cell_count : (block + 1) * cell_count] for block in range(own_blocks)]
         top = jnp.abs(values[0])
         for value in values[1:]:
             top = jnp.maximum(top, jnp.abs(value))
@@ -103,8 +105,8 @@
         for block, value in enumerate(values):
             steps = jnp.round(value * half * (half * STEPS))
             coded_ref[slot, pl.ds(block * height, height)] = steps.astype(jnp.int32).astype(jnp.int16)
-        spread = jnp.broadcast_to(level.astype(jnp.int32), (16, cell_count))
-        coded_ref[slot, pl.ds(coded_rows, 16)] = spread.astype(jnp.int16)
+        spread = jnp.broadcast_to(level.astype(jnp.int32), (SCALE_ROWS, cell_count))
+        coded_ref[slot, pl.ds(coded_rows, SCALE_ROWS)] = spread.astype(jnp.int16)
 
     each(size, code)
 
@@ -116,7 +118,7 @@
     total_ref[...] = jnp.zeros(total_ref.shape, total_ref.dtype)
 
     def add(slot):
-        level = coded_ref[slot, pl.ds(coded_rows, 16)].astype(jnp.int32).astype(jnp.float32)[:1]
+        level = coded_ref[slot, pl.ds(coded_rows, SCALE_ROWS)].astype(jnp.int32).astype(jnp.float32)[:1]
         half = jnp.exp2(level * (0.5 / LEVELS))
         for block in range(own_blocks):
             steps = coded_ref[slot, pl.ds(block * height, height)].astype(jnp.int32)
@@ -129,7 +131,6 @@
     size = lax.axis_size("tm")
     own_blocks, tracer_count, source_width = histories.shape
     slot_count, source_width, months, cell_count = propagator.shape
-    block_count = size * own_blocks
     height = tracer_count * months
     tile_height = source_width * months
 
@@ -146,7 +147,7 @@
     sorted_tiles, pick = pl.pallas_call(
         lambda *refs: stage(size, months, own_blocks, *refs),
         out_shape=[
-            jax.ShapeDtypeStruct((block_count, 2, tile_height, cell_count), propagator.dtype),
+            jax.ShapeDtypeStruct((size, 2, tile_height, own_blocks * cell_count), propagator.dtype),
             jax.ShapeDtypeStruct((2 * height, size * copies.shape[1]), jnp.bfloat16),
         ],
         in_specs=[smem, vmem],
@@ -157,7 +158,7 @@
 
     coded = pl.pallas_call(
         lambda *refs: tile_sums(months, *refs),
-        out_shape=jax.ShapeDtypeStruct((size, own_blocks * height + 16, cell_count), jnp.int16),
+        out_shape=jax.ShapeDtypeStruct((size, own_blocks * height + SCALE_ROWS, cell_count), jnp.int16),
         in_specs=[vmem, vmem, vmem],
         out_specs=vmem,
         compiler_params=pltpu.CompilerParams(vmem_limit_bytes=20 * 1024 * 1024),

time: 24.9 us -> 24.5 us (0.984)
  Pallas kernels: 2.43 us -> 2.17 us
    pallas_call x1, Pallas kernels: 0.92 us -> 0.66 us  [shards(): pl.pallas_call(lambda *refs: tile_sums(months, *refs), out_shape=jax.Shap...]
where the time goes in v11:
time: 24.5 us; the launch traced here: 24.2 us
  blocking collectives  9.61 us (39%)
  starting transfers between devices  8.26 us (34%)
  local copies, waits for them, and re-layouts  3.16 us (13%)
  Pallas kernels  2.17 us (9%)
  waiting for transfers between devices  0.98 us (4%)
    all_to_all x1, blocking collectives, exchange(): lax.all_to_all(value, 'tm', 0, 0, axis_index_groups=[order], tiled=True)  9.61 us
    all_to_all x1, starting transfers between devices, exchange(): lax.all_to_all(value, 'tm', 0, 0, axis_index_groups=[order], tiled=True)  8.26 us
    unnamed x4, local copies, waits for them, and re-layouts  1.83 us
    pad x2, local copies, waits for them, and re-layouts, shards(): jnp.pad(jnp.broadcast_to(rows, (size, used_rows, source_width)), ((0, 0),...  1.33 us
    all_to_all x1, waiting for transfers between devices, exchange(): lax.all_to_all(value, 'tm', 0, 0, axis_index_groups=[order], tiled=True)  0.98 us
    pallas_call x1, Pallas kernels, shards(): pl.pallas_call(lambda *refs: stage(size, months, own_blocks, *refs), out_...  0.82 us
    pallas_call x1, Pallas kernels, shards(): pl.pallas_call(add_parts, out_shape=jax.ShapeDtypeStruct((own_blocks, hei...  0.69 us
    pallas_call x1, Pallas kernels, shards(): pl.pallas_call(lambda *refs: tile_sums(months, *refs), out_shape=jax.Shap...  0.66 us
  transfers between devices with their start and end apart: 1, of which 1 were waited for; matrix products, arithmetic and copies ran while one was open for 0% of the time, Pallas kernels for 3%

profile of v11, /device:TPU:0, one launch (start us, length us, event | category | flops | bytes accessed | tf_op | source)
XLA Modules:
  0.0 24.2 jit_solution(9474589728537070271)
XLA Ops:
  0.0 0.7 %pad.6 = bf16[32,128]{1,0:T(8,128)(2,1)S(1)} pad(bf16[24,48]{1,0:T(8,128)(2,1)} %bitcast.8, bf16[]{:T(256)} %constant.2.clone.1), padding=0_8x0_80 | pad | bytes 10498 | tf_op jit(solution)/shard_map/jit(_pad)/pad | solution.py:139
  0.7 0.6 %pad.7 = bf16[8,32,128]{2,1,0:T(8,128)(2,1)} broadcast(bf16[32,128]{1,0:T(8,128)(2,1)S(1)} %pad.6), dimensions={1,2} | broadcast | bytes 73728 | tf_op jit(solution)/shard_map/jit(_pad)/pad | solution.py:139
  1.3 8.3 %all-to-all-start = ((bf16[8,32,128]{2,1,0:T(8,128)(2,1)}), bf16[8,32,128]{2,1,0:T(8,128)(2,1)S(1)}, u32[]{:S(2)}, u32[]{:S(2)}) async-start(bf16[8,32,128]{2,1,0:T(8,128)(2,1)} %pad.7), calls=%async_computation | async-start | bytes 131072 | tf_op jit(solution)/shard_map/all_to_all | solution.py:32
  9.6 0.0 copy-start
  9.6 1.1 %copy-done = bf16[17,48,4,128]{3,2,1,0:T(4,128)(2,1)S(1)} copy-done((bf16[17,48,4,128]{3,2,1,0:T(4,128)(2,1)S(1)}, bf16[17,48,4,128]{3,2,1,0:T(4,128)(2,1)}, u32[]{:S(2)}) %copy-start) | copy-done | bytes 835608
  10.7 0.0 copy-start.1
  10.7 0.7 %copy-done.1 = s32[17,2]{0,1:T(2,128)S(1)} copy-done((s32[17,2]{0,1:T(2,128)S(1)}, s32[17,2]{0,1:T(2,128)}, u32[]{:S(2)}) %copy-start.1) | copy-done | bytes 160
  11.4 0.8 %shard_map.37 = (bf16[8,2,192,256]{3,2,1,0:T(8,128)(2,1)S(1)}, bf16[96,256]{1,0:T(8,128)(2,1)S(1)}) custom-call(s32[2,17]{1,0:T(2,128)S(1)} %bitcast.7, bf16[17,192,128]{2,1,0:T(8,128)(2,1)S(1)} %bitcast.6), custom_call_target="tpu_custom_call" | custom-call | bytes 1671168 | tf_op jit(solution)/shard_map/pallas_call | solution.py:147
  12.2 1.0 %all-to-all-done.refs_0_ = bf16[8,32,128]{2,1,0:T(8,128)(2,1)S(1)} async-done(((bf16[8,32,128]{2,1,0:T(8,128)(2,1)}), bf16[8,32,128]{2,1,0:T(8,128)(2,1)S(1)}, u32[]{:S(2)}, u32[]{:S(2)}) %all-to-all-start) | async-done | bytes 65568 | tf_op jit(solution)/shard_map/all_to_all | solution.py:32
  13.2 0.7 %shard_map.38 = s16[8,104,128]{2,1,0:T(8,128)(2,1)S(1)} custom-call(bf16[8,32,128]{2,1,0:T(8,128)(2,1)S(1)} %all-to-all-done.refs_0_, bf16[96,256]{1,0:T(8,128)(2,1)S(1)} %get-tuple-element.7.refs_1_, bf16[8,2,192,256]{3,2,1,0:T(8,128)(2,1)S(1)} %get-tuple-element.8.refs_2_), custom_call_target="tpu_custom_call" | custom-call | flops 40108032 | bytes 1671168 | tf_op jit(solution)/shard_map/pallas_call | solution.py:159
  13.9 9.6 %all_to_all.10.coded_ref = s16[8,104,128]{2,1,0:T(8,128)(2,1)S(1)} all-to-all(s16[8,104,128]{2,1,0:T(8,128)(2,1)S(1)} %shard_map.38), channel_id=1, replica_groups={{10,2,4,6,8,12,14,0},{11,3,5,7,9,13,15,1},{26,18,20,22,24,28,30,16},{27..., dimensions={0} | all-to-all | bytes 425984 | tf_op jit(solution)/shard_map/all_to_all | solution.py:32
  23.5 0.7 %shard_map.39 = f32[2,48,128]{2,1,0:T(8,128)} custom-call(s16[8,104,128]{2,1,0:T(8,128)(2,1)S(1)} %all_to_all.10.coded_ref), custom_call_target="tpu_custom_call" | custom-call | tf_op jit(solution)/shard_map/pallas_call | solution.py:172
Async XLA Ops:
  1.3 11.9 %all-to-all-start = ((bf16[8,32,128]{2,1,0:T(8,128)(2,1)}), bf16[8,32,128]{2,1,0:T(8,128)(2,1)S(1)}, u32[]{:S(2)}, u32[]{:S(2)}) async-start(bf16[8,32,128]{2,1,0:T(8,128)(2,1)} %pad.7), calls=%async_computation | async-start | bytes 131072 | tf_op jit(solution)/shard_map/all_to_all | solution.py:32
  9.6 1.1 %copy-start = (bf16[17,48,4,128]{3,2,1,0:T(4,128)(2,1)S(1)}, bf16[17,48,4,128]{3,2,1,0:T(4,128)(2,1)}, u32[]{:S(2)}) copy-start(bf16[17,48,4,128]{3,2,1,0:T(4,128)(2,1)} %param.3) | copy-start | bytes 2506756
  10.7 0.7 %copy-start.1 = (s32[17,2]{0,1:T(2,128)S(1)}, s32[17,2]{0,1:T(2,128)}, u32[]{:S(2)}) copy-start(s32[17,2]{0,1:T(2,128)} %param.4) | copy-start | bytes 412

commit v12 on v11

--- a/solution.py
+++ b/solution.py
@@ -40,15 +40,34 @@
         lax.fori_loop(0, count, lambda index, carry: (body(index), carry)[1], 0)
 
 
-def stage(size, months, own_blocks, blocks_ref, tiles_ref, sorted_ref, pick_ref):
+def spread(rows_in, copies_ref, rows_ref, semaphore):
+    used_rows, source_width = rows_ref.shape
+    load = pltpu.make_async_copy(rows_in, rows_ref, semaphore)
+    load.start()
+    copies_ref[...] = jnp.zeros(copies_ref.shape, copies_ref.dtype)
+    load.wait()
+    for slot in range(copies_ref.shape[0]):
+        copies_ref[slot, :used_rows, :source_width] = rows_ref[...]
+
+
+def stage(
+    size, months, own_blocks, blocks_in, tiles_in, sorted_ref, pick_ref, blocks_ref, tiles_ref, semaphores
+):
     block_count = sorted_ref.shape[0] * own_blocks
     slot_count, tile_height, cell_count = tiles_ref.shape
     height = pick_ref.shape[0] // 2
     packed_rows = pick_ref.shape[1] // size
-    first = blocks_ref[0, 0]
+    load_blocks = pltpu.make_async_copy(blocks_in, blocks_ref, semaphores.at[0])
+    load_tiles = pltpu.make_async_copy(tiles_in, tiles_ref, semaphores.at[1])
+    load_blocks.start()
+    load_tiles.start()
 
     def clear(owner):
         sorted_ref[owner] = jnp.zeros(sorted_ref.shape[1:], sorted_ref.dtype)
+
+    each(size, clear)
+    load_blocks.wait()
+    first = blocks_ref[0, 0]
 
     def place(slot):
         which = (blocks_ref[0, slot] != first).astype(jnp.int32)
@@ -56,14 +75,14 @@
         start = pl.multiple_of(arrival % own_blocks * cell_count, cell_count)
         sorted_ref[arrival // own_blocks, which, :, pl.ds(start, cell_count)] = tiles_ref[slot]
 
-    each(size, clear)
-    each(slot_count, place)
     row = lax.broadcasted_iota(jnp.int32, (height, pick_ref.shape[1]), 0)
     column = lax.broadcasted_iota(jnp.int32, (height, pick_ref.shape[1]), 1)
     for which, source in enumerate((first, block_count - 1 - first)):
         start = slot_of(source // own_blocks, size) * packed_rows + source % own_blocks
         picked = column == start + row // months * own_blocks
         pick_ref[pl.ds(which * height, height)] = picked.astype(jnp.bfloat16)
+    load_tiles.wait()
+    each(slot_count, place)
 
 
 def tile_sums(months, histories_ref, pick_ref, sorted_ref, coded_ref):
@@ -135,26 +154,41 @@
     tile_height = source_width * months
 
     used_rows = tracer_count * own_blocks
-    rows = jnp.swapaxes(histories, 0, 1).reshape(1, used_rows, source_width)
-    copies = jnp.pad(
-        jnp.broadcast_to(rows, (size, used_rows, source_width)),
-        ((0, 0), (0, -used_rows % 16), (0, -source_width % 128)),
-    )
+    rows = jnp.swapaxes(histories, 0, 1).reshape(used_rows, source_width)
+    packed_shape = (used_rows + -used_rows % 16, source_width + -source_width % 128)
+    vmem = pl.BlockSpec(memory_space=pltpu.VMEM)
+    hbm = pl.BlockSpec(memory_space=pltpu.HBM)
+    copies = pl.pallas_call(
+        spread,
+        out_shape=pltpu.VMEM((size,) + packed_shape, histories.dtype),
+        in_specs=[hbm],
+        out_specs=vmem,
+        scratch_shapes=[pltpu.VMEM(rows.shape, rows.dtype), pltpu.SemaphoreType.DMA],
+        compiler_params=pltpu.CompilerParams(vmem_limit_bytes=4 * 1024 * 1024),
+    )(pltpu.with_memory_space_constraint(rows, pltpu.HBM))
     received = exchange(copies, size)
 
-    vmem = pl.BlockSpec(memory_space=pltpu.VMEM)
-    smem = pl.BlockSpec(memory_space=pltpu.SMEM)
+    blocks = tile_blocks.T
+    tiles = propagator.reshape(slot_count, tile_height, cell_count)
     sorted_tiles, pick = pl.pallas_call(
         lambda *refs: stage(size, months, own_blocks, *refs),
         out_shape=[
-            jax.ShapeDtypeStruct((size, 2, tile_height, own_blocks * cell_count), propagator.dtype),
+            jax.ShapeDtypeStruct((size, 2, tile_height, own_blocks * cell_count), tiles.dtype),
             jax.ShapeDtypeStruct((2 * height, size * copies.shape[1]), jnp.bfloat16),
         ],
-        in_specs=[smem, vmem],
+        in_specs=[hbm, hbm],
         out_specs=[vmem, vmem],
-        compiler_params=pltpu.CompilerParams(vmem_limit_bytes=20 * 1024 * 1024),
-        cost_estimate=pl.CostEstimate(flops=0, bytes_accessed=propagator.size * 4, transcendentals=0),
-    )(tile_blocks.T, propagator.reshape(slot_count, tile_height, cell_count))
+        scratch_shapes=[
+            pltpu.SMEM(blocks.shape, blocks.dtype),
+            pltpu.VMEM(tiles.shape, tiles.dtype),
+            pltpu.SemaphoreType.DMA((2,)),
+        ],
+        compiler_params=pltpu.CompilerParams(vmem_limit_bytes=24 * 1024 * 1024),
+        cost_estimate=pl.CostEstimate(flops=0, bytes_accessed=tiles.size * 4, transcendentals=0),
+    )(
+        pltpu.with_memory_space_constraint(blocks, pltpu.HBM),
+        pltpu.with_memory_space_constraint(tiles, pltpu.HBM),
+    )
 
     coded = pl.pallas_call(
         lambda *refs: tile_sums(months, *refs),

time: 24.5 us -> 24.5 us (level)
  local copies, waits for them, and re-layouts: 3.16 us -> 0 us
  Pallas kernels: 2.17 us -> 4.02 us
  waiting for transfers between devices: 0.98 us -> 2.28 us
    unnamed x4 -> x0, local copies, waits for them, and re-layouts: 1.83 us -> none
    pad x2 -> x0, local copies, waits for them, and re-layouts: 1.33 us -> none  [shards(): jnp.pad(jnp.broadcast_to(rows, (size, used_rows, source_width)), ((0, 0),...]
    pallas_call x0 -> x1, Pallas kernels: none -> 1.32 us  [shards(): pl.pallas_call(spread, out_shape=pltpu.VMEM((size,) + packed_shape, histo...]
    all_to_all x1, waiting for transfers between devices: 0.98 us -> 2.28 us  [exchange(): lax.all_to_all(value, 'tm', 0, 0, axis_index_groups=[order], tiled=True)]
    pallas_call x1, Pallas kernels: 0.82 us -> 1.35 us  [shards(): pl.pallas_call(lambda *refs: stage(size, months, own_blocks, *refs), out_...]
  transfers between devices with their start and end apart: 1 -> 1, of which waited for: 1 -> 1; matrix products, arithmetic and copies ran while one was open for 0% -> 0% of each run, Pallas kernels for 3% -> 6%
where the time goes in v12:
time: 24.5 us; the launch traced here: 24.2 us
  blocking collectives  9.61 us (39%)
  starting transfers between devices  8.27 us (34%)
  Pallas kernels  4.02 us (16%)
  waiting for transfers between devices  2.28 us (9%)
    all_to_all x1, blocking collectives, exchange(): lax.all_to_all(value, 'tm', 0, 0, axis_index_groups=[order], tiled=True)  9.61 us
    all_to_all x1, starting transfers between devices, exchange(): lax.all_to_all(value, 'tm', 0, 0, axis_index_groups=[order], tiled=True)  8.27 us
    all_to_all x1, waiting for transfers between devices, exchange(): lax.all_to_all(value, 'tm', 0, 0, axis_index_groups=[order], tiled=True)  2.28 us
    pallas_call x1, Pallas kernels, shards(): pl.pallas_call(lambda *refs: stage(size, months, own_blocks, *refs), out_...  1.35 us
    pallas_call x1, Pallas kernels, shards(): pl.pallas_call(spread, out_shape=pltpu.VMEM((size,) + packed_shape, histo...  1.32 us
    pallas_call x1, Pallas kernels, shards(): pl.pallas_call(add_parts, out_shape=jax.ShapeDtypeStruct((own_blocks, hei...  0.69 us
    pallas_call x1, Pallas kernels, shards(): pl.pallas_call(lambda *refs: tile_sums(months, *refs), out_shape=jax.Shap...  0.66 us
  transfers between devices with their start and end apart: 1, of which 1 were waited for; matrix products, arithmetic and copies ran while one was open for 0% of the time, Pallas kernels for 6%

profile of v12, /device:TPU:0, one launch (start us, length us, event | category | flops | bytes accessed | tf_op | source)
XLA Modules:
  0.0 24.2 jit_solution(7558883958399620912)
XLA Ops:
  0.0 1.3 %shard_map.37 = bf16[8,32,128]{2,1,0:T(8,128)(2,1)} custom-call(bf16[24,48]{1,0:T(8,128)(2,1)} %bitcast.7), custom_call_target="tpu_custom_call" | custom-call | tf_op jit(solution)/shard_map/pallas_call | solution.py:161
  1.3 8.3 %all-to-all-start = ((bf16[8,32,128]{2,1,0:T(8,128)(2,1)}), bf16[8,32,128]{2,1,0:T(8,128)(2,1)S(1)}, u32[]{:S(2)}, u32[]{:S(2)}) async-start(bf16[8,32,128]{2,1,0:T(8,128)(2,1)} %shard_map.37), calls=%async_computation | async-start | bytes 131072 | tf_op jit(solution)/shard_map/all_to_all | solution.py:32
  9.6 1.4 %shard_map.38 = (bf16[8,2,192,256]{3,2,1,0:T(8,128)(2,1)S(1)}, bf16[96,256]{1,0:T(8,128)(2,1)S(1)}) custom-call(s32[2,17]{1,0:T(2,128)} %bitcast.8, bf16[17,192,128]{2,1,0:T(8,128)(2,1)} %bitcast.6), custom_call_target="tpu_custom_call" | custom-call | bytes 1671168 | tf_op jit(solution)/shard_map/pallas_call | solution.py:173
  11.0 2.3 %all-to-all-done.refs_0_ = bf16[8,32,128]{2,1,0:T(8,128)(2,1)S(1)} async-done(((bf16[8,32,128]{2,1,0:T(8,128)(2,1)}), bf16[8,32,128]{2,1,0:T(8,128)(2,1)S(1)}, u32[]{:S(2)}, u32[]{:S(2)}) %all-to-all-start) | async-done | bytes 65568 | tf_op jit(solution)/shard_map/all_to_all | solution.py:32
  13.2 0.7 %shard_map.39 = s16[8,104,128]{2,1,0:T(8,128)(2,1)S(1)} custom-call(bf16[8,32,128]{2,1,0:T(8,128)(2,1)S(1)} %all-to-all-done.refs_0_, bf16[96,256]{1,0:T(8,128)(2,1)S(1)} %get-tuple-element.7.refs_1_, bf16[8,2,192,256]{3,2,1,0:T(8,128)(2,1)S(1)} %get-tuple-element.8.refs_2_), custom_call_target="tpu_custom_call" | custom-call | flops 40108032 | bytes 1671168 | tf_op jit(solution)/shard_map/pallas_call | solution.py:193
  13.9 9.6 %all_to_all.10.coded_ref = s16[8,104,128]{2,1,0:T(8,128)(2,1)S(1)} all-to-all(s16[8,104,128]{2,1,0:T(8,128)(2,1)S(1)} %shard_map.39), channel_id=1, replica_groups={{10,2,4,6,8,12,14,0},{11,3,5,7,9,13,15,1},{26,18,20,22,24,28,30,16},{27..., dimensions={0} | all-to-all | bytes 425984 | tf_op jit(solution)/shard_map/all_to_all | solution.py:32
  23.5 0.7 %shard_map.40 = f32[2,48,128]{2,1,0:T(8,128)} custom-call(s16[8,104,128]{2,1,0:T(8,128)(2,1)S(1)} %all_to_all.10.coded_ref), custom_call_target="tpu_custom_call" | custom-call | tf_op jit(solution)/shard_map/pallas_call | solution.py:206
Async XLA Ops:
  1.3 11.9 %all-to-all-start = ((bf16[8,32,128]{2,1,0:T(8,128)(2,1)}), bf16[8,32,128]{2,1,0:T(8,128)(2,1)S(1)}, u32[]{:S(2)}, u32[]{:S(2)}) async-start(bf16[8,32,128]{2,1,0:T(8,128)(2,1)} %shard_map.37), calls=%async_computation | async-start | bytes 131072 | tf_op jit(solution)/shard_map/all_to_all | solution.py:32

commit v13 on v11

--- a/solution.py
+++ b/solution.py
@@ -40,15 +40,50 @@
         lax.fori_loop(0, count, lambda index, carry: (body(index), carry)[1], 0)
 
 
-def stage(size, months, own_blocks, blocks_ref, tiles_ref, sorted_ref, pick_ref):
-    block_count = sorted_ref.shape[0] * own_blocks
+def prepare(
+    months,
+    rows_in,
+    blocks_in,
+    tiles_in,
+    copies_ref,
+    sorted_ref,
+    pick_ref,
+    rows_ref,
+    blocks_ref,
+    tiles_ref,
+    semaphores,
+):
+    size, packed_rows, packed_width = copies_ref.shape
     slot_count, tile_height, cell_count = tiles_ref.shape
+    used_rows, source_width = rows_ref.shape
+    own_blocks = sorted_ref.shape[3] // cell_count
     height = pick_ref.shape[0] // 2
-    packed_rows = pick_ref.shape[1] // size
-    first = blocks_ref[0, 0]
+    loads = [
+        pltpu.make_async_copy(source, target, semaphores.at[index])
+        for index, (source, target) in enumerate(
+            [(tiles_in, tiles_ref), (blocks_in, blocks_ref), (rows_in, rows_ref)]
+        )
+    ]
+    for load in loads:
+        load.start()
 
     def clear(owner):
         sorted_ref[owner] = jnp.zeros(sorted_ref.shape[1:], sorted_ref.dtype)
+        copies_ref[owner] = jnp.zeros(copies_ref.shape[1:], copies_ref.dtype)
+
+    each(size, clear)
+    loads[1].wait()
+    first = blocks_ref[0, 0]
+    row = lax.broadcasted_iota(jnp.int32, (height, pick_ref.shape[1]), 0)
+    column = lax.broadcasted_iota(jnp.int32, (height, pick_ref.shape[1]), 1)
+    for which, source in enumerate((first, size * own_blocks - 1 - first)):
+        start = slot_of(source // own_blocks, size) * packed_rows + source % own_blocks
+        picked = column == start + row // months * own_blocks
+        pick_ref[pl.ds(which * height, height)] = picked.astype(jnp.bfloat16)
+    loads[2].wait()
+
+    def copy(owner):
+        copies_ref[owner, :used_rows, :source_width] = rows_ref[...]
 
     def place(slot):
         which = (blocks_ref[0, slot] != first).astype(jnp.int32)
@@ -56,14 +91,9 @@
         start = pl.multiple_of(arrival % own_blocks * cell_count, cell_count)
         sorted_ref[arrival // own_blocks, which, :, pl.ds(start, cell_count)] = tiles_ref[slot]
 
-    each(size, clear)
+    each(size, copy)
+    loads[0].wait()
     each(slot_count, place)
-    row = lax.broadcasted_iota(jnp.int32, (height, pick_ref.shape[1]), 0)
-    column = lax.broadcasted_iota(jnp.int32, (height, pick_ref.shape[1]), 1)
-    for which, source in enumerate((first, block_count - 1 - first)):
-        start = slot_of(source // own_blocks, size) * packed_rows + source % own_blocks
-        picked = column == start + row // months * own_blocks
-        pick_ref[pl.ds(which * height, height)] = picked.astype(jnp.bfloat16)
 
 
 def tile_sums(months, histories_ref, pick_ref, sorted_ref, coded_ref):
@@ -135,26 +165,32 @@
     tile_height = source_width * months
 
     used_rows = tracer_count * own_blocks
-    rows = jnp.swapaxes(histories, 0, 1).reshape(1, used_rows, source_width)
-    copies = jnp.pad(
-        jnp.broadcast_to(rows, (size, used_rows, source_width)),
-        ((0, 0), (0, -used_rows % 16), (0, -source_width % 128)),
-    )
+    packed_rows = used_rows + -used_rows % 16
+    packed_width = source_width + -source_width % 128
+    rows = jnp.swapaxes(histories, 0, 1).reshape(used_rows, source_width)
+    blocks = tile_blocks.T
+    tiles = propagator.reshape(slot_count, tile_height, cell_count)
+    vmem = pl.BlockSpec(memory_space=pltpu.VMEM)
+    hbm = pl.BlockSpec(memory_space=pltpu.HBM)
+    copies, sorted_tiles, pick = pl.pallas_call(
+        lambda *refs: prepare(months, *refs),
+        out_shape=[
+            jax.ShapeDtypeStruct((size, packed_rows, packed_width), rows.dtype),
+            jax.ShapeDtypeStruct((size, 2, tile_height, own_blocks * cell_count), tiles.dtype),
+            jax.ShapeDtypeStruct((2 * height, size * packed_rows), jnp.bfloat16),
+        ],
+        in_specs=[hbm, hbm, hbm],
+        out_specs=[vmem, vmem, vmem],
+        scratch_shapes=[
+            pltpu.VMEM(rows.shape, rows.dtype),
+            pltpu.SMEM(blocks.shape, blocks.dtype),
+            pltpu.VMEM(tiles.shape, tiles.dtype),
+            pltpu.SemaphoreType.DMA((3,)),
+        ],
+        compiler_params=pltpu.CompilerParams(vmem_limit_bytes=24 * 1024 * 1024),
+        cost_estimate=pl.CostEstimate(flops=0, bytes_accessed=tiles.size * 4, transcendentals=0),
+    )(*(pltpu.with_memory_space_constraint(value, pltpu.HBM) for value in (rows, blocks, tiles)))
     received = exchange(copies, size)
-
-    vmem = pl.BlockSpec(memory_space=pltpu.VMEM)
-    smem = pl.BlockSpec(memory_space=pltpu.SMEM)
-    sorted_tiles, pick = pl.pallas_call(
-        lambda *refs: stage(size, months, own_blocks, *refs),
-        out_shape=[
-            jax.ShapeDtypeStruct((size, 2, tile_height, own_blocks * cell_count), propagator.dtype),
-            jax.ShapeDtypeStruct((2 * height, size * copies.shape[1]), jnp.bfloat16),
-        ],
-        in_specs=[smem, vmem],
-        out_specs=[vmem, vmem],
-        compiler_params=pltpu.CompilerParams(vmem_limit_bytes=20 * 1024 * 1024),
-        cost_estimate=pl.CostEstimate(flops=0, bytes_accessed=propagator.size * 4, transcendentals=0),
-    )(tile_blocks.T, propagator.reshape(slot_count, tile_height, cell_count))
 
     coded = pl.pallas_call(
         lambda *refs: tile_sums(months, *refs),

time: 24.5 us -> 23.9 us (0.976)
  blocking collectives: 9.61 us -> 20.9 us
  starting transfers between devices: 8.26 us -> 0 us
  local copies, waits for them, and re-layouts: 3.16 us -> 0 us
  waiting for transfers between devices: 0.98 us -> 0 us
  Pallas kernels: 2.17 us -> 2.71 us
    all_to_all x1 -> x2, blocking collectives: 9.61 us -> 20.9 us  [exchange(): lax.all_to_all(value, 'tm', 0, 0, axis_index_groups=[order], tiled=True)]
    all_to_all x1 -> x0, starting transfers between devices: 8.26 us -> none  [exchange(): lax.all_to_all(value, 'tm', 0, 0, axis_index_groups=[order], tiled=True)]
    unnamed x4 -> x0, local copies, waits for them, and re-layouts: 1.83 us -> none
    pad x2 -> x0, local copies, waits for them, and re-layouts: 1.33 us -> none  [shards(): jnp.pad(jnp.broadcast_to(rows, (size, used_rows, source_width)), ((0, 0),...]
    all_to_all x1 -> x0, waiting for transfers between devices: 0.98 us -> none  [exchange(): lax.all_to_all(value, 'tm', 0, 0, axis_index_groups=[order], tiled=True)]
    pallas_call x1, Pallas kernels: 0.82 us -> 1.36 us  [shards(): pl.pallas_call(lambda *refs: prepare(months, *refs), out_shape=[jax.Shape...]
  transfers between devices with their start and end apart: 1 -> 0, of which waited for: 1 -> 0; matrix products, arithmetic and copies ran while one was open for 0% -> 0% of each run, Pallas kernels for 3% -> 0%
where the time goes in v13:
time: 23.9 us; the launch traced here: 23.6 us
  blocking collectives  20.9 us (87%)
  Pallas kernels  2.71 us (11%)
    all_to_all x2, blocking collectives, exchange(): lax.all_to_all(value, 'tm', 0, 0, axis_index_groups=[order], tiled=True)  20.9 us
    pallas_call x1, Pallas kernels, shards(): pl.pallas_call(lambda *refs: prepare(months, *refs), out_shape=[jax.Shape...  1.36 us
    pallas_call x1, Pallas kernels, shards(): pl.pallas_call(add_parts, out_shape=jax.ShapeDtypeStruct((own_blocks, hei...  0.69 us
    pallas_call x1, Pallas kernels, shards(): pl.pallas_call(lambda *refs: tile_sums(months, *refs), out_shape=jax.Shap...  0.66 us

profile of v13, /device:TPU:0, one launch (start us, length us, event | category | flops | bytes accessed | tf_op | source)
XLA Modules:
  0.0 23.6 jit_solution(17256104863930934709)
XLA Ops:
  0.0 1.4 %shard_map.37 = (bf16[8,32,128]{2,1,0:T(8,128)(2,1)S(1)}, bf16[8,2,192,256]{3,2,1,0:T(8,128)(2,1)S(1)}, bf16[96,256]{1,0:T(8,128)(2,1)S(1)}) custom-call(bf16[24,48]{1,0:T(8,128)(2,1)} %bitcast.7, s32[2,17]{1,0:T(2,128)} %bitcast.8, bf16[17,192,128]{2,1,0:T(8,128)(2,1)} %bitcast.6), custom_call_target="tpu_custom_call" | custom-call | bytes 1671168 | tf_op jit(solution)/shard_map/pallas_call | solution.py:175
  1.4 11.3 %all_to_all.10.refs_0_ = bf16[8,32,128]{2,1,0:T(8,128)(2,1)S(1)} all-to-all(bf16[8,32,128]{2,1,0:T(8,128)(2,1)S(1)} %get-tuple-element.8), channel_id=1, replica_groups={{10,2,4,6,8,12,14,0},{11,3,5,7,9,13,15,1},{26,18,20,22,24,28,30,16},{27..., dimensions={0} | all-to-all | bytes 131072 | tf_op jit(solution)/shard_map/all_to_all | solution.py:32
  12.6 0.7 %shard_map.38 = s16[8,104,128]{2,1,0:T(8,128)(2,1)S(1)} custom-call(bf16[8,32,128]{2,1,0:T(8,128)(2,1)S(1)} %all_to_all.10.refs_0_, bf16[96,256]{1,0:T(8,128)(2,1)S(1)} %get-tuple-element.9.refs_1_, bf16[8,2,192,256]{3,2,1,0:T(8,128)(2,1)S(1)} %get-tuple-element.10.refs_2_), custom_call_target="tpu_custom_call" | custom-call | flops 40108032 | bytes 1671168 | tf_op jit(solution)/shard_map/pallas_call | solution.py:195
  13.3 9.6 %all_to_all.11.coded_ref = s16[8,104,128]{2,1,0:T(8,128)(2,1)S(1)} all-to-all(s16[8,104,128]{2,1,0:T(8,128)(2,1)S(1)} %shard_map.38), channel_id=1, replica_groups={{10,2,4,6,8,12,14,0},{11,3,5,7,9,13,15,1},{26,18,20,22,24,28,30,16},{27..., dimensions={0} | all-to-all | bytes 425984 | tf_op jit(solution)/shard_map/all_to_all | solution.py:32
  22.9 0.7 %shard_map.39 = f32[2,48,128]{2,1,0:T(8,128)} custom-call(s16[8,104,128]{2,1,0:T(8,128)(2,1)S(1)} %all_to_all.11.coded_ref), custom_call_target="tpu_custom_call" | custom-call | tf_op jit(solution)/shard_map/pallas_call | solution.py:208

commit v14 on v13

--- a/solution.py
+++ b/solution.py
@@ -9,6 +9,7 @@
 LEVELS = 128
 SMALLEST = 2.0**-126
 SCALE_ROWS = 8
+PARTS = 6
 
 
 def centre(size):
@@ -58,13 +59,20 @@
     used_rows, source_width = rows_ref.shape
     own_blocks = sorted_ref.shape[3] // cell_count
     height = pick_ref.shape[0] // 2
-    loads = [
-        pltpu.make_async_copy(source, target, semaphores.at[index])
-        for index, (source, target) in enumerate(
-            [(tiles_in, tiles_ref), (blocks_in, blocks_ref), (rows_in, rows_ref)]
+    load_blocks = pltpu.make_async_copy(blocks_in, blocks_ref, semaphores.at[0])
+    load_rows = pltpu.make_async_copy(rows_in, rows_ref, semaphores.at[1])
+    parts = [range(slot_count * part // PARTS, slot_count * (part + 1) // PARTS) for part in range(PARTS)]
+    load_parts = [
+        pltpu.make_async_copy(
+            tiles_in.at[pl.ds(part.start, len(part))],
+            tiles_ref.at[pl.ds(part.start, len(part))],
+            semaphores.at[2 + index],
         )
+        for index, part in enumerate(parts)
     ]
-    for load in loads:
+    load_blocks.start()
+    load_rows.start()
+    for load in load_parts:
         load.start()
 
     def clear(owner):
@@ -72,7 +80,7 @@
         copies_ref[owner] = jnp.zeros(copies_ref.shape[1:], copies_ref.dtype)
 
     each(size, clear)
-    loads[1].wait()
+    load_blocks.wait()
     first = blocks_ref[0, 0]
     row = lax.broadcasted_iota(jnp.int32, (height, pick_ref.shape[1]), 0)
     column = lax.broadcasted_iota(jnp.int32, (height, pick_ref.shape[1]), 1)
@@ -80,7 +88,7 @@
         start = slot_of(source // own_blocks, size) * packed_rows + source % own_blocks
         picked = column == start + row // months * own_blocks
         pick_ref[pl.ds(which * height, height)] = picked.astype(jnp.bfloat16)
-    loads[2].wait()
+    load_rows.wait()
 
     def copy(owner):
         copies_ref[owner, :used_rows, :source_width] = rows_ref[...]
@@ -92,8 +100,9 @@
         sorted_ref[arrival // own_blocks, which, :, pl.ds(start, cell_count)] = tiles_ref[slot]
 
     each(size, copy)
-    loads[0].wait()
-    each(slot_count, place)
+    for load, part in zip(load_parts, parts):
+        load.wait()
+        each(len(part), lambda slot: place(part.start + slot))
 
 
 def tile_sums(months, histories_ref, pick_ref, sorted_ref, coded_ref):
@@ -185,7 +194,7 @@
             pltpu.VMEM(rows.shape, rows.dtype),
             pltpu.SMEM(blocks.shape, blocks.dtype),
             pltpu.VMEM(tiles.shape, tiles.dtype),
-            pltpu.SemaphoreType.DMA((3,)),
+            pltpu.SemaphoreType.DMA((2 + PARTS,)),
         ],
         compiler_params=pltpu.CompilerParams(vmem_limit_bytes=24 * 1024 * 1024),
         cost_estimate=pl.CostEstimate(flops=0, bytes_accessed=tiles.size * 4, transcendentals=0),

time: 23.9 us -> 23.8 us (level)
  no operation moved by 1% of the time
where the time goes in v14:
time: 23.8 us; the launch traced here: 23.6 us
  blocking collectives  20.9 us (88%)
  Pallas kernels  2.69 us (11%)
    all_to_all x2, blocking collectives, exchange(): lax.all_to_all(value, 'tm', 0, 0, axis_index_groups=[order], tiled=True)  20.9 us
    pallas_call x1, Pallas kernels, shards(): pl.pallas_call(lambda *refs: prepare(months, *refs), out_shape=[jax.Shape...  1.34 us
    pallas_call x1, Pallas kernels, shards(): pl.pallas_call(add_parts, out_shape=jax.ShapeDtypeStruct((own_blocks, hei...  0.69 us
    pallas_call x1, Pallas kernels, shards(): pl.pallas_call(lambda *refs: tile_sums(months, *refs), out_shape=jax.Shap...  0.66 us

profile of v14, /device:TPU:0, one launch (start us, length us, event | category | flops | bytes accessed | tf_op | source)
XLA Modules:
  0.0 23.6 jit_solution(10285449842169109838)
XLA Ops:
  0.0 1.3 %shard_map.37 = (bf16[8,32,128]{2,1,0:T(8,128)(2,1)S(1)}, bf16[8,2,192,256]{3,2,1,0:T(8,128)(2,1)S(1)}, bf16[96,256]{1,0:T(8,128)(2,1)S(1)}) custom-call(bf16[24,48]{1,0:T(8,128)(2,1)} %bitcast.7, s32[2,17]{1,0:T(2,128)} %bitcast.8, bf16[17,192,128]{2,1,0:T(8,128)(2,1)} %bitcast.6), custom_call_target="tpu_custom_call" | custom-call | bytes 1671168 | tf_op jit(solution)/shard_map/pallas_call | solution.py:184
  1.3 11.3 %all_to_all.10.refs_0_ = bf16[8,32,128]{2,1,0:T(8,128)(2,1)S(1)} all-to-all(bf16[8,32,128]{2,1,0:T(8,128)(2,1)S(1)} %get-tuple-element.8), channel_id=1, replica_groups={{10,2,4,6,8,12,14,0},{11,3,5,7,9,13,15,1},{26,18,20,22,24,28,30,16},{27..., dimensions={0} | all-to-all | bytes 131072 | tf_op jit(solution)/shard_map/all_to_all | solution.py:33
  12.6 0.7 %shard_map.38 = s16[8,104,128]{2,1,0:T(8,128)(2,1)S(1)} custom-call(bf16[8,32,128]{2,1,0:T(8,128)(2,1)S(1)} %all_to_all.10.refs_0_, bf16[96,256]{1,0:T(8,128)(2,1)S(1)} %get-tuple-element.9.refs_1_, bf16[8,2,192,256]{3,2,1,0:T(8,128)(2,1)S(1)} %get-tuple-element.10.refs_2_), custom_call_target="tpu_custom_call" | custom-call | flops 40108032 | bytes 1671168 | tf_op jit(solution)/shard_map/pallas_call | solution.py:204
  13.3 9.6 %all_to_all.11.coded_ref = s16[8,104,128]{2,1,0:T(8,128)(2,1)S(1)} all-to-all(s16[8,104,128]{2,1,0:T(8,128)(2,1)S(1)} %shard_map.38), channel_id=1, replica_groups={{10,2,4,6,8,12,14,0},{11,3,5,7,9,13,15,1},{26,18,20,22,24,28,30,16},{27..., dimensions={0} | all-to-all | bytes 425984 | tf_op jit(solution)/shard_map/all_to_all | solution.py:33
  22.9 0.7 %shard_map.39 = f32[2,48,128]{2,1,0:T(8,128)} custom-call(s16[8,104,128]{2,1,0:T(8,128)(2,1)S(1)} %all_to_all.11.coded_ref), custom_call_target="tpu_custom_call" | custom-call | tf_op jit(solution)/shard_map/pallas_call | solution.py:217

commit v15 on v14

--- a/solution.py
+++ b/solution.py
@@ -16,20 +16,19 @@
     return size * 5 // 8
 
 
-def slot_of(device, size):
-    after = device - (device > centre(size)).astype(jnp.int32)
-    return jnp.where(device == centre(size), 0, jnp.where(device == 0, size - 1, after))
-
-
-def device_of(slot, size):
+def history_slot(device, size):
+    rest = size + 2 - device - (device < centre(size)).astype(jnp.int32)
+    return jnp.where(device == centre(size), 0, jnp.where(device < 2, 2 - device, rest))
+
+
+def sums_device(slot, size):
     if isinstance(slot, int):
         return centre(size) if slot == 0 else 0 if slot == size - 1 else slot + (slot >= centre(size))
     after = slot + (slot >= centre(size)).astype(jnp.int32)
     return jnp.where(slot == 0, centre(size), jnp.where(slot == size - 1, 0, after))
 
 
-def exchange(value, size):
-    order = [device_of(slot, size) for slot in range(size)]
+def exchange(value, order):
     return lax.all_to_all(value, "tm", 0, 0, axis_index_groups=[order], tiled=True)
 
 
@@ -85,7 +84,7 @@
     row = lax.broadcasted_iota(jnp.int32, (height, pick_ref.shape[1]), 0)
     column = lax.broadcasted_iota(jnp.int32, (height, pick_ref.shape[1]), 1)
     for which, source in enumerate((first, size * own_blocks - 1 - first)):
-        start = slot_of(source // own_blocks, size) * packed_rows + source % own_blocks
+        start = history_slot(source // own_blocks, size) * packed_rows + source % own_blocks
         picked = column == start + row // months * own_blocks
         pick_ref[pl.ds(which * height, height)] = picked.astype(jnp.bfloat16)
     load_rows.wait()
@@ -128,7 +127,7 @@
         parts = [
             jnp.dot(
                 wide[which * height : (which + 1) * height],
-                sorted_ref[device_of(slot, size), which],
+                sorted_ref[sums_device(slot, size), which],
                 preferred_element_type=jnp.float32,
             )
             for which in range(sources)
@@ -199,7 +198,8 @@
         compiler_params=pltpu.CompilerParams(vmem_limit_bytes=24 * 1024 * 1024),
         cost_estimate=pl.CostEstimate(flops=0, bytes_accessed=tiles.size * 4, transcendentals=0),
     )(*(pltpu.with_memory_space_constraint(value, pltpu.HBM) for value in (rows, blocks, tiles)))
-    received = exchange(copies, size)
+    near = [centre(size), 1, 0]
+    received = exchange(copies, near + [device for device in range(size - 1, 1, -1) if device not in near])
 
     coded = pl.pallas_call(
         lambda *refs: tile_sums(months, *refs),
@@ -220,7 +220,7 @@
         in_specs=[vmem],
         out_specs=vmem,
         compiler_params=pltpu.CompilerParams(vmem_limit_bytes=16 * 1024 * 1024),
-    )(exchange(coded, size))
+    )(exchange(coded, [sums_device(slot, size) for slot in range(size)]))
     return owned.reshape(own_blocks, tracer_count, months, cell_count)
 
 

time: 23.8 us -> 23.7 us (level)
  no operation moved by 1% of the time
where the time goes in v15:
time: 23.7 us; the launch traced here: 23.5 us
  blocking collectives  20.8 us (88%)
  Pallas kernels  2.69 us (11%)
    all_to_all x2, blocking collectives, exchange(): lax.all_to_all(value, 'tm', 0, 0, axis_index_groups=[order], tiled=True)  20.8 us
    pallas_call x1, Pallas kernels, shards(): pl.pallas_call(lambda *refs: prepare(months, *refs), out_shape=[jax.Shape...  1.34 us
    pallas_call x1, Pallas kernels, shards(): pl.pallas_call(add_parts, out_shape=jax.ShapeDtypeStruct((own_blocks, hei...  0.69 us
    pallas_call x1, Pallas kernels, shards(): pl.pallas_call(lambda *refs: tile_sums(months, *refs), out_shape=jax.Shap...  0.66 us

profile of v15, /device:TPU:0, one launch (start us, length us, event | category | flops | bytes accessed | tf_op | source)
XLA Modules:
  0.0 23.5 jit_solution(4411419300166880412)
XLA Ops:
  0.0 1.3 %shard_map.37 = (bf16[8,32,128]{2,1,0:T(8,128)(2,1)S(1)}, bf16[8,2,192,256]{3,2,1,0:T(8,128)(2,1)S(1)}, bf16[96,256]{1,0:T(8,128)(2,1)S(1)}) custom-call(bf16[24,48]{1,0:T(8,128)(2,1)} %bitcast.7, s32[2,17]{1,0:T(2,128)} %bitcast.8, bf16[17,192,128]{2,1,0:T(8,128)(2,1)} %bitcast.6), custom_call_target="tpu_custom_call" | custom-call | bytes 1671168 | tf_op jit(solution)/shard_map/pallas_call | solution.py:183
  1.3 11.0 %all_to_all.10.refs_0_ = bf16[8,32,128]{2,1,0:T(8,128)(2,1)S(1)} all-to-all(bf16[8,32,128]{2,1,0:T(8,128)(2,1)S(1)} %get-tuple-element.8), channel_id=1, replica_groups={{10,2,0,14,12,8,6,4},{11,3,1,15,13,9,7,5},{26,18,16,30,28,24,22,20},{27..., dimensions={0} | all-to-all | bytes 131072 | tf_op jit(solution)/shard_map/all_to_all | solution.py:32
  12.3 0.7 %shard_map.38 = s16[8,104,128]{2,1,0:T(8,128)(2,1)S(1)} custom-call(bf16[8,32,128]{2,1,0:T(8,128)(2,1)S(1)} %all_to_all.10.refs_0_, bf16[96,256]{1,0:T(8,128)(2,1)S(1)} %get-tuple-element.9.refs_1_, bf16[8,2,192,256]{3,2,1,0:T(8,128)(2,1)S(1)} %get-tuple-element.10.refs_2_), custom_call_target="tpu_custom_call" | custom-call | flops 40108032 | bytes 1671168 | tf_op jit(solution)/shard_map/pallas_call | solution.py:204
  13.0 9.8 %all_to_all.11.coded_ref = s16[8,104,128]{2,1,0:T(8,128)(2,1)S(1)} all-to-all(s16[8,104,128]{2,1,0:T(8,128)(2,1)S(1)} %shard_map.38), channel_id=1, replica_groups={{10,2,4,6,8,12,14,0},{11,3,5,7,9,13,15,1},{26,18,20,22,24,28,30,16},{27..., dimensions={0} | all-to-all | bytes 425984 | tf_op jit(solution)/shard_map/all_to_all | solution.py:32
  22.8 0.7 %shard_map.39 = f32[2,48,128]{2,1,0:T(8,128)} custom-call(s16[8,104,128]{2,1,0:T(8,128)(2,1)S(1)} %all_to_all.11.coded_ref), custom_call_target="tpu_custom_call" | custom-call | tf_op jit(solution)/shard_map/pallas_call | solution.py:217

commit v16 on v15

--- a/solution.py
+++ b/solution.py
@@ -9,7 +9,7 @@
 LEVELS = 128
 SMALLEST = 2.0**-126
 SCALE_ROWS = 8
-PARTS = 6
+PARTS = 4
 
 
 def centre(size):
@@ -17,15 +17,15 @@
 
 
 def history_slot(device, size):
-    rest = size + 2 - device - (device < centre(size)).astype(jnp.int32)
-    return jnp.where(device == centre(size), 0, jnp.where(device < 2, 2 - device, rest))
+    after = device - (device > centre(size)).astype(jnp.int32)
+    return jnp.where(device == centre(size), 0, jnp.where(device == 0, size - 1, after))
 
 
 def sums_device(slot, size):
     if isinstance(slot, int):
-        return centre(size) if slot == 0 else 0 if slot == size - 1 else slot + (slot >= centre(size))
-    after = slot + (slot >= centre(size)).astype(jnp.int32)
-    return jnp.where(slot == 0, centre(size), jnp.where(slot == size - 1, 0, after))
+        return centre(size) if slot == 0 else size - slot - (size - slot <= centre(size))
+    after = size - slot - (size - slot <= centre(size)).astype(jnp.int32)
+    return jnp.where(slot == 0, centre(size), after)
 
 
 def exchange(value, order):
@@ -60,7 +60,8 @@
     height = pick_ref.shape[0] // 2
     load_blocks = pltpu.make_async_copy(blocks_in, blocks_ref, semaphores.at[0])
     load_rows = pltpu.make_async_copy(rows_in, rows_ref, semaphores.at[1])
-    parts = [range(slot_count * part // PARTS, slot_count * (part + 1) // PARTS) for part in range(PARTS)]
+    ends = [slot_count * (part * (part + 1)) // (PARTS * (PARTS + 1)) for part in range(PARTS + 1)]
+    parts = [range(start, end) for start, end in zip(ends, ends[1:])]
     load_parts = [
         pltpu.make_async_copy(
             tiles_in.at[pl.ds(part.start, len(part))],
@@ -198,8 +199,8 @@
         compiler_params=pltpu.CompilerParams(vmem_limit_bytes=24 * 1024 * 1024),
         cost_estimate=pl.CostEstimate(flops=0, bytes_accessed=tiles.size * 4, transcendentals=0),
     )(*(pltpu.with_memory_space_constraint(value, pltpu.HBM) for value in (rows, blocks, tiles)))
-    near = [centre(size), 1, 0]
-    received = exchange(copies, near + [device for device in range(size - 1, 1, -1) if device not in near])
+    inner = [device for device in range(1, size) if device != centre(size)]
+    received = exchange(copies, [centre(size)] + inner + [0])
 
     coded = pl.pallas_call(
         lambda *refs: tile_sums(months, *refs),

time: 23.7 us -> 23.5 us (level)
  no operation moved by 1% of the time
where the time goes in v16:
time: 23.5 us; the launch traced here: 23.3 us
  blocking collectives  20.6 us (88%)
  Pallas kernels  2.72 us (12%)
    all_to_all x2, blocking collectives, exchange(): lax.all_to_all(value, 'tm', 0, 0, axis_index_groups=[order], tiled=True)  20.6 us
    pallas_call x1, Pallas kernels, shards(): pl.pallas_call(lambda *refs: prepare(months, *refs), out_shape=[jax.Shape...  1.37 us
    pallas_call x1, Pallas kernels, shards(): pl.pallas_call(add_parts, out_shape=jax.ShapeDtypeStruct((own_blocks, hei...  0.69 us
    pallas_call x1, Pallas kernels, shards(): pl.pallas_call(lambda *refs: tile_sums(months, *refs), out_shape=jax.Shap...  0.66 us

profile of v16, /device:TPU:0, one launch (start us, length us, event | category | flops | bytes accessed | tf_op | source)
XLA Modules:
  0.0 23.3 jit_solution(10849202654825373531)
XLA Ops:
  0.0 1.4 %shard_map.37 = (bf16[8,32,128]{2,1,0:T(8,128)(2,1)S(1)}, bf16[8,2,192,256]{3,2,1,0:T(8,128)(2,1)S(1)}, bf16[96,256]{1,0:T(8,128)(2,1)S(1)}) custom-call(bf16[24,48]{1,0:T(8,128)(2,1)} %bitcast.7, s32[2,17]{1,0:T(2,128)} %bitcast.8, bf16[17,192,128]{2,1,0:T(8,128)(2,1)} %bitcast.6), custom_call_target="tpu_custom_call" | custom-call | bytes 1671168 | tf_op jit(solution)/shard_map/pallas_call | solution.py:184
  1.4 11.3 %all_to_all.10.refs_0_ = bf16[8,32,128]{2,1,0:T(8,128)(2,1)S(1)} all-to-all(bf16[8,32,128]{2,1,0:T(8,128)(2,1)S(1)} %get-tuple-element.8), channel_id=1, replica_groups={{10,2,4,6,8,12,14,0},{11,3,5,7,9,13,15,1},{26,18,20,22,24,28,30,16},{27..., dimensions={0} | all-to-all | bytes 131072 | tf_op jit(solution)/shard_map/all_to_all | solution.py:32
  12.6 0.7 %shard_map.38 = s16[8,104,128]{2,1,0:T(8,128)(2,1)S(1)} custom-call(bf16[8,32,128]{2,1,0:T(8,128)(2,1)S(1)} %all_to_all.10.refs_0_, bf16[96,256]{1,0:T(8,128)(2,1)S(1)} %get-tuple-element.9.refs_1_, bf16[8,2,192,256]{3,2,1,0:T(8,128)(2,1)S(1)} %get-tuple-element.10.refs_2_), custom_call_target="tpu_custom_call" | custom-call | flops 40108032 | bytes 1671168 | tf_op jit(solution)/shard_map/pallas_call | solution.py:205
  13.3 9.3 %all_to_all.11.coded_ref = s16[8,104,128]{2,1,0:T(8,128)(2,1)S(1)} all-to-all(s16[8,104,128]{2,1,0:T(8,128)(2,1)S(1)} %shard_map.38), channel_id=1, replica_groups={{10,14,12,8,6,4,2,0},{11,15,13,9,7,5,3,1},{26,30,28,24,22,20,18,16},{27..., dimensions={0} | all-to-all | bytes 425984 | tf_op jit(solution)/shard_map/all_to_all | solution.py:32
  22.6 0.7 %shard_map.39 = f32[2,48,128]{2,1,0:T(8,128)} custom-call(s16[8,104,128]{2,1,0:T(8,128)(2,1)S(1)} %all_to_all.11.coded_ref), custom_call_target="tpu_custom_call" | custom-call | tf_op jit(solution)/shard_map/pallas_call | solution.py:218

commit v17 on v16

--- a/solution.py
+++ b/solution.py
@@ -56,7 +56,7 @@
     size, packed_rows, packed_width = copies_ref.shape
     slot_count, tile_height, cell_count = tiles_ref.shape
     used_rows, source_width = rows_ref.shape
-    own_blocks = sorted_ref.shape[3] // cell_count
+    own_blocks = sorted_ref.shape[2]
     height = pick_ref.shape[0] // 2
     load_blocks = pltpu.make_async_copy(blocks_in, blocks_ref, semaphores.at[0])
     load_rows = pltpu.make_async_copy(rows_in, rows_ref, semaphores.at[1])
@@ -96,8 +96,7 @@
     def place(slot):
         which = (blocks_ref[0, slot] != first).astype(jnp.int32)
         arrival = blocks_ref[1, slot]
-        start = pl.multiple_of(arrival % own_blocks * cell_count, cell_count)
-        sorted_ref[arrival // own_blocks, which, :, pl.ds(start, cell_count)] = tiles_ref[slot]
+        sorted_ref[arrival // own_blocks, which, arrival % own_blocks] = tiles_ref[slot]
 
     each(size, copy)
     for load, part in zip(load_parts, parts):
@@ -107,9 +106,7 @@
 
 def tile_sums(months, histories_ref, pick_ref, sorted_ref, coded_ref):
     size, packed_rows, packed_width = histories_ref.shape
-    sources, tile_height, row_length = sorted_ref.shape[1:]
-    cell_count = coded_ref.shape[2]
-    own_blocks = row_length // cell_count
+    sources, own_blocks, tile_height, cell_count = sorted_ref.shape[1:]
     height = pick_ref.shape[0] // sources
 
     column_of = lax.broadcasted_iota(jnp.int32, (packed_width, tile_height), 1) // months
@@ -125,10 +122,11 @@
     coded_rows = own_blocks * height
 
     def code(slot):
+        owner = sums_device(slot, size)
         parts = [
             jnp.dot(
                 wide[which * height : (which + 1) * height],
-                sorted_ref[sums_device(slot, size), which],
+                jnp.concatenate([sorted_ref[owner, which, block] for block in range(own_blocks)], axis=1),
                 preferred_element_type=jnp.float32,
             )
             for which in range(sources)
@@ -185,7 +183,7 @@
         lambda *refs: prepare(months, *refs),
         out_shape=[
             jax.ShapeDtypeStruct((size, packed_rows, packed_width), rows.dtype),
-            jax.ShapeDtypeStruct((size, 2, tile_height, own_blocks * cell_count), tiles.dtype),
+            jax.ShapeDtypeStruct((size, 2, own_blocks, tile_height, cell_count), tiles.dtype),
             jax.ShapeDtypeStruct((2 * height, size * packed_rows), jnp.bfloat16),
         ],
         in_specs=[hbm, hbm, hbm],

time: 23.5 us -> 23.5 us (level)
  no operation moved by 1% of the time
where the time goes in v17:
time: 23.5 us; the launch traced here: 23.3 us
  blocking collectives  20.6 us (88%)
  Pallas kernels  2.7 us (11%)
    all_to_all x2, blocking collectives, exchange(): lax.all_to_all(value, 'tm', 0, 0, axis_index_groups=[order], tiled=True)  20.6 us
    pallas_call x1, Pallas kernels, shards(): pl.pallas_call(lambda *refs: prepare(months, *refs), out_shape=[jax.Shape...  1.35 us
    pallas_call x1, Pallas kernels, shards(): pl.pallas_call(add_parts, out_shape=jax.ShapeDtypeStruct((own_blocks, hei...  0.69 us
    pallas_call x1, Pallas kernels, shards(): pl.pallas_call(lambda *refs: tile_sums(months, *refs), out_shape=jax.Shap...  0.66 us

profile of v17, /device:TPU:0, one launch (start us, length us, event | category | flops | bytes accessed | tf_op | source)
XLA Modules:
  0.0 23.3 jit_solution(1476315021299227823)
XLA Ops:
  0.0 1.3 %shard_map.37 = (bf16[8,32,128]{2,1,0:T(8,128)(2,1)S(1)}, bf16[8,2,2,192,128]{4,3,2,1,0:T(8,128)(2,1)S(1)}, bf16[96,256]{1,0:T(8,128)(2,1)S(1)}) custom-call(bf16[24,48]{1,0:T(8,128)(2,1)} %bitcast.7, s32[2,17]{1,0:T(2,128)} %bitcast.8, bf16[17,192,128]{2,1,0:T(8,128)(2,1)} %bitcast.6), custom_call_target="tpu_custom_call" | custom-call | bytes 1671168 | tf_op jit(solution)/shard_map/pallas_call | solution.py:182
  1.4 11.3 %all_to_all.10.refs_0_ = bf16[8,32,128]{2,1,0:T(8,128)(2,1)S(1)} all-to-all(bf16[8,32,128]{2,1,0:T(8,128)(2,1)S(1)} %get-tuple-element.8), channel_id=1, replica_groups={{10,2,4,6,8,12,14,0},{11,3,5,7,9,13,15,1},{26,18,20,22,24,28,30,16},{27..., dimensions={0} | all-to-all | bytes 131072 | tf_op jit(solution)/shard_map/all_to_all | solution.py:32
  12.6 0.7 %shard_map.38 = s16[8,104,128]{2,1,0:T(8,128)(2,1)S(1)} custom-call(bf16[8,32,128]{2,1,0:T(8,128)(2,1)S(1)} %all_to_all.10.refs_0_, bf16[96,256]{1,0:T(8,128)(2,1)S(1)} %get-tuple-element.9.refs_1_, bf16[8,2,2,192,128]{4,3,2,1,0:T(8,128)(2,1)S(1)} %get-tuple-element.10.refs_2_), custom_call_target="tpu_custom_call" | custom-call | flops 40108032 | bytes 1671168 | tf_op jit(solution)/shard_map/pallas_call | solution.py:203
  13.3 9.3 %all_to_all.11.coded_ref = s16[8,104,128]{2,1,0:T(8,128)(2,1)S(1)} all-to-all(s16[8,104,128]{2,1,0:T(8,128)(2,1)S(1)} %shard_map.38), channel_id=1, replica_groups={{10,14,12,8,6,4,2,0},{11,15,13,9,7,5,3,1},{26,30,28,24,22,20,18,16},{27..., dimensions={0} | all-to-all | bytes 425984 | tf_op jit(solution)/shard_map/all_to_all | solution.py:32
  22.6 0.7 %shard_map.39 = f32[2,48,128]{2,1,0:T(8,128)} custom-call(s16[8,104,128]{2,1,0:T(8,128)(2,1)S(1)} %all_to_all.11.coded_ref), custom_call_target="tpu_custom_call" | custom-call | tf_op jit(solution)/shard_map/pallas_call | solution.py:216

commit v18 on v16

--- a/solution.py
+++ b/solution.py
@@ -60,7 +60,7 @@
     height = pick_ref.shape[0] // 2
     load_blocks = pltpu.make_async_copy(blocks_in, blocks_ref, semaphores.at[0])
     load_rows = pltpu.make_async_copy(rows_in, rows_ref, semaphores.at[1])
-    ends = [slot_count * (part * (part + 1)) // (PARTS * (PARTS + 1)) for part in range(PARTS + 1)]
+    ends = [slot_count * part // PARTS for part in range(PARTS + 1)]
     parts = [range(start, end) for start, end in zip(ends, ends[1:])]
     load_parts = [
         pltpu.make_async_copy(
@@ -72,8 +72,8 @@
     ]
     load_blocks.start()
     load_rows.start()
-    for load in load_parts:
-        load.start()
+    for index, load in enumerate(load_parts):
+        load.start(priority=index % 2)
 
     def clear(owner):
         sorted_ref[owner] = jnp.zeros(sorted_ref.shape[1:], sorted_ref.dtype)

time: 23.5 us -> 23.5 us (level)
  no operation moved by 1% of the time
where the time goes in v18:
time: 23.5 us; the launch traced here: 23.3 us
  blocking collectives  20.6 us (88%)
  Pallas kernels  2.7 us (11%)
    all_to_all x2, blocking collectives, exchange(): lax.all_to_all(value, 'tm', 0, 0, axis_index_groups=[order], tiled=True)  20.6 us
    pallas_call x1, Pallas kernels, shards(): pl.pallas_call(lambda *refs: prepare(months, *refs), out_shape=[jax.Shape...  1.35 us
    pallas_call x1, Pallas kernels, shards(): pl.pallas_call(add_parts, out_shape=jax.ShapeDtypeStruct((own_blocks, hei...  0.69 us
    pallas_call x1, Pallas kernels, shards(): pl.pallas_call(lambda *refs: tile_sums(months, *refs), out_shape=jax.Shap...  0.66 us

profile of v18, /device:TPU:0, one launch (start us, length us, event | category | flops | bytes accessed | tf_op | source)
XLA Modules:
  0.0 23.3 jit_solution(9345490793130341430)
XLA Ops:
  0.0 1.4 %shard_map.37 = (bf16[8,32,128]{2,1,0:T(8,128)(2,1)S(1)}, bf16[8,2,192,256]{3,2,1,0:T(8,128)(2,1)S(1)}, bf16[96,256]{1,0:T(8,128)(2,1)S(1)}) custom-call(bf16[24,48]{1,0:T(8,128)(2,1)} %bitcast.7, s32[2,17]{1,0:T(2,128)} %bitcast.8, bf16[17,192,128]{2,1,0:T(8,128)(2,1)} %bitcast.6), custom_call_target="tpu_custom_call" | custom-call | bytes 1671168 | tf_op jit(solution)/shard_map/pallas_call | solution.py:184
  1.4 11.3 %all_to_all.10.refs_0_ = bf16[8,32,128]{2,1,0:T(8,128)(2,1)S(1)} all-to-all(bf16[8,32,128]{2,1,0:T(8,128)(2,1)S(1)} %get-tuple-element.8), channel_id=1, replica_groups={{10,2,4,6,8,12,14,0},{11,3,5,7,9,13,15,1},{26,18,20,22,24,28,30,16},{27..., dimensions={0} | all-to-all | bytes 131072 | tf_op jit(solution)/shard_map/all_to_all | solution.py:32
  12.6 0.7 %shard_map.38 = s16[8,104,128]{2,1,0:T(8,128)(2,1)S(1)} custom-call(bf16[8,32,128]{2,1,0:T(8,128)(2,1)S(1)} %all_to_all.10.refs_0_, bf16[96,256]{1,0:T(8,128)(2,1)S(1)} %get-tuple-element.9.refs_1_, bf16[8,2,192,256]{3,2,1,0:T(8,128)(2,1)S(1)} %get-tuple-element.10.refs_2_), custom_call_target="tpu_custom_call" | custom-call | flops 40108032 | bytes 1671168 | tf_op jit(solution)/shard_map/pallas_call | solution.py:205
  13.3 9.3 %all_to_all.11.coded_ref = s16[8,104,128]{2,1,0:T(8,128)(2,1)S(1)} all-to-all(s16[8,104,128]{2,1,0:T(8,128)(2,1)S(1)} %shard_map.38), channel_id=1, replica_groups={{10,14,12,8,6,4,2,0},{11,15,13,9,7,5,3,1},{26,30,28,24,22,20,18,16},{27..., dimensions={0} | all-to-all | bytes 425984 | tf_op jit(solution)/shard_map/all_to_all | solution.py:32
  22.6 0.7 %shard_map.39 = f32[2,48,128]{2,1,0:T(8,128)} custom-call(s16[8,104,128]{2,1,0:T(8,128)(2,1)S(1)} %all_to_all.11.coded_ref), custom_call_target="tpu_custom_call" | custom-call | tf_op jit(solution)/shard_map/pallas_call | solution.py:218

commit v19 on v18

--- a/solution.py
+++ b/solution.py
@@ -10,6 +10,7 @@
 SMALLEST = 2.0**-126
 SCALE_ROWS = 8
 PARTS = 4
+WRITTEN_OUT = 17
 
 
 def centre(size):
@@ -33,7 +34,7 @@
 
 
 def each(count, body):
-    if count <= 17:
+    if count <= WRITTEN_OUT:
         for index in range(count):
             body(index)
     else:
@@ -81,7 +82,8 @@
 
     each(size, clear)
     load_blocks.wait()
-    first = blocks_ref[0, 0]
+    blocks = blocks_ref[...] if slot_count <= WRITTEN_OUT else blocks_ref
+    first = blocks[0, 0]
     row = lax.broadcasted_iota(jnp.int32, (height, pick_ref.shape[1]), 0)
     column = lax.broadcasted_iota(jnp.int32, (height, pick_ref.shape[1]), 1)
     for which, source in enumerate((first, size * own_blocks - 1 - first)):
@@ -94,8 +96,8 @@
         copies_ref[owner, :used_rows, :source_width] = rows_ref[...]
 
     def place(slot):
-        which = (blocks_ref[0, slot] != first).astype(jnp.int32)
-        arrival = blocks_ref[1, slot]
+        which = (blocks[0, slot] != first).astype(jnp.int32)
+        arrival = blocks[1, slot]
         start = pl.multiple_of(arrival % own_blocks * cell_count, cell_count)
         sorted_ref[arrival // own_blocks, which, :, pl.ds(start, cell_count)] = tiles_ref[slot]
 
@@ -192,7 +194,7 @@
         out_specs=[vmem, vmem, vmem],
         scratch_shapes=[
             pltpu.VMEM(rows.shape, rows.dtype),
-            pltpu.SMEM(blocks.shape, blocks.dtype),
+            (pltpu.VMEM if slot_count <= WRITTEN_OUT else pltpu.SMEM)(blocks.shape, blocks.dtype),
             pltpu.VMEM(tiles.shape, tiles.dtype),
             pltpu.SemaphoreType.DMA((2 + PARTS,)),
         ],

time: 23.5 us -> 23.8 us (1.013)
  Pallas kernels: 2.7 us -> 3 us
    pallas_call x1, Pallas kernels: 1.35 us -> 1.64 us  [shards(): pl.pallas_call(lambda *refs: prepare(months, *refs), out_shape=[jax.Shape...]
where the time goes in v19:
time: 23.8 us; the launch traced here: 23.6 us
  blocking collectives  20.6 us (87%)
  Pallas kernels  3 us (13%)
    all_to_all x2, blocking collectives, exchange(): lax.all_to_all(value, 'tm', 0, 0, axis_index_groups=[order], tiled=True)  20.6 us
    pallas_call x1, Pallas kernels, shards(): pl.pallas_call(lambda *refs: prepare(months, *refs), out_shape=[jax.Shape...  1.64 us
    pallas_call x1, Pallas kernels, shards(): pl.pallas_call(add_parts, out_shape=jax.ShapeDtypeStruct((own_blocks, hei...  0.69 us
    pallas_call x1, Pallas kernels, shards(): pl.pallas_call(lambda *refs: tile_sums(months, *refs), out_shape=jax.Shap...  0.66 us

profile of v19, /device:TPU:0, one launch (start us, length us, event | category | flops | bytes accessed | tf_op | source)
XLA Modules:
  0.0 23.6 jit_solution(9562942344039077737)
XLA Ops:
  0.0 1.6 %shard_map.37 = (bf16[8,32,128]{2,1,0:T(8,128)(2,1)S(1)}, bf16[8,2,192,256]{3,2,1,0:T(8,128)(2,1)S(1)}, bf16[96,256]{1,0:T(8,128)(2,1)S(1)}) custom-call(bf16[24,48]{1,0:T(8,128)(2,1)} %bitcast.7, s32[2,17]{1,0:T(2,128)} %bitcast.8, bf16[17,192,128]{2,1,0:T(8,128)(2,1)} %bitcast.6), custom_call_target="tpu_custom_call" | custom-call | bytes 1671168 | tf_op jit(solution)/shard_map/pallas_call | solution.py:186
  1.7 11.3 %all_to_all.10.refs_0_ = bf16[8,32,128]{2,1,0:T(8,128)(2,1)S(1)} all-to-all(bf16[8,32,128]{2,1,0:T(8,128)(2,1)S(1)} %get-tuple-element.8), channel_id=1, replica_groups={{10,2,4,6,8,12,14,0},{11,3,5,7,9,13,15,1},{26,18,20,22,24,28,30,16},{27..., dimensions={0} | all-to-all | bytes 131072 | tf_op jit(solution)/shard_map/all_to_all | solution.py:33
  12.9 0.7 %shard_map.38 = s16[8,104,128]{2,1,0:T(8,128)(2,1)S(1)} custom-call(bf16[8,32,128]{2,1,0:T(8,128)(2,1)S(1)} %all_to_all.10.refs_0_, bf16[96,256]{1,0:T(8,128)(2,1)S(1)} %get-tuple-element.9.refs_1_, bf16[8,2,192,256]{3,2,1,0:T(8,128)(2,1)S(1)} %get-tuple-element.10.refs_2_), custom_call_target="tpu_custom_call" | custom-call | flops 40108032 | bytes 1671168 | tf_op jit(solution)/shard_map/pallas_call | solution.py:207
  13.6 9.3 %all_to_all.11.coded_ref = s16[8,104,128]{2,1,0:T(8,128)(2,1)S(1)} all-to-all(s16[8,104,128]{2,1,0:T(8,128)(2,1)S(1)} %shard_map.38), channel_id=1, replica_groups={{10,14,12,8,6,4,2,0},{11,15,13,9,7,5,3,1},{26,30,28,24,22,20,18,16},{27..., dimensions={0} | all-to-all | bytes 425984 | tf_op jit(solution)/shard_map/all_to_all | solution.py:33
  22.9 0.7 %shard_map.39 = f32[2,48,128]{2,1,0:T(8,128)} custom-call(s16[8,104,128]{2,1,0:T(8,128)(2,1)S(1)} %all_to_all.11.coded_ref), custom_call_target="tpu_custom_call" | custom-call | tf_op jit(solution)/shard_map/pallas_call | solution.py:220

commit v20 on v17

--- a/solution.py
+++ b/solution.py
@@ -10,6 +10,8 @@
 SMALLEST = 2.0**-126
 SCALE_ROWS = 8
 PARTS = 4
+WRITTEN_OUT = 17
+SOURCES = 2
 
 
 def centre(size):
@@ -32,8 +34,14 @@
     return lax.all_to_all(value, "tm", 0, 0, axis_index_groups=[order], tiled=True)
 
 
+def split(value, divisor):
+    if divisor & (divisor - 1):
+        return lax.div(value, jnp.full_like(value, divisor)), lax.rem(value, jnp.full_like(value, divisor))
+    return value >> (divisor.bit_length() - 1), value & (divisor - 1)
+
+
 def each(count, body):
-    if count <= 17:
+    if count <= WRITTEN_OUT:
         for index in range(count):
             body(index)
     else:
@@ -48,6 +56,8 @@
     copies_ref,
     sorted_ref,
     pick_ref,
+    columns_ref,
+    same_ref,
     rows_ref,
     blocks_ref,
     tiles_ref,
@@ -56,12 +66,13 @@
     size, packed_rows, packed_width = copies_ref.shape
     slot_count, tile_height, cell_count = tiles_ref.shape
     used_rows, source_width = rows_ref.shape
-    own_blocks = sorted_ref.shape[2]
-    height = pick_ref.shape[0] // 2
+    block_count = sorted_ref.shape[0] // SOURCES
+    own_blocks = block_count // size
+    height = pick_ref.shape[0] // SOURCES
+    ends = [slot_count * part // PARTS for part in range(PARTS + 1)]
+    parts = [range(start, end) for start, end in zip(ends, ends[1:])]
     load_blocks = pltpu.make_async_copy(blocks_in, blocks_ref, semaphores.at[0])
     load_rows = pltpu.make_async_copy(rows_in, rows_ref, semaphores.at[1])
-    ends = [slot_count * (part * (part + 1)) // (PARTS * (PARTS + 1)) for part in range(PARTS + 1)]
-    parts = [range(start, end) for start, end in zip(ends, ends[1:])]
     load_parts = [
         pltpu.make_async_copy(
             tiles_in.at[pl.ds(part.start, len(part))],
@@ -76,62 +87,72 @@
         load.start()
 
     def clear(owner):
-        sorted_ref[owner] = jnp.zeros(sorted_ref.shape[1:], sorted_ref.dtype)
+        rows = pl.ds(owner * SOURCES * own_blocks, SOURCES * own_blocks)
+        sorted_ref[rows] = jnp.zeros((SOURCES * own_blocks, tile_height, cell_count), sorted_ref.dtype)
         copies_ref[owner] = jnp.zeros(copies_ref.shape[1:], copies_ref.dtype)
 
     each(size, clear)
+    packed_column = lax.broadcasted_iota(jnp.int32, columns_ref.shape, 0)
+    column_of = split(lax.broadcasted_iota(jnp.int32, columns_ref.shape, 1), months)[0]
+    columns_ref[...] = (column_of == packed_column).astype(columns_ref.dtype)
+    month_of_row = split(lax.broadcasted_iota(jnp.int32, same_ref.shape, 0), months)[1]
+    month_of_column = split(lax.broadcasted_iota(jnp.int32, same_ref.shape, 1), months)[1]
+    same_ref[...] = (month_of_row == month_of_column).astype(same_ref.dtype)
+    tracer = split(lax.broadcasted_iota(jnp.int32, (height, pick_ref.shape[1]), 0), months)[0]
+    offset = lax.broadcasted_iota(jnp.int32, (height, pick_ref.shape[1]), 1) - tracer * own_blocks
+
     load_blocks.wait()
     first = blocks_ref[0, 0]
-    row = lax.broadcasted_iota(jnp.int32, (height, pick_ref.shape[1]), 0)
-    column = lax.broadcasted_iota(jnp.int32, (height, pick_ref.shape[1]), 1)
-    for which, source in enumerate((first, size * own_blocks - 1 - first)):
-        start = history_slot(source // own_blocks, size) * packed_rows + source % own_blocks
-        picked = column == start + row // months * own_blocks
-        pick_ref[pl.ds(which * height, height)] = picked.astype(jnp.bfloat16)
+
+    def place_of(slot):
+        which = (blocks_ref[0, slot] != first).astype(jnp.int32)
+        return which * block_count + blocks_ref[1, slot]
+
+    places = [place_of(slot) for slot in range(slot_count)] if slot_count <= WRITTEN_OUT else None
+    for which, source in enumerate((first, block_count - 1 - first)):
+        owner, block = split(source, own_blocks)
+        picked = offset == history_slot(owner, size) * packed_rows + block
+        pick_ref[pl.ds(which * height, height)] = picked.astype(pick_ref.dtype)
     load_rows.wait()
 
     def copy(owner):
         copies_ref[owner, :used_rows, :source_width] = rows_ref[...]
-
-    def place(slot):
-        which = (blocks_ref[0, slot] != first).astype(jnp.int32)
-        arrival = blocks_ref[1, slot]
-        sorted_ref[arrival // own_blocks, which, arrival % own_blocks] = tiles_ref[slot]
 
     each(size, copy)
     for load, part in zip(load_parts, parts):
         load.wait()
-        each(len(part), lambda slot: place(part.start + slot))
-
-
-def tile_sums(months, histories_ref, pick_ref, sorted_ref, coded_ref):
+        if places:
+            for slot in part:
+                sorted_ref[places[slot]] = tiles_ref[slot]
+    if not places:
+
+        def place(slot):
+            sorted_ref[place_of(slot)] = tiles_ref[slot]
+
+        each(slot_count, place)
+
+
+def tile_sums(histories_ref, pick_ref, columns_ref, same_ref, sorted_ref, coded_ref):
     size, packed_rows, packed_width = histories_ref.shape
-    sources, own_blocks, tile_height, cell_count = sorted_ref.shape[1:]
-    height = pick_ref.shape[0] // sources
-
-    column_of = lax.broadcasted_iota(jnp.int32, (packed_width, tile_height), 1) // months
-    packed_column = lax.broadcasted_iota(jnp.int32, (packed_width, tile_height), 0)
-    repeat_columns = (column_of == packed_column).astype(jnp.bfloat16)
-    month_of_row = lax.broadcasted_iota(jnp.int32, (sources * height, tile_height), 0) % months
-    month_of_column = lax.broadcasted_iota(jnp.int32, (sources * height, tile_height), 1) % months
+    block_count = sorted_ref.shape[0] // SOURCES
+    own_blocks = block_count // size
+    height = pick_ref.shape[0] // SOURCES
+    cell_count = coded_ref.shape[2]
+    coded_rows = own_blocks * height
+
     histories = histories_ref[...].reshape(size * packed_rows, packed_width)
     tall = jnp.dot(pick_ref[...], histories, preferred_element_type=jnp.float32)
-    wide = jnp.dot(tall.astype(jnp.bfloat16), repeat_columns, preferred_element_type=jnp.float32)
-    wide = jnp.where(month_of_row == month_of_column, wide, 0.0).astype(jnp.bfloat16)
-
-    coded_rows = own_blocks * height
+    wide = jnp.dot(tall.astype(jnp.bfloat16), columns_ref[...], preferred_element_type=jnp.float32)
+    wide = (wide * same_ref[...]).astype(jnp.bfloat16)
 
     def code(slot):
-        owner = sums_device(slot, size)
-        parts = [
-            jnp.dot(
-                wide[which * height : (which + 1) * height],
-                jnp.concatenate([sorted_ref[owner, which, block] for block in range(own_blocks)], axis=1),
-                preferred_element_type=jnp.float32,
-            )
-            for which in range(sources)
-        ]
-        total = sum(parts[1:], parts[0])
+        total = None
+        for which in range(SOURCES):
+            start = which * block_count + sums_device(slot, size) * own_blocks
+            tiles = jnp.concatenate([sorted_ref[start + block] for block in range(own_blocks)], axis=1)
+            rows = wide[which * height : (which + 1) * height]
+            part = jnp.dot(rows, tiles, preferred_element_type=jnp.float32)
+            total = part if total is None else total + part
         values = [total[:, block * cell_count : (block + 1) * cell_count] for block in range(own_blocks)]
         top = jnp.abs(values[0])
         for value in values[1:]:
@@ -168,6 +189,7 @@
     size = lax.axis_size("tm")
     own_blocks, tracer_count, source_width = histories.shape
     slot_count, source_width, months, cell_count = propagator.shape
+    block_count = size * own_blocks
     height = tracer_count * months
     tile_height = source_width * months
 
@@ -179,15 +201,17 @@
     tiles = propagator.reshape(slot_count, tile_height, cell_count)
     vmem = pl.BlockSpec(memory_space=pltpu.VMEM)
     hbm = pl.BlockSpec(memory_space=pltpu.HBM)
-    copies, sorted_tiles, pick = pl.pallas_call(
+    copies, sorted_tiles, pick, columns, same = pl.pallas_call(
         lambda *refs: prepare(months, *refs),
         out_shape=[
             jax.ShapeDtypeStruct((size, packed_rows, packed_width), rows.dtype),
-            jax.ShapeDtypeStruct((size, 2, own_blocks, tile_height, cell_count), tiles.dtype),
-            jax.ShapeDtypeStruct((2 * height, size * packed_rows), jnp.bfloat16),
+            jax.ShapeDtypeStruct((SOURCES * block_count, tile_height, cell_count), tiles.dtype),
+            jax.ShapeDtypeStruct((SOURCES * height, size * packed_rows), jnp.bfloat16),
+            jax.ShapeDtypeStruct((packed_width, tile_height), jnp.bfloat16),
+            jax.ShapeDtypeStruct((SOURCES * height, tile_height), jnp.float32),
         ],
-        in_specs=[hbm, hbm, hbm],
-        out_specs=[vmem, vmem, vmem],
+        in_specs=[hbm] * 3,
+        out_specs=[vmem] * 5,
         scratch_shapes=[
             pltpu.VMEM(rows.shape, rows.dtype),
             pltpu.SMEM(blocks.shape, blocks.dtype),
@@ -197,13 +221,14 @@
         compiler_params=pltpu.CompilerParams(vmem_limit_bytes=24 * 1024 * 1024),
         cost_estimate=pl.CostEstimate(flops=0, bytes_accessed=tiles.size * 4, transcendentals=0),
     )(*(pltpu.with_memory_space_constraint(value, pltpu.HBM) for value in (rows, blocks, tiles)))
+
     inner = [device for device in range(1, size) if device != centre(size)]
     received = exchange(copies, [centre(size)] + inner + [0])
 
     coded = pl.pallas_call(
-        lambda *refs: tile_sums(months, *refs),
+        tile_sums,
         out_shape=jax.ShapeDtypeStruct((size, own_blocks * height + SCALE_ROWS, cell_count), jnp.int16),
-        in_specs=[vmem, vmem, vmem],
+        in_specs=[vmem] * 5,
         out_specs=vmem,
         compiler_params=pltpu.CompilerParams(vmem_limit_bytes=20 * 1024 * 1024),
         cost_estimate=pl.CostEstimate(
@@ -211,7 +236,7 @@
             bytes_accessed=propagator.size * 4,
             transcendentals=0,
         ),
-    )(received, pick, sorted_tiles)
+    )(received, pick, columns, same, sorted_tiles)
 
     owned = pl.pallas_call(
         add_parts,

time: 23.5 us -> 23.5 us (level)
  no operation moved by 1% of the time
where the time goes in v20:
time: 23.5 us; the launch traced here: 23.3 us
  blocking collectives  20.6 us (88%)
  Pallas kernels  2.68 us (11%)
    all_to_all x2, blocking collectives, exchange(): lax.all_to_all(value, 'tm', 0, 0, axis_index_groups=[order], tiled=True)  20.6 us
    pallas_call x1, Pallas kernels, shards(): pl.pallas_call(lambda *refs: prepare(months, *refs), out_shape=[jax.Shape...  1.32 us
    pallas_call x1, Pallas kernels, shards(): pl.pallas_call(add_parts, out_shape=jax.ShapeDtypeStruct((own_blocks, hei...  0.69 us
    pallas_call x1, Pallas kernels, shards(): pl.pallas_call(tile_sums, out_shape=jax.ShapeDtypeStruct((size, own_block...  0.66 us

profile of v20, /device:TPU:0, one launch (start us, length us, event | category | flops | bytes accessed | tf_op | source)
XLA Modules:
  0.0 23.3 jit_solution(11463266996103046078)
XLA Ops:
  0.0 1.3 %shard_map.37 = (bf16[8,32,128]{2,1,0:T(8,128)(2,1)S(1)}, bf16[32,192,128]{2,1,0:T(8,128)(2,1)S(1)}, bf16[96,256]{1,0:T(8,128)(2,1)S(1)}, bf16[128,192]{1,0:T(8,128)(2,1)S(1)}, f32[96,192]{1,0:T(8,128)S(1)}) custom-call(bf16[24,48]{1,0:T(8,128)(2,1)} %bitcast.7, s32[2,17]{1,0:T(2,128)} %bitcast.8, bf16[17,192,128]{2,1,0:T(8,128)(2,1)} %bitcast.6), custom_call_target="tpu_custom_call" | custom-call | bytes 1671168 | tf_op jit(solution)/shard_map/pallas_call | solution.py:204
  1.3 11.3 %all_to_all.10.histories_ref = bf16[8,32,128]{2,1,0:T(8,128)(2,1)S(1)} all-to-all(bf16[8,32,128]{2,1,0:T(8,128)(2,1)S(1)} %get-tuple-element.10), channel_id=1, replica_groups={{10,2,4,6,8,12,14,0},{11,3,5,7,9,13,15,1},{26,18,20,22,24,28,30,16},{27..., dimensions={0} | all-to-all | bytes 131072 | tf_op jit(solution)/shard_map/all_to_all | solution.py:34
  12.6 0.7 %shard_map.38 = s16[8,104,128]{2,1,0:T(8,128)(2,1)S(1)} custom-call(bf16[8,32,128]{2,1,0:T(8,128)(2,1)S(1)} %all_to_all.10.histories_ref, bf16[96,256]{1,0:T(8,128)(2,1)S(1)} %get-tuple-element.11.pick_ref, bf16[128,192]{1,0:T(8,128)(2,1)S(1)} %get-tuple-element.12.columns_ref, f32[96,192]{1,0:T(8,128)S(1)} %get-tuple-element.13.same_ref, ...), custom_call_target="tpu_custom_call" | custom-call | flops 40108032 | bytes 1671168 | tf_op jit(solution)/shard_map/pallas_call | solution.py:228
  13.3 9.3 %all_to_all.11.coded_ref = s16[8,104,128]{2,1,0:T(8,128)(2,1)S(1)} all-to-all(s16[8,104,128]{2,1,0:T(8,128)(2,1)S(1)} %shard_map.38), channel_id=1, replica_groups={{10,14,12,8,6,4,2,0},{11,15,13,9,7,5,3,1},{26,30,28,24,22,20,18,16},{27..., dimensions={0} | all-to-all | bytes 425984 | tf_op jit(solution)/shard_map/all_to_all | solution.py:34
  22.6 0.7 %shard_map.39 = f32[2,48,128]{2,1,0:T(8,128)} custom-call(s16[8,104,128]{2,1,0:T(8,128)(2,1)S(1)} %all_to_all.11.coded_ref), custom_call_target="tpu_custom_call" | custom-call | tf_op jit(solution)/shard_map/pallas_call | solution.py:241

commit v21 on v20

--- a/solution.py
+++ b/solution.py
@@ -9,7 +9,6 @@
 LEVELS = 128
 SMALLEST = 2.0**-126
 SCALE_ROWS = 8
-PARTS = 4
 WRITTEN_OUT = 17
 SOURCES = 2
 
@@ -24,10 +23,11 @@
 
 
 def sums_device(slot, size):
-    if isinstance(slot, int):
-        return centre(size) if slot == 0 else size - slot - (size - slot <= centre(size))
-    after = size - slot - (size - slot <= centre(size)).astype(jnp.int32)
-    return jnp.where(slot == 0, centre(size), after)
+    return size - 1 - slot
+
+
+def starts_late(size):
+    return lax.axis_index("tm") >= size * 3 // 4
 
 
 def exchange(value, order):
@@ -46,6 +46,47 @@
             body(index)
     else:
         lax.fori_loop(0, count, lambda index, carry: (body(index), carry)[1], 0)
+
+
+def tile_loads(blocks_in, tiles_in, blocks_ref, tiles_ref, semaphores):
+    return [
+        pltpu.make_async_copy(blocks_in, blocks_ref, semaphores.at[0]),
+        pltpu.make_async_copy(tiles_in, tiles_ref, semaphores.at[1]),
+    ]
+
+
+def arrange(size, months, loads, blocks_ref, tiles_ref, sorted_ref, pick_ref):
+    slot_count, tile_height, cell_count = tiles_ref.shape
+    block_count = sorted_ref.shape[0] // SOURCES
+    own_blocks = block_count // size
+    height = pick_ref.shape[0] // SOURCES
+    packed_rows = pick_ref.shape[1] // size
+
+    def clear(owner):
+        rows = pl.ds(owner * SOURCES * own_blocks, SOURCES * own_blocks)
+        sorted_ref[rows] = jnp.zeros((SOURCES * own_blocks, tile_height, cell_count), sorted_ref.dtype)
+
+    each(size, clear)
+    tracer = split(lax.broadcasted_iota(jnp.int32, (height, pick_ref.shape[1]), 0), months)[0]
+    offset = lax.broadcasted_iota(jnp.int32, (height, pick_ref.shape[1]), 1) - tracer * own_blocks
+    loads[0].wait()
+    first = blocks_ref[0, 0]
+
+    def place_of(slot):
+        which = (blocks_ref[0, slot] != first).astype(jnp.int32)
+        return which * block_count + blocks_ref[1, slot]
+
+    places = [place_of(slot) for slot in range(slot_count)] if slot_count <= WRITTEN_OUT else None
+    for which, source in enumerate((first, block_count - 1 - first)):
+        owner, block = split(source, own_blocks)
+        picked = offset == history_slot(owner, size) * packed_rows + block
+        pick_ref[pl.ds(which * height, height)] = picked.astype(pick_ref.dtype)
+    loads[1].wait()
+
+    def place(slot):
+        sorted_ref[places[slot] if places else place_of(slot)] = tiles_ref[slot]
+
+    each(slot_count, place)
 
 
 def prepare(
@@ -63,76 +104,70 @@
     tiles_ref,
     semaphores,
 ):
-    size, packed_rows, packed_width = copies_ref.shape
-    slot_count, tile_height, cell_count = tiles_ref.shape
+    size = copies_ref.shape[0]
     used_rows, source_width = rows_ref.shape
-    block_count = sorted_ref.shape[0] // SOURCES
-    own_blocks = block_count // size
-    height = pick_ref.shape[0] // SOURCES
-    ends = [slot_count * part // PARTS for part in range(PARTS + 1)]
-    parts = [range(start, end) for start, end in zip(ends, ends[1:])]
-    load_blocks = pltpu.make_async_copy(blocks_in, blocks_ref, semaphores.at[0])
-    load_rows = pltpu.make_async_copy(rows_in, rows_ref, semaphores.at[1])
-    load_parts = [
-        pltpu.make_async_copy(
-            tiles_in.at[pl.ds(part.start, len(part))],
-            tiles_ref.at[pl.ds(part.start, len(part))],
-            semaphores.at[2 + index],
-        )
-        for index, part in enumerate(parts)
-    ]
-    load_blocks.start()
+    early = jnp.logical_not(starts_late(size))
+    load_rows = pltpu.make_async_copy(rows_in, rows_ref, semaphores.at[2])
+    loads = tile_loads(blocks_in, tiles_in, blocks_ref, tiles_ref, semaphores)
     load_rows.start()
-    for load in load_parts:
-        load.start()
-
-    def clear(owner):
-        rows = pl.ds(owner * SOURCES * own_blocks, SOURCES * own_blocks)
-        sorted_ref[rows] = jnp.zeros((SOURCES * own_blocks, tile_height, cell_count), sorted_ref.dtype)
-        copies_ref[owner] = jnp.zeros(copies_ref.shape[1:], copies_ref.dtype)
-
-    each(size, clear)
+
+    @pl.when(early)
+    def _():
+        for load in loads:
+            load.start()
+
     packed_column = lax.broadcasted_iota(jnp.int32, columns_ref.shape, 0)
     column_of = split(lax.broadcasted_iota(jnp.int32, columns_ref.shape, 1), months)[0]
     columns_ref[...] = (column_of == packed_column).astype(columns_ref.dtype)
     month_of_row = split(lax.broadcasted_iota(jnp.int32, same_ref.shape, 0), months)[1]
     month_of_column = split(lax.broadcasted_iota(jnp.int32, same_ref.shape, 1), months)[1]
     same_ref[...] = (month_of_row == month_of_column).astype(same_ref.dtype)
-    tracer = split(lax.broadcasted_iota(jnp.int32, (height, pick_ref.shape[1]), 0), months)[0]
-    offset = lax.broadcasted_iota(jnp.int32, (height, pick_ref.shape[1]), 1) - tracer * own_blocks
-
-    load_blocks.wait()
-    first = blocks_ref[0, 0]
-
-    def place_of(slot):
-        which = (blocks_ref[0, slot] != first).astype(jnp.int32)
-        return which * block_count + blocks_ref[1, slot]
-
-    places = [place_of(slot) for slot in range(slot_count)] if slot_count <= WRITTEN_OUT else None
-    for which, source in enumerate((first, block_count - 1 - first)):
-        owner, block = split(source, own_blocks)
-        picked = offset == history_slot(owner, size) * packed_rows + block
-        pick_ref[pl.ds(which * height, height)] = picked.astype(pick_ref.dtype)
+    copies_ref[...] = jnp.zeros(copies_ref.shape, copies_ref.dtype)
     load_rows.wait()
 
     def copy(owner):
         copies_ref[owner, :used_rows, :source_width] = rows_ref[...]
 
     each(size, copy)
-    for load, part in zip(load_parts, parts):
-        load.wait()
-        if places:
-            for slot in part:
-                sorted_ref[places[slot]] = tiles_ref[slot]
-    if not places:
-
-        def place(slot):
-            sorted_ref[place_of(slot)] = tiles_ref[slot]
-
-        each(slot_count, place)
-
-
-def tile_sums(histories_ref, pick_ref, columns_ref, same_ref, sorted_ref, coded_ref):
+
+    @pl.when(early)
+    def _():
+        arrange(size, months, loads, blocks_ref, tiles_ref, sorted_ref, pick_ref)
+
+
+def tile_sums(
+    months,
+    histories_ref,
+    pick_ref,
+    columns_ref,
+    same_ref,
+    sorted_ref,
+    blocks_in,
+    tiles_in,
+    coded_ref,
+    late_pick_ref,
+    late_sorted_ref,
+    blocks_ref,
+    tiles_ref,
+    semaphores,
+):
+    size = histories_ref.shape[0]
+    late = starts_late(size)
+
+    @pl.when(late)
+    def _():
+        loads = tile_loads(blocks_in, tiles_in, blocks_ref, tiles_ref, semaphores)
+        for load in loads:
+            load.start()
+        arrange(size, months, loads, blocks_ref, tiles_ref, late_sorted_ref, late_pick_ref)
+        code_sums(histories_ref, late_pick_ref, columns_ref, same_ref, late_sorted_ref, coded_ref)
+
+    @pl.when(jnp.logical_not(late))
+    def _():
+        code_sums(histories_ref, pick_ref, columns_ref, same_ref, sorted_ref, coded_ref)
+
+
+def code_sums(histories_ref, pick_ref, columns_ref, same_ref, sorted_ref, coded_ref):
     size, packed_rows, packed_width = histories_ref.shape
     block_count = sorted_ref.shape[0] // SOURCES
     own_blocks = block_count // size
@@ -196,9 +231,14 @@
     used_rows = tracer_count * own_blocks
     packed_rows = used_rows + -used_rows % 16
     packed_width = source_width + -source_width % 128
-    rows = jnp.swapaxes(histories, 0, 1).reshape(used_rows, source_width)
-    blocks = tile_blocks.T
-    tiles = propagator.reshape(slot_count, tile_height, cell_count)
+    rows, blocks, tiles = (
+        pltpu.with_memory_space_constraint(value, pltpu.HBM)
+        for value in (
+            jnp.swapaxes(histories, 0, 1).reshape(used_rows, source_width),
+            tile_blocks.T,
+            propagator.reshape(slot_count, tile_height, cell_count),
+        )
+    )
     vmem = pl.BlockSpec(memory_space=pltpu.VMEM)
     hbm = pl.BlockSpec(memory_space=pltpu.HBM)
     copies, sorted_tiles, pick, columns, same = pl.pallas_call(
@@ -216,27 +256,34 @@
             pltpu.VMEM(rows.shape, rows.dtype),
             pltpu.SMEM(blocks.shape, blocks.dtype),
             pltpu.VMEM(tiles.shape, tiles.dtype),
-            pltpu.SemaphoreType.DMA((2 + PARTS,)),
+            pltpu.SemaphoreType.DMA((3,)),
         ],
         compiler_params=pltpu.CompilerParams(vmem_limit_bytes=24 * 1024 * 1024),
         cost_estimate=pl.CostEstimate(flops=0, bytes_accessed=tiles.size * 4, transcendentals=0),
-    )(*(pltpu.with_memory_space_constraint(value, pltpu.HBM) for value in (rows, blocks, tiles)))
+    )(rows, blocks, tiles)
 
     inner = [device for device in range(1, size) if device != centre(size)]
     received = exchange(copies, [centre(size)] + inner + [0])
 
     coded = pl.pallas_call(
-        tile_sums,
+        lambda *refs: tile_sums(months, *refs),
         out_shape=jax.ShapeDtypeStruct((size, own_blocks * height + SCALE_ROWS, cell_count), jnp.int16),
-        in_specs=[vmem] * 5,
+        in_specs=[vmem] * 5 + [hbm] * 2,
         out_specs=vmem,
-        compiler_params=pltpu.CompilerParams(vmem_limit_bytes=20 * 1024 * 1024),
+        scratch_shapes=[
+            pltpu.VMEM(pick.shape, pick.dtype),
+            pltpu.VMEM(sorted_tiles.shape, sorted_tiles.dtype),
+            pltpu.SMEM(blocks.shape, blocks.dtype),
+            pltpu.VMEM(tiles.shape, tiles.dtype),
+            pltpu.SemaphoreType.DMA((2,)),
+        ],
+        compiler_params=pltpu.CompilerParams(vmem_limit_bytes=28 * 1024 * 1024),
         cost_estimate=pl.CostEstimate(
             flops=2 * slot_count * height * tile_height * cell_count,
             bytes_accessed=propagator.size * 4,
             transcendentals=0,
         ),
-    )(received, pick, columns, same, sorted_tiles)
+    )(received, pick, columns, same, sorted_tiles, blocks, tiles)
 
     owned = pl.pallas_call(
         add_parts,

time: 23.5 us -> 24.9 us (1.060)
  blocking collectives: 20.6 us -> 22 us
    all_to_all x2, blocking collectives: 20.6 us -> 22 us  [exchange(): lax.all_to_all(value, 'tm', 0, 0, axis_index_groups=[order], tiled=True)]
where the time goes in v21:
time: 24.9 us; the launch traced here: 24.7 us
  blocking collectives  22 us (88%)
  Pallas kernels  2.62 us (11%)
    all_to_all x2, blocking collectives, exchange(): lax.all_to_all(value, 'tm', 0, 0, axis_index_groups=[order], tiled=True)  22 us
    pallas_call x1, Pallas kernels, shards(): pl.pallas_call(lambda *refs: prepare(months, *refs), out_shape=[jax.Shape...  1.25 us
    pallas_call x1, Pallas kernels, shards(): pl.pallas_call(add_parts, out_shape=jax.ShapeDtypeStruct((own_blocks, hei...  0.69 us
    pallas_call x1, Pallas kernels, shards(): pl.pallas_call(lambda *refs: tile_sums(months, *refs), out_shape=jax.Shap...  0.68 us

profile of v21, /device:TPU:0, one launch (start us, length us, event | category | flops | bytes accessed | tf_op | source)
XLA Modules:
  0.0 24.7 jit_solution(13208776639595072314)
XLA Ops:
  0.0 1.2 %shard_map.37 = (bf16[8,32,128]{2,1,0:T(8,128)(2,1)S(1)}, bf16[32,192,128]{2,1,0:T(8,128)(2,1)S(1)}, bf16[96,256]{1,0:T(8,128)(2,1)S(1)}, bf16[128,192]{1,0:T(8,128)(2,1)S(1)}, f32[96,192]{1,0:T(8,128)S(1)}) custom-call(bf16[24,48]{1,0:T(8,128)(2,1)} %bitcast.8, s32[2,17]{1,0:T(2,128)} %bitcast.9, bf16[17,192,128]{2,1,0:T(8,128)(2,1)} %bitcast.6), custom_call_target="tpu_custom_call" | custom-call | bytes 1671168 | tf_op jit(solution)/shard_map/pallas_call | solution.py:244
  1.3 11.0 %all_to_all.10.refs_0_ = bf16[8,32,128]{2,1,0:T(8,128)(2,1)S(1)} all-to-all(bf16[8,32,128]{2,1,0:T(8,128)(2,1)S(1)} %get-tuple-element.10), channel_id=1, replica_groups={{10,2,4,6,8,12,14,0},{11,3,5,7,9,13,15,1},{26,18,20,22,24,28,30,16},{27..., dimensions={0} | all-to-all | bytes 131072 | tf_op jit(solution)/shard_map/all_to_all | solution.py:34
  12.2 0.7 %shard_map.38 = s16[8,104,128]{2,1,0:T(8,128)(2,1)S(1)} custom-call(bf16[8,32,128]{2,1,0:T(8,128)(2,1)S(1)} %all_to_all.10.refs_0_, bf16[96,256]{1,0:T(8,128)(2,1)S(1)} %get-tuple-element.11.refs_1_, bf16[128,192]{1,0:T(8,128)(2,1)S(1)} %get-tuple-element.12.refs_2_, f32[96,192]{1,0:T(8,128)S(1)} %get-tuple-element.13.refs_3_, ...), custom_call_target="tpu_custom_call" | custom-call | flops 40108032 | bytes 1671168 | tf_op jit(solution)/shard_map/pallas_call | solution.py:268
  12.9 11.0 %all_to_all.11.coded_ref = s16[8,104,128]{2,1,0:T(8,128)(2,1)S(1)} all-to-all(s16[8,104,128]{2,1,0:T(8,128)(2,1)S(1)} %shard_map.38), channel_id=1, replica_groups={{14,12,10,8,6,4,2,0},{15,13,11,9,7,5,3,1},{30,28,26,24,22,20,18,16},{31..., dimensions={0} | all-to-all | bytes 425984 | tf_op jit(solution)/shard_map/all_to_all | solution.py:34
  24.0 0.7 %shard_map.39 = f32[2,48,128]{2,1,0:T(8,128)} custom-call(s16[8,104,128]{2,1,0:T(8,128)(2,1)S(1)} %all_to_all.11.coded_ref), custom_call_target="tpu_custom_call" | custom-call | tf_op jit(solution)/shard_map/pallas_call | solution.py:288

commit v22 on v21

--- a/solution.py
+++ b/solution.py
@@ -23,11 +23,10 @@
 
 
 def sums_device(slot, size):
-    return size - 1 - slot
-
-
-def starts_late(size):
-    return lax.axis_index("tm") >= size * 3 // 4
+    if isinstance(slot, int):
+        return centre(size) if slot == 0 else size - slot - (size - slot <= centre(size))
+    after = size - slot - (size - slot <= centre(size)).astype(jnp.int32)
+    return jnp.where(slot == 0, centre(size), after)
 
 
 def exchange(value, order):
@@ -48,14 +47,7 @@
         lax.fori_loop(0, count, lambda index, carry: (body(index), carry)[1], 0)
 
 
-def tile_loads(blocks_in, tiles_in, blocks_ref, tiles_ref, semaphores):
-    return [
-        pltpu.make_async_copy(blocks_in, blocks_ref, semaphores.at[0]),
-        pltpu.make_async_copy(tiles_in, tiles_ref, semaphores.at[1]),
-    ]
-
-
-def arrange(size, months, loads, blocks_ref, tiles_ref, sorted_ref, pick_ref):
+def arrange(size, months, load_blocks, load_tiles, blocks_ref, tiles_ref, sorted_ref, pick_ref):
     slot_count, tile_height, cell_count = tiles_ref.shape
     block_count = sorted_ref.shape[0] // SOURCES
     own_blocks = block_count // size
@@ -69,7 +61,7 @@
     each(size, clear)
     tracer = split(lax.broadcasted_iota(jnp.int32, (height, pick_ref.shape[1]), 0), months)[0]
     offset = lax.broadcasted_iota(jnp.int32, (height, pick_ref.shape[1]), 1) - tracer * own_blocks
-    loads[0].wait()
+    load_blocks.wait()
     first = blocks_ref[0, 0]
 
     def place_of(slot):
@@ -81,7 +73,7 @@
         owner, block = split(source, own_blocks)
         picked = offset == history_slot(owner, size) * packed_rows + block
         pick_ref[pl.ds(which * height, height)] = picked.astype(pick_ref.dtype)
-    loads[1].wait()
+    load_tiles.wait()
 
     def place(slot):
         sorted_ref[places[slot] if places else place_of(slot)] = tiles_ref[slot]
@@ -106,16 +98,11 @@
 ):
     size = copies_ref.shape[0]
     used_rows, source_width = rows_ref.shape
-    early = jnp.logical_not(starts_late(size))
-    load_rows = pltpu.make_async_copy(rows_in, rows_ref, semaphores.at[2])
-    loads = tile_loads(blocks_in, tiles_in, blocks_ref, tiles_ref, semaphores)
-    load_rows.start()
-
-    @pl.when(early)
-    def _():
-        for load in loads:
-            load.start()
-
+    load_rows = pltpu.make_async_copy(rows_in, rows_ref, semaphores.at[0])
+    load_blocks = pltpu.make_async_copy(blocks_in, blocks_ref, semaphores.at[1])
+    load_tiles = pltpu.make_async_copy(tiles_in, tiles_ref, semaphores.at[2])
+    for load in (load_rows, load_blocks, load_tiles):
+        load.start()
     packed_column = lax.broadcasted_iota(jnp.int32, columns_ref.shape, 0)
     column_of = split(lax.broadcasted_iota(jnp.int32, columns_ref.shape, 1), months)[0]
     columns_ref[...] = (column_of == packed_column).astype(columns_ref.dtype)
@@ -129,45 +116,10 @@
         copies_ref[owner, :used_rows, :source_width] = rows_ref[...]
 
     each(size, copy)
-
-    @pl.when(early)
-    def _():
-        arrange(size, months, loads, blocks_ref, tiles_ref, sorted_ref, pick_ref)
-
-
-def tile_sums(
-    months,
-    histories_ref,
-    pick_ref,
-    columns_ref,
-    same_ref,
-    sorted_ref,
-    blocks_in,
-    tiles_in,
-    coded_ref,
-    late_pick_ref,
-    late_sorted_ref,
-    blocks_ref,
-    tiles_ref,
-    semaphores,
-):
-    size = histories_ref.shape[0]
-    late = starts_late(size)
-
-    @pl.when(late)
-    def _():
-        loads = tile_loads(blocks_in, tiles_in, blocks_ref, tiles_ref, semaphores)
-        for load in loads:
-            load.start()
-        arrange(size, months, loads, blocks_ref, tiles_ref, late_sorted_ref, late_pick_ref)
-        code_sums(histories_ref, late_pick_ref, columns_ref, same_ref, late_sorted_ref, coded_ref)
-
-    @pl.when(jnp.logical_not(late))
-    def _():
-        code_sums(histories_ref, pick_ref, columns_ref, same_ref, sorted_ref, coded_ref)
-
-
-def code_sums(histories_ref, pick_ref, columns_ref, same_ref, sorted_ref, coded_ref):
+    arrange(size, months, load_blocks, load_tiles, blocks_ref, tiles_ref, sorted_ref, pick_ref)
+
+
+def tile_sums(histories_ref, pick_ref, columns_ref, same_ref, sorted_ref, coded_ref):
     size, packed_rows, packed_width = histories_ref.shape
     block_count = sorted_ref.shape[0] // SOURCES
     own_blocks = block_count // size
@@ -266,24 +218,17 @@
     received = exchange(copies, [centre(size)] + inner + [0])
 
     coded = pl.pallas_call(
-        lambda *refs: tile_sums(months, *refs),
+        tile_sums,
         out_shape=jax.ShapeDtypeStruct((size, own_blocks * height + SCALE_ROWS, cell_count), jnp.int16),
-        in_specs=[vmem] * 5 + [hbm] * 2,
+        in_specs=[vmem] * 5,
         out_specs=vmem,
-        scratch_shapes=[
-            pltpu.VMEM(pick.shape, pick.dtype),
-            pltpu.VMEM(sorted_tiles.shape, sorted_tiles.dtype),
-            pltpu.SMEM(blocks.shape, blocks.dtype),
-            pltpu.VMEM(tiles.shape, tiles.dtype),
-            pltpu.SemaphoreType.DMA((2,)),
-        ],
-        compiler_params=pltpu.CompilerParams(vmem_limit_bytes=28 * 1024 * 1024),
+        compiler_params=pltpu.CompilerParams(vmem_limit_bytes=20 * 1024 * 1024),
         cost_estimate=pl.CostEstimate(
             flops=2 * slot_count * height * tile_height * cell_count,
             bytes_accessed=propagator.size * 4,
             transcendentals=0,
         ),
-    )(received, pick, columns, same, sorted_tiles, blocks, tiles)
+    )(received, pick, columns, same, sorted_tiles)
 
     owned = pl.pallas_call(
         add_parts,

time: 24.9 us -> 23.5 us (0.944)
  blocking collectives: 22 us -> 20.6 us
    all_to_all x2, blocking collectives: 22 us -> 20.6 us  [exchange(): lax.all_to_all(value, 'tm', 0, 0, axis_index_groups=[order], tiled=True)]
where the time goes in v22:
time: 23.5 us; the launch traced here: 23.2 us
  blocking collectives  20.6 us (88%)
  Pallas kernels  2.6 us (11%)
    all_to_all x2, blocking collectives, exchange(): lax.all_to_all(value, 'tm', 0, 0, axis_index_groups=[order], tiled=True)  20.6 us
    pallas_call x1, Pallas kernels, shards(): pl.pallas_call(lambda *refs: prepare(months, *refs), out_shape=[jax.Shape...  1.25 us
    pallas_call x1, Pallas kernels, shards(): pl.pallas_call(add_parts, out_shape=jax.ShapeDtypeStruct((own_blocks, hei...  0.69 us
    pallas_call x1, Pallas kernels, shards(): pl.pallas_call(tile_sums, out_shape=jax.ShapeDtypeStruct((size, own_block...  0.66 us

profile of v22, /device:TPU:0, one launch (start us, length us, event | category | flops | bytes accessed | tf_op | source)
XLA Modules:
  0.0 23.2 jit_solution(4325049016683061831)
XLA Ops:
  0.0 1.2 %shard_map.37 = (bf16[8,32,128]{2,1,0:T(8,128)(2,1)S(1)}, bf16[32,192,128]{2,1,0:T(8,128)(2,1)S(1)}, bf16[96,256]{1,0:T(8,128)(2,1)S(1)}, bf16[128,192]{1,0:T(8,128)(2,1)S(1)}, f32[96,192]{1,0:T(8,128)S(1)}) custom-call(bf16[24,48]{1,0:T(8,128)(2,1)} %bitcast.7, s32[2,17]{1,0:T(2,128)} %bitcast.8, bf16[17,192,128]{2,1,0:T(8,128)(2,1)} %bitcast.6), custom_call_target="tpu_custom_call" | custom-call | bytes 1671168 | tf_op jit(solution)/shard_map/pallas_call | solution.py:196
  1.3 11.3 %all_to_all.10.histories_ref = bf16[8,32,128]{2,1,0:T(8,128)(2,1)S(1)} all-to-all(bf16[8,32,128]{2,1,0:T(8,128)(2,1)S(1)} %get-tuple-element.10), channel_id=1, replica_groups={{10,2,4,6,8,12,14,0},{11,3,5,7,9,13,15,1},{26,18,20,22,24,28,30,16},{27..., dimensions={0} | all-to-all | bytes 131072 | tf_op jit(solution)/shard_map/all_to_all | solution.py:33
  12.5 0.7 %shard_map.38 = s16[8,104,128]{2,1,0:T(8,128)(2,1)S(1)} custom-call(bf16[8,32,128]{2,1,0:T(8,128)(2,1)S(1)} %all_to_all.10.histories_ref, bf16[96,256]{1,0:T(8,128)(2,1)S(1)} %get-tuple-element.11.pick_ref, bf16[128,192]{1,0:T(8,128)(2,1)S(1)} %get-tuple-element.12.columns_ref, f32[96,192]{1,0:T(8,128)S(1)} %get-tuple-element.13.same_ref, ...), custom_call_target="tpu_custom_call" | custom-call | flops 40108032 | bytes 1671168 | tf_op jit(solution)/shard_map/pallas_call | solution.py:220
  13.2 9.3 %all_to_all.11.coded_ref = s16[8,104,128]{2,1,0:T(8,128)(2,1)S(1)} all-to-all(s16[8,104,128]{2,1,0:T(8,128)(2,1)S(1)} %shard_map.38), channel_id=1, replica_groups={{10,14,12,8,6,4,2,0},{11,15,13,9,7,5,3,1},{26,30,28,24,22,20,18,16},{27..., dimensions={0} | all-to-all | bytes 425984 | tf_op jit(solution)/shard_map/all_to_all | solution.py:33
  22.5 0.7 %shard_map.39 = f32[2,48,128]{2,1,0:T(8,128)} custom-call(s16[8,104,128]{2,1,0:T(8,128)(2,1)S(1)} %all_to_all.11.coded_ref), custom_call_target="tpu_custom_call" | custom-call | tf_op jit(solution)/shard_map/pallas_call | solution.py:233

commit v23 on v22

--- a/solution.py
+++ b/solution.py
@@ -48,28 +48,28 @@
 
 
 def arrange(size, months, load_blocks, load_tiles, blocks_ref, tiles_ref, sorted_ref, pick_ref):
-    slot_count, tile_height, cell_count = tiles_ref.shape
-    block_count = sorted_ref.shape[0] // SOURCES
+    slot_count = tiles_ref.shape[0]
+    half_count = sorted_ref.shape[0] // 3
+    block_count = half_count * 2
     own_blocks = block_count // size
     height = pick_ref.shape[0] // SOURCES
     packed_rows = pick_ref.shape[1] // size
-
-    def clear(owner):
-        rows = pl.ds(owner * SOURCES * own_blocks, SOURCES * own_blocks)
-        sorted_ref[rows] = jnp.zeros((SOURCES * own_blocks, tile_height, cell_count), sorted_ref.dtype)
+    group = sorted_ref.shape[0] // size
+
+    def clear(index):
+        sorted_ref[pl.ds(index * group, group)] = jnp.zeros((group,) + tiles_ref.shape[1:], sorted_ref.dtype)
 
     each(size, clear)
     tracer = split(lax.broadcasted_iota(jnp.int32, (height, pick_ref.shape[1]), 0), months)[0]
     offset = lax.broadcasted_iota(jnp.int32, (height, pick_ref.shape[1]), 1) - tracer * own_blocks
     load_blocks.wait()
-    first = blocks_ref[0, 0]
+    lower = jnp.minimum(blocks_ref[0, 0], block_count - 1 - blocks_ref[0, 0])
 
     def place_of(slot):
-        which = (blocks_ref[0, slot] != first).astype(jnp.int32)
-        return which * block_count + blocks_ref[1, slot]
+        return blocks_ref[1, slot] + jnp.where(blocks_ref[0, slot] == lower, 0, half_count)
 
     places = [place_of(slot) for slot in range(slot_count)] if slot_count <= WRITTEN_OUT else None
-    for which, source in enumerate((first, block_count - 1 - first)):
+    for which, source in enumerate((lower, block_count - 1 - lower)):
         owner, block = split(source, own_blocks)
         picked = offset == history_slot(owner, size) * packed_rows + block
         pick_ref[pl.ds(which * height, height)] = picked.astype(pick_ref.dtype)
@@ -121,8 +121,8 @@
 
 def tile_sums(histories_ref, pick_ref, columns_ref, same_ref, sorted_ref, coded_ref):
     size, packed_rows, packed_width = histories_ref.shape
-    block_count = sorted_ref.shape[0] // SOURCES
-    own_blocks = block_count // size
+    half_count = sorted_ref.shape[0] // 3
+    own_blocks = half_count * 2 // size
     height = pick_ref.shape[0] // SOURCES
     cell_count = coded_ref.shape[2]
     coded_rows = own_blocks * height
@@ -132,14 +132,21 @@
     wide = jnp.dot(tall.astype(jnp.bfloat16), columns_ref[...], preferred_element_type=jnp.float32)
     wide = (wide * same_ref[...]).astype(jnp.bfloat16)
 
+    def product(which, start):
+        tiles = jnp.concatenate([sorted_ref[start + block] for block in range(own_blocks)], axis=1)
+        rows = wide[which * height : (which + 1) * height]
+        return jnp.dot(rows, tiles, preferred_element_type=jnp.float32)
+
     def code(slot):
-        total = None
-        for which in range(SOURCES):
-            start = which * block_count + sums_device(slot, size) * own_blocks
-            tiles = jnp.concatenate([sorted_ref[start + block] for block in range(own_blocks)], axis=1)
-            rows = wide[which * height : (which + 1) * height]
-            part = jnp.dot(rows, tiles, preferred_element_type=jnp.float32)
-            total = part if total is None else total + part
+        owner = sums_device(slot, size)
+        start = owner * own_blocks
+        total = product(0, start)
+        if isinstance(slot, int):
+            if owner >= size // 2:
+                total += product(1, half_count + start)
+        else:
+            upper = product(1, half_count + jnp.maximum(start, half_count))
+            total += jnp.where(owner >= size // 2, upper, 0.0)
         values = [total[:, block * cell_count : (block + 1) * cell_count] for block in range(own_blocks)]
         top = jnp.abs(values[0])
         for value in values[1:]:
@@ -197,7 +204,7 @@
         lambda *refs: prepare(months, *refs),
         out_shape=[
             jax.ShapeDtypeStruct((size, packed_rows, packed_width), rows.dtype),
-            jax.ShapeDtypeStruct((SOURCES * block_count, tile_height, cell_count), tiles.dtype),
+            jax.ShapeDtypeStruct((block_count + block_count // 2, tile_height, cell_count), tiles.dtype),
             jax.ShapeDtypeStruct((SOURCES * height, size * packed_rows), jnp.bfloat16),
             jax.ShapeDtypeStruct((packed_width, tile_height), jnp.bfloat16),
             jax.ShapeDtypeStruct((SOURCES * height, tile_height), jnp.float32),

time: 23.5 us -> 23.4 us (level)
  no operation moved by 1% of the time
where the time goes in v23:
time: 23.4 us; the launch traced here: 23.2 us
  blocking collectives  20.6 us (88%)
  Pallas kernels  2.55 us (11%)
    all_to_all x2, blocking collectives, exchange(): lax.all_to_all(value, 'tm', 0, 0, axis_index_groups=[order], tiled=True)  20.6 us
    pallas_call x1, Pallas kernels, shards(): pl.pallas_call(lambda *refs: prepare(months, *refs), out_shape=[jax.Shape...  1.25 us
    pallas_call x1, Pallas kernels, shards(): pl.pallas_call(add_parts, out_shape=jax.ShapeDtypeStruct((own_blocks, hei...  0.69 us
    pallas_call x1, Pallas kernels, shards(): pl.pallas_call(tile_sums, out_shape=jax.ShapeDtypeStruct((size, own_block...  0.61 us

profile of v23, /device:TPU:0, one launch (start us, length us, event | category | flops | bytes accessed | tf_op | source)
XLA Modules:
  0.0 23.2 jit_solution(9960548921814537090)
XLA Ops:
  0.0 1.2 %shard_map.37 = (bf16[8,32,128]{2,1,0:T(8,128)(2,1)S(1)}, bf16[24,192,128]{2,1,0:T(8,128)(2,1)S(1)}, bf16[96,256]{1,0:T(8,128)(2,1)S(1)}, bf16[128,192]{1,0:T(8,128)(2,1)S(1)}, f32[96,192]{1,0:T(8,128)S(1)}) custom-call(bf16[24,48]{1,0:T(8,128)(2,1)} %bitcast.7, s32[2,17]{1,0:T(2,128)} %bitcast.8, bf16[17,192,128]{2,1,0:T(8,128)(2,1)} %bitcast.6), custom_call_target="tpu_custom_call" | custom-call | bytes 1671168 | tf_op jit(solution)/shard_map/pallas_call | solution.py:203
  1.3 11.3 %all_to_all.10.histories_ref = bf16[8,32,128]{2,1,0:T(8,128)(2,1)S(1)} all-to-all(bf16[8,32,128]{2,1,0:T(8,128)(2,1)S(1)} %get-tuple-element.10), channel_id=1, replica_groups={{10,2,4,6,8,12,14,0},{11,3,5,7,9,13,15,1},{26,18,20,22,24,28,30,16},{27..., dimensions={0} | all-to-all | bytes 131072 | tf_op jit(solution)/shard_map/all_to_all | solution.py:33
  12.5 0.6 %shard_map.38 = s16[8,104,128]{2,1,0:T(8,128)(2,1)S(1)} custom-call(bf16[8,32,128]{2,1,0:T(8,128)(2,1)S(1)} %all_to_all.10.histories_ref, bf16[96,256]{1,0:T(8,128)(2,1)S(1)} %get-tuple-element.11.pick_ref, bf16[128,192]{1,0:T(8,128)(2,1)S(1)} %get-tuple-element.12.columns_ref, f32[96,192]{1,0:T(8,128)S(1)} %get-tuple-element.13.same_ref, ...), custom_call_target="tpu_custom_call" | custom-call | flops 40108032 | bytes 1671168 | tf_op jit(solution)/shard_map/pallas_call | solution.py:227
  13.1 9.3 %all_to_all.11.coded_ref = s16[8,104,128]{2,1,0:T(8,128)(2,1)S(1)} all-to-all(s16[8,104,128]{2,1,0:T(8,128)(2,1)S(1)} %shard_map.38), channel_id=1, replica_groups={{10,14,12,8,6,4,2,0},{11,15,13,9,7,5,3,1},{26,30,28,24,22,20,18,16},{27..., dimensions={0} | all-to-all | bytes 425984 | tf_op jit(solution)/shard_map/all_to_all | solution.py:33
  22.5 0.7 %shard_map.39 = f32[2,48,128]{2,1,0:T(8,128)} custom-call(s16[8,104,128]{2,1,0:T(8,128)(2,1)S(1)} %all_to_all.11.coded_ref), custom_call_target="tpu_custom_call" | custom-call | tf_op jit(solution)/shard_map/pallas_call | solution.py:240

commit v24 on v23

--- a/solution.py
+++ b/solution.py
@@ -47,7 +47,9 @@
         lax.fori_loop(0, count, lambda index, carry: (body(index), carry)[1], 0)
 
 
-def arrange(size, months, load_blocks, load_tiles, blocks_ref, tiles_ref, sorted_ref, pick_ref):
+def arrange(
+    size, months, source_width, load_blocks, load_tiles, blocks_ref, tiles_ref, sorted_ref, pick_ref, columns_ref
+):
     slot_count = tiles_ref.shape[0]
     half_count = sorted_ref.shape[0] // 3
     block_count = half_count * 2
@@ -61,7 +63,9 @@
 
     each(size, clear)
     tracer = split(lax.broadcasted_iota(jnp.int32, (height, pick_ref.shape[1]), 0), months)[0]
-    offset = lax.broadcasted_iota(jnp.int32, (height, pick_ref.shape[1]), 1) - tracer * own_blocks
+    offset = lax.broadcasted_iota(jnp.int32, (height, pick_ref.shape[1]), 1) - tracer
+    column_of = split(lax.broadcasted_iota(jnp.int32, columns_ref.shape[1:], 1), months)[0]
+    shift = lax.broadcasted_iota(jnp.int32, columns_ref.shape[1:], 0) - column_of
     load_blocks.wait()
     lower = jnp.minimum(blocks_ref[0, 0], block_count - 1 - blocks_ref[0, 0])
 
@@ -71,8 +75,9 @@
     places = [place_of(slot) for slot in range(slot_count)] if slot_count <= WRITTEN_OUT else None
     for which, source in enumerate((lower, block_count - 1 - lower)):
         owner, block = split(source, own_blocks)
-        picked = offset == history_slot(owner, size) * packed_rows + block
+        picked = offset == history_slot(owner, size) * packed_rows
         pick_ref[pl.ds(which * height, height)] = picked.astype(pick_ref.dtype)
+        columns_ref[which] = (shift == block * source_width).astype(columns_ref.dtype)
     load_tiles.wait()
 
     def place(slot):
@@ -92,31 +97,55 @@
     columns_ref,
     same_ref,
     rows_ref,
+    padded_ref,
     blocks_ref,
     tiles_ref,
     semaphores,
 ):
-    size = copies_ref.shape[0]
+    size, packed_rows, packed_width = copies_ref.shape
     used_rows, source_width = rows_ref.shape
+    own_blocks = sorted_ref.shape[0] // 3 * 2 // size
     load_rows = pltpu.make_async_copy(rows_in, rows_ref, semaphores.at[0])
     load_blocks = pltpu.make_async_copy(blocks_in, blocks_ref, semaphores.at[1])
     load_tiles = pltpu.make_async_copy(tiles_in, tiles_ref, semaphores.at[2])
     for load in (load_rows, load_blocks, load_tiles):
         load.start()
-    packed_column = lax.broadcasted_iota(jnp.int32, columns_ref.shape, 0)
-    column_of = split(lax.broadcasted_iota(jnp.int32, columns_ref.shape, 1), months)[0]
-    columns_ref[...] = (column_of == packed_column).astype(columns_ref.dtype)
     month_of_row = split(lax.broadcasted_iota(jnp.int32, same_ref.shape, 0), months)[1]
     month_of_column = split(lax.broadcasted_iota(jnp.int32, same_ref.shape, 1), months)[1]
     same_ref[...] = (month_of_row == month_of_column).astype(same_ref.dtype)
-    copies_ref[...] = jnp.zeros(copies_ref.shape, copies_ref.dtype)
+    padded_ref[...] = jnp.zeros(padded_ref.shape, padded_ref.dtype)
+    taker = (packed_rows, padded_ref.shape[0])
+    placer = (padded_ref.shape[1], packed_width)
+    take = lax.broadcasted_iota(jnp.int32, taker, 1) - lax.broadcasted_iota(jnp.int32, taker, 0) * own_blocks
+    put = lax.broadcasted_iota(jnp.int32, placer, 1) - lax.broadcasted_iota(jnp.int32, placer, 0)
     load_rows.wait()
+    padded_ref[:used_rows, :source_width] = rows_ref[...]
+    packed = jnp.zeros((packed_rows, packed_width), jnp.float32)
+    for block in range(own_blocks):
+        taken = jnp.dot((take == block).astype(padded_ref.dtype), padded_ref[...], preferred_element_type=jnp.float32)
+        packed += jnp.dot(
+            taken.astype(padded_ref.dtype),
+            (put == block * source_width).astype(padded_ref.dtype),
+            preferred_element_type=jnp.float32,
+        )
+    packed = packed.astype(copies_ref.dtype)
 
     def copy(owner):
-        copies_ref[owner, :used_rows, :source_width] = rows_ref[...]
+        copies_ref[owner] = packed
 
     each(size, copy)
-    arrange(size, months, load_blocks, load_tiles, blocks_ref, tiles_ref, sorted_ref, pick_ref)
+    arrange(
+        size,
+        months,
+        source_width,
+        load_blocks,
+        load_tiles,
+        blocks_ref,
+        tiles_ref,
+        sorted_ref,
+        pick_ref,
+        columns_ref,
+    )
 
 
 def tile_sums(histories_ref, pick_ref, columns_ref, same_ref, sorted_ref, coded_ref):
@@ -129,13 +158,16 @@
 
     histories = histories_ref[...].reshape(size * packed_rows, packed_width)
     tall = jnp.dot(pick_ref[...], histories, preferred_element_type=jnp.float32)
-    wide = jnp.dot(tall.astype(jnp.bfloat16), columns_ref[...], preferred_element_type=jnp.float32)
-    wide = (wide * same_ref[...]).astype(jnp.bfloat16)
+    tall = tall.astype(jnp.bfloat16)
+    wide = []
+    for which in range(SOURCES):
+        rows = tall[which * height : (which + 1) * height]
+        widened = jnp.dot(rows, columns_ref[which], preferred_element_type=jnp.float32)
+        wide.append((widened * same_ref[...]).astype(jnp.bfloat16))
 
     def product(which, start):
         tiles = jnp.concatenate([sorted_ref[start + block] for block in range(own_blocks)], axis=1)
-        rows = wide[which * height : (which + 1) * height]
-        return jnp.dot(rows, tiles, preferred_element_type=jnp.float32)
+        return jnp.dot(wide[which], tiles, preferred_element_type=jnp.float32)
 
     def code(slot):
         owner = sums_device(slot, size)
@@ -188,8 +220,9 @@
     tile_height = source_width * months
 
     used_rows = tracer_count * own_blocks
-    packed_rows = used_rows + -used_rows % 16
-    packed_width = source_width + -source_width % 128
+    padded_shape = (used_rows + -used_rows % 16, source_width + -source_width % 128)
+    packed_rows = tracer_count + -tracer_count % 16
+    packed_width = own_blocks * source_width + -(own_blocks * source_width) % 128
     rows, blocks, tiles = (
         pltpu.with_memory_space_constraint(value, pltpu.HBM)
         for value in (
@@ -206,13 +239,14 @@
             jax.ShapeDtypeStruct((size, packed_rows, packed_width), rows.dtype),
             jax.ShapeDtypeStruct((block_count + block_count // 2, tile_height, cell_count), tiles.dtype),
             jax.ShapeDtypeStruct((SOURCES * height, size * packed_rows), jnp.bfloat16),
-            jax.ShapeDtypeStruct((packed_width, tile_height), jnp.bfloat16),
-            jax.ShapeDtypeStruct((SOURCES * height, tile_height), jnp.float32),
+            jax.ShapeDtypeStruct((SOURCES, packed_width, tile_height), jnp.bfloat16),
+            jax.ShapeDtypeStruct((height, tile_height), jnp.float32),
         ],
         in_specs=[hbm] * 3,
         out_specs=[vmem] * 5,
         scratch_shapes=[
             pltpu.VMEM(rows.shape, rows.dtype),
+            pltpu.VMEM(padded_shape, rows.dtype),
             pltpu.SMEM(blocks.shape, blocks.dtype),
             pltpu.VMEM(tiles.shape, tiles.dtype),
             pltpu.SemaphoreType.DMA((3,)),

time: 23.4 us -> 23.1 us (0.987)
  blocking collectives: 20.6 us -> 20.3 us
    all_to_all x2, blocking collectives: 20.6 us -> 20.3 us  [exchange(): lax.all_to_all(value, 'tm', 0, 0, axis_index_groups=[order], tiled=True)]
where the time goes in v24:
time: 23.1 us; the launch traced here: 22.9 us
  blocking collectives  20.3 us (88%)
  Pallas kernels  2.54 us (11%)
    all_to_all x2, blocking collectives, exchange(): lax.all_to_all(value, 'tm', 0, 0, axis_index_groups=[order], tiled=True)  20.3 us
    pallas_call x1, Pallas kernels, shards(): pl.pallas_call(lambda *refs: prepare(months, *refs), out_shape=[jax.Shape...  1.25 us
    pallas_call x1, Pallas kernels, shards(): pl.pallas_call(add_parts, out_shape=jax.ShapeDtypeStruct((own_blocks, hei...  0.69 us
    pallas_call x1, Pallas kernels, shards(): pl.pallas_call(tile_sums, out_shape=jax.ShapeDtypeStruct((size, own_block...  0.6 us

profile of v24, /device:TPU:0, one launch (start us, length us, event | category | flops | bytes accessed | tf_op | source)
XLA Modules:
  0.0 22.9 jit_solution(9081806109922033284)
XLA Ops:
  0.0 1.2 %shard_map.37 = (bf16[8,16,128]{2,1,0:T(8,128)(2,1)S(1)}, bf16[24,192,128]{2,1,0:T(8,128)(2,1)S(1)}, bf16[96,128]{1,0:T(8,128)(2,1)S(1)}, bf16[2,128,192]{2,1,0:T(8,128)(2,1)S(1)}, f32[48,192]{1,0:T(8,128)S(1)}) custom-call(bf16[24,48]{1,0:T(8,128)(2,1)} %bitcast.7, s32[2,17]{1,0:T(2,128)} %bitcast.8, bf16[17,192,128]{2,1,0:T(8,128)(2,1)} %bitcast.6), custom_call_target="tpu_custom_call" | custom-call | bytes 1671168 | tf_op jit(solution)/shard_map/pallas_call | solution.py:236
  1.3 11.0 %all_to_all.10.histories_ref = bf16[8,16,128]{2,1,0:T(8,128)(2,1)S(1)} all-to-all(bf16[8,16,128]{2,1,0:T(8,128)(2,1)S(1)} %get-tuple-element.10), channel_id=1, replica_groups={{10,2,4,6,8,12,14,0},{11,3,5,7,9,13,15,1},{26,18,20,22,24,28,30,16},{27..., dimensions={0} | all-to-all | bytes 65536 | tf_op jit(solution)/shard_map/all_to_all | solution.py:33
  12.3 0.6 %shard_map.38 = s16[8,104,128]{2,1,0:T(8,128)(2,1)S(1)} custom-call(bf16[8,16,128]{2,1,0:T(8,128)(2,1)S(1)} %all_to_all.10.histories_ref, bf16[96,128]{1,0:T(8,128)(2,1)S(1)} %get-tuple-element.11.pick_ref, bf16[2,128,192]{2,1,0:T(8,128)(2,1)S(1)} %get-tuple-element.12.columns_ref, f32[48,192]{1,0:T(8,128)S(1)} %get-tuple-element.13.same_ref, ...), custom_call_target="tpu_custom_call" | custom-call | flops 40108032 | bytes 1671168 | tf_op jit(solution)/shard_map/pallas_call | solution.py:261
  12.9 9.3 %all_to_all.11.coded_ref = s16[8,104,128]{2,1,0:T(8,128)(2,1)S(1)} all-to-all(s16[8,104,128]{2,1,0:T(8,128)(2,1)S(1)} %shard_map.38), channel_id=1, replica_groups={{10,14,12,8,6,4,2,0},{11,15,13,9,7,5,3,1},{26,30,28,24,22,20,18,16},{27..., dimensions={0} | all-to-all | bytes 425984 | tf_op jit(solution)/shard_map/all_to_all | solution.py:33
  22.2 0.7 %shard_map.39 = f32[2,48,128]{2,1,0:T(8,128)} custom-call(s16[8,104,128]{2,1,0:T(8,128)(2,1)S(1)} %all_to_all.11.coded_ref), custom_call_target="tpu_custom_call" | custom-call | tf_op jit(solution)/shard_map/pallas_call | solution.py:274

commit v25 on v24

--- a/solution.py
+++ b/solution.py
@@ -195,20 +195,29 @@
     each(size, code)
 
 
-def add_parts(coded_ref, total_ref):
+def add_parts(coded_ref, total_out, total_ref, semaphores):
     size = coded_ref.shape[0]
     own_blocks, height, cell_count = total_ref.shape
-    coded_rows = own_blocks * height
-    total_ref[...] = jnp.zeros(total_ref.shape, total_ref.dtype)
-
-    def add(slot):
-        level = coded_ref[slot, pl.ds(coded_rows, SCALE_ROWS)].astype(jnp.int32).astype(jnp.float32)[:1]
-        half = jnp.exp2(level * (0.5 / LEVELS))
-        for block in range(own_blocks):
+    stores = []
+    for block in range(own_blocks):
+
+        def add(slot, total):
+            level = coded_ref[slot, pl.ds(own_blocks * height, SCALE_ROWS)].astype(jnp.int32)
+            half = jnp.exp2(level.astype(jnp.float32)[:1] * (0.5 / LEVELS))
             steps = coded_ref[slot, pl.ds(block * height, height)].astype(jnp.int32)
-            total_ref[block] += steps.astype(jnp.float32) * (half * (1.0 / STEPS)) * half
-
-    each(size, add)
+            return total + steps.astype(jnp.float32) * (half * (1.0 / STEPS)) * half
+
+        total = jnp.zeros((height, cell_count), jnp.float32)
+        if size <= WRITTEN_OUT:
+            for slot in range(size):
+                total = add(slot, total)
+        else:
+            total = lax.fori_loop(0, size, add, total)
+        total_ref[block] = total
+        stores.append(pltpu.make_async_copy(total_ref.at[block], total_out.at[block], semaphores.at[block]))
+        stores[-1].start()
+    for store in stores:
+        store.wait()
 
 
 def shards(propagator, tile_blocks, histories):
@@ -275,7 +284,11 @@
         add_parts,
         out_shape=jax.ShapeDtypeStruct((own_blocks, height, cell_count), jnp.float32),
         in_specs=[vmem],
-        out_specs=vmem,
+        out_specs=hbm,
+        scratch_shapes=[
+            pltpu.VMEM((own_blocks, height, cell_count), jnp.float32),
+            pltpu.SemaphoreType.DMA((own_blocks,)),
+        ],
         compiler_params=pltpu.CompilerParams(vmem_limit_bytes=16 * 1024 * 1024),
     )(exchange(coded, [sums_device(slot, size) for slot in range(size)]))
     return owned.reshape(own_blocks, tracer_count, months, cell_count)

time: 23.1 us -> 23.1 us (level)
  no operation moved by 1% of the time
where the time goes in v25:
time: 23.1 us; the launch traced here: 22.9 us
  blocking collectives  20.3 us (88%)
  Pallas kernels  2.55 us (11%)
    all_to_all x2, blocking collectives, exchange(): lax.all_to_all(value, 'tm', 0, 0, axis_index_groups=[order], tiled=True)  20.3 us
    pallas_call x1, Pallas kernels, shards(): pl.pallas_call(lambda *refs: prepare(months, *refs), out_shape=[jax.Shape...  1.25 us
    pallas_call x1, Pallas kernels, shards(): pl.pallas_call(add_parts, out_shape=jax.ShapeDtypeStruct((own_blocks, hei...  0.7 us
    pallas_call x1, Pallas kernels, shards(): pl.pallas_call(tile_sums, out_shape=jax.ShapeDtypeStruct((size, own_block...  0.6 us

profile of v25, /device:TPU:0, one launch (start us, length us, event | category | flops | bytes accessed | tf_op | source)
XLA Modules:
  0.0 22.9 jit_solution(6973285096115103580)
XLA Ops:
  0.0 1.2 %shard_map.37 = (bf16[8,16,128]{2,1,0:T(8,128)(2,1)S(1)}, bf16[24,192,128]{2,1,0:T(8,128)(2,1)S(1)}, bf16[96,128]{1,0:T(8,128)(2,1)S(1)}, bf16[2,128,192]{2,1,0:T(8,128)(2,1)S(1)}, f32[48,192]{1,0:T(8,128)S(1)}) custom-call(bf16[24,48]{1,0:T(8,128)(2,1)} %bitcast.7, s32[2,17]{1,0:T(2,128)} %bitcast.8, bf16[17,192,128]{2,1,0:T(8,128)(2,1)} %bitcast.6), custom_call_target="tpu_custom_call" | custom-call | bytes 1671168 | tf_op jit(solution)/shard_map/pallas_call | solution.py:245
  1.3 11.0 %all_to_all.10.histories_ref = bf16[8,16,128]{2,1,0:T(8,128)(2,1)S(1)} all-to-all(bf16[8,16,128]{2,1,0:T(8,128)(2,1)S(1)} %get-tuple-element.10), channel_id=1, replica_groups={{10,2,4,6,8,12,14,0},{11,3,5,7,9,13,15,1},{26,18,20,22,24,28,30,16},{27..., dimensions={0} | all-to-all | bytes 65536 | tf_op jit(solution)/shard_map/all_to_all | solution.py:33
  12.3 0.6 %shard_map.38 = s16[8,104,128]{2,1,0:T(8,128)(2,1)S(1)} custom-call(bf16[8,16,128]{2,1,0:T(8,128)(2,1)S(1)} %all_to_all.10.histories_ref, bf16[96,128]{1,0:T(8,128)(2,1)S(1)} %get-tuple-element.11.pick_ref, bf16[2,128,192]{2,1,0:T(8,128)(2,1)S(1)} %get-tuple-element.12.columns_ref, f32[48,192]{1,0:T(8,128)S(1)} %get-tuple-element.13.same_ref, ...), custom_call_target="tpu_custom_call" | custom-call | flops 40108032 | bytes 1671168 | tf_op jit(solution)/shard_map/pallas_call | solution.py:270
  12.9 9.3 %all_to_all.11.coded_ref = s16[8,104,128]{2,1,0:T(8,128)(2,1)S(1)} all-to-all(s16[8,104,128]{2,1,0:T(8,128)(2,1)S(1)} %shard_map.38), channel_id=1, replica_groups={{10,14,12,8,6,4,2,0},{11,15,13,9,7,5,3,1},{26,30,28,24,22,20,18,16},{27..., dimensions={0} | all-to-all | bytes 425984 | tf_op jit(solution)/shard_map/all_to_all | solution.py:33
  22.2 0.7 %shard_map.39 = f32[2,48,128]{2,1,0:T(8,128)} custom-call(s16[8,104,128]{2,1,0:T(8,128)(2,1)S(1)} %all_to_all.11.coded_ref), custom_call_target="tpu_custom_call" | custom-call | tf_op jit(solution)/shard_map/pallas_call | solution.py:283

commit v26 on v25

--- a/solution.py
+++ b/solution.py
@@ -23,10 +23,11 @@
 
 
 def sums_device(slot, size):
+    after = slot - (slot > size // 2) * 1
     if isinstance(slot, int):
-        return centre(size) if slot == 0 else size - slot - (size - slot <= centre(size))
-    after = size - slot - (size - slot <= centre(size)).astype(jnp.int32)
-    return jnp.where(slot == 0, centre(size), after)
+        return centre(size) if slot == 0 else 0 if slot == size // 2 else after + (after >= centre(size))
+    after = after + (after >= centre(size)).astype(jnp.int32)
+    return jnp.where(slot == 0, centre(size), jnp.where(slot == size // 2, 0, after))
 
 
 def exchange(value, order):

time: 23.1 us -> 23.1 us (level)
  no operation moved by 1% of the time
where the time goes in v26:
time: 23.1 us; the launch traced here: 22.9 us
  blocking collectives  20.3 us (88%)
  Pallas kernels  2.52 us (11%)
    all_to_all x2, blocking collectives, exchange(): lax.all_to_all(value, 'tm', 0, 0, axis_index_groups=[order], tiled=True)  20.3 us
    pallas_call x1, Pallas kernels, shards(): pl.pallas_call(lambda *refs: prepare(months, *refs), out_shape=[jax.Shape...  1.25 us
    pallas_call x1, Pallas kernels, shards(): pl.pallas_call(add_parts, out_shape=jax.ShapeDtypeStruct((own_blocks, hei...  0.7 us
    pallas_call x1, Pallas kernels, shards(): pl.pallas_call(tile_sums, out_shape=jax.ShapeDtypeStruct((size, own_block...  0.57 us

profile of v26, /device:TPU:0, one launch (start us, length us, event | category | flops | bytes accessed | tf_op | source)
XLA Modules:
  0.0 22.9 jit_solution(10791936879729956338)
XLA Ops:
  0.0 1.2 %shard_map.37 = (bf16[8,16,128]{2,1,0:T(8,128)(2,1)S(1)}, bf16[24,192,128]{2,1,0:T(8,128)(2,1)S(1)}, bf16[96,128]{1,0:T(8,128)(2,1)S(1)}, bf16[2,128,192]{2,1,0:T(8,128)(2,1)S(1)}, f32[48,192]{1,0:T(8,128)S(1)}) custom-call(bf16[24,48]{1,0:T(8,128)(2,1)} %bitcast.7, s32[2,17]{1,0:T(2,128)} %bitcast.8, bf16[17,192,128]{2,1,0:T(8,128)(2,1)} %bitcast.6), custom_call_target="tpu_custom_call" | custom-call | bytes 1671168 | tf_op jit(solution)/shard_map/pallas_call | solution.py:246
  1.3 11.0 %all_to_all.10.histories_ref = bf16[8,16,128]{2,1,0:T(8,128)(2,1)S(1)} all-to-all(bf16[8,16,128]{2,1,0:T(8,128)(2,1)S(1)} %get-tuple-element.10), channel_id=1, replica_groups={{10,2,4,6,8,12,14,0},{11,3,5,7,9,13,15,1},{26,18,20,22,24,28,30,16},{27..., dimensions={0} | all-to-all | bytes 65536 | tf_op jit(solution)/shard_map/all_to_all | solution.py:34
  12.3 0.6 %shard_map.38 = s16[8,104,128]{2,1,0:T(8,128)(2,1)S(1)} custom-call(bf16[8,16,128]{2,1,0:T(8,128)(2,1)S(1)} %all_to_all.10.histories_ref, bf16[96,128]{1,0:T(8,128)(2,1)S(1)} %get-tuple-element.11.pick_ref, bf16[2,128,192]{2,1,0:T(8,128)(2,1)S(1)} %get-tuple-element.12.columns_ref, f32[48,192]{1,0:T(8,128)S(1)} %get-tuple-element.13.same_ref, ...), custom_call_target="tpu_custom_call" | custom-call | flops 40108032 | bytes 1671168 | tf_op jit(solution)/shard_map/pallas_call | solution.py:271
  12.9 9.3 %all_to_all.11.coded_ref = s16[8,104,128]{2,1,0:T(8,128)(2,1)S(1)} all-to-all(s16[8,104,128]{2,1,0:T(8,128)(2,1)S(1)} %shard_map.38), channel_id=1, replica_groups={{10,2,4,6,0,8,12,14},{11,3,5,7,1,9,13,15},{26,18,20,22,16,24,28,30},{27..., dimensions={0} | all-to-all | bytes 425984 | tf_op jit(solution)/shard_map/all_to_all | solution.py:34
  22.2 0.7 %shard_map.39 = f32[2,48,128]{2,1,0:T(8,128)} custom-call(s16[8,104,128]{2,1,0:T(8,128)(2,1)S(1)} %all_to_all.11.coded_ref), custom_call_target="tpu_custom_call" | custom-call | tf_op jit(solution)/shard_map/pallas_call | solution.py:284

commit v27 on v25

--- a/solution.py
+++ b/solution.py
@@ -17,9 +17,15 @@
     return size * 5 // 8
 
 
+def history_order(size):
+    inner = [device for device in range(1, size) if device != centre(size)]
+    return [centre(size)] + inner[: size // 2 - 1] + [0] + inner[size // 2 - 1 :]
+
+
 def history_slot(device, size):
     after = device - (device > centre(size)).astype(jnp.int32)
-    return jnp.where(device == centre(size), 0, jnp.where(device == 0, size - 1, after))
+    after = after + (after >= size // 2).astype(jnp.int32)
+    return jnp.where(device == centre(size), 0, jnp.where(device == 0, size // 2, after))
 
 
 def sums_device(slot, size):
@@ -264,8 +270,7 @@
         cost_estimate=pl.CostEstimate(flops=0, bytes_accessed=tiles.size * 4, transcendentals=0),
     )(rows, blocks, tiles)
 
-    inner = [device for device in range(1, size) if device != centre(size)]
-    received = exchange(copies, [centre(size)] + inner + [0])
+    received = exchange(copies, history_order(size))
 
     coded = pl.pallas_call(
         tile_sums,

time: 23.1 us -> 23.1 us (level)
  no operation moved by 1% of the time
where the time goes in v27:
time: 23.1 us; the launch traced here: 22.8 us
  blocking collectives  20.2 us (87%)
  Pallas kernels  2.54 us (11%)
    all_to_all x2, blocking collectives, exchange(): lax.all_to_all(value, 'tm', 0, 0, axis_index_groups=[order], tiled=True)  20.2 us
    pallas_call x1, Pallas kernels, shards(): pl.pallas_call(lambda *refs: prepare(months, *refs), out_shape=[jax.Shape...  1.25 us
    pallas_call x1, Pallas kernels, shards(): pl.pallas_call(add_parts, out_shape=jax.ShapeDtypeStruct((own_blocks, hei...  0.7 us
    pallas_call x1, Pallas kernels, shards(): pl.pallas_call(tile_sums, out_shape=jax.ShapeDtypeStruct((size, own_block...  0.6 us

profile of v27, /device:TPU:0, one launch (start us, length us, event | category | flops | bytes accessed | tf_op | source)
XLA Modules:
  0.0 22.8 jit_solution(15840194270991081532)
XLA Ops:
  0.0 1.2 %shard_map.37 = (bf16[8,16,128]{2,1,0:T(8,128)(2,1)S(1)}, bf16[24,192,128]{2,1,0:T(8,128)(2,1)S(1)}, bf16[96,128]{1,0:T(8,128)(2,1)S(1)}, bf16[2,128,192]{2,1,0:T(8,128)(2,1)S(1)}, f32[48,192]{1,0:T(8,128)S(1)}) custom-call(bf16[24,48]{1,0:T(8,128)(2,1)} %bitcast.7, s32[2,17]{1,0:T(2,128)} %bitcast.8, bf16[17,192,128]{2,1,0:T(8,128)(2,1)} %bitcast.6), custom_call_target="tpu_custom_call" | custom-call | bytes 1671168 | tf_op jit(solution)/shard_map/pallas_call | solution.py:251
  1.3 11.0 %all_to_all.10.histories_ref = bf16[8,16,128]{2,1,0:T(8,128)(2,1)S(1)} all-to-all(bf16[8,16,128]{2,1,0:T(8,128)(2,1)S(1)} %get-tuple-element.10), channel_id=1, replica_groups={{10,2,4,6,0,8,12,14},{11,3,5,7,1,9,13,15},{26,18,20,22,16,24,28,30},{27..., dimensions={0} | all-to-all | bytes 65536 | tf_op jit(solution)/shard_map/all_to_all | solution.py:39
  12.3 0.6 %shard_map.38 = s16[8,104,128]{2,1,0:T(8,128)(2,1)S(1)} custom-call(bf16[8,16,128]{2,1,0:T(8,128)(2,1)S(1)} %all_to_all.10.histories_ref, bf16[96,128]{1,0:T(8,128)(2,1)S(1)} %get-tuple-element.11.pick_ref, bf16[2,128,192]{2,1,0:T(8,128)(2,1)S(1)} %get-tuple-element.12.columns_ref, f32[48,192]{1,0:T(8,128)S(1)} %get-tuple-element.13.same_ref, ...), custom_call_target="tpu_custom_call" | custom-call | flops 40108032 | bytes 1671168 | tf_op jit(solution)/shard_map/pallas_call | solution.py:275
  12.9 9.2 %all_to_all.11.coded_ref = s16[8,104,128]{2,1,0:T(8,128)(2,1)S(1)} all-to-all(s16[8,104,128]{2,1,0:T(8,128)(2,1)S(1)} %shard_map.38), channel_id=1, replica_groups={{10,14,12,8,6,4,2,0},{11,15,13,9,7,5,3,1},{26,30,28,24,22,20,18,16},{27..., dimensions={0} | all-to-all | bytes 425984 | tf_op jit(solution)/shard_map/all_to_all | solution.py:39
  22.1 0.7 %shard_map.39 = f32[2,48,128]{2,1,0:T(8,128)} custom-call(s16[8,104,128]{2,1,0:T(8,128)(2,1)S(1)} %all_to_all.11.coded_ref), custom_call_target="tpu_custom_call" | custom-call | tf_op jit(solution)/shard_map/pallas_call | solution.py:288

commit v28 on v27

--- a/solution.py
+++ b/solution.py
@@ -1,3 +1,5 @@
+import functools
+
 import jax
 import jax.numpy as jnp
 from jax import lax
@@ -154,7 +156,9 @@
     )
 
 
-def tile_sums(histories_ref, pick_ref, columns_ref, same_ref, sorted_ref, coded_ref):
+def tile_sums(
+    histories_ref, pick_ref, columns_ref, same_ref, sorted_ref, coded_ref, sums_ref, top_ref, level_ref, half_ref
+):
     size, packed_rows, packed_width = histories_ref.shape
     half_count = sorted_ref.shape[0] // 3
     own_blocks = half_count * 2 // size
@@ -175,7 +179,7 @@
         tiles = jnp.concatenate([sorted_ref[start + block] for block in range(own_blocks)], axis=1)
         return jnp.dot(wide[which], tiles, preferred_element_type=jnp.float32)
 
-    def code(slot):
+    def add_up(slot):
         owner = sums_device(slot, size)
         start = owner * own_blocks
         total = product(0, start)
@@ -185,19 +189,24 @@
         else:
             upper = product(1, half_count + jnp.maximum(start, half_count))
             total += jnp.where(owner >= size // 2, upper, 0.0)
-        values = [total[:, block * cell_count : (block + 1) * cell_count] for block in range(own_blocks)]
-        top = jnp.abs(values[0])
-        for value in values[1:]:
-            top = jnp.maximum(top, jnp.abs(value))
-        top = jnp.max(top, axis=0, keepdims=True)
-        level = jnp.ceil(jnp.log2(jnp.maximum(top, SMALLEST)) * LEVELS)
-        half = jnp.exp2(level * (-0.5 / LEVELS))
-        for block, value in enumerate(values):
+        sums_ref[slot] = total
+        top = jnp.max(jnp.abs(total), axis=0, keepdims=True)
+        tops = [top[:, block * cell_count : (block + 1) * cell_count] for block in range(own_blocks)]
+        top_ref[pl.ds(slot, 1)] = functools.reduce(jnp.maximum, tops)
+
+    def code(slot):
+        half = half_ref[pl.ds(slot, 1)]
+        for block in range(own_blocks):
+            value = sums_ref[slot, :, pl.ds(block * cell_count, cell_count)]
             steps = jnp.round(value * half * (half * STEPS))
             coded_ref[slot, pl.ds(block * height, height)] = steps.astype(jnp.int32).astype(jnp.int16)
-        spread = jnp.broadcast_to(level.astype(jnp.int32), (SCALE_ROWS, cell_count))
+        spread = jnp.broadcast_to(level_ref[pl.ds(slot, 1)], (SCALE_ROWS, cell_count))
         coded_ref[slot, pl.ds(coded_rows, SCALE_ROWS)] = spread.astype(jnp.int16)
 
+    each(size, add_up)
+    level = jnp.ceil(jnp.log2(jnp.maximum(top_ref[...], SMALLEST)) * LEVELS)
+    level_ref[...] = level.astype(jnp.int32)
+    half_ref[...] = jnp.exp2(level * (-0.5 / LEVELS))
     each(size, code)
 
 
@@ -277,6 +286,12 @@
         out_shape=jax.ShapeDtypeStruct((size, own_blocks * height + SCALE_ROWS, cell_count), jnp.int16),
         in_specs=[vmem] * 5,
         out_specs=vmem,
+        scratch_shapes=[
+            pltpu.VMEM((size, height, own_blocks * cell_count), jnp.float32),
+            pltpu.VMEM((size, cell_count), jnp.float32),
+            pltpu.VMEM((size, cell_count), jnp.int32),
+            pltpu.VMEM((size, cell_count), jnp.float32),
+        ],
         compiler_params=pltpu.CompilerParams(vmem_limit_bytes=20 * 1024 * 1024),
         cost_estimate=pl.CostEstimate(
             flops=2 * slot_count * height * tile_height * cell_count,

time: 23.1 us -> 23.1 us (level)
  no operation moved by 1% of the time
where the time goes in v28:
time: 23.1 us; the launch traced here: 22.8 us
  blocking collectives  20.2 us (87%)
  Pallas kernels  2.59 us (11%)
    all_to_all x2, blocking collectives, exchange(): lax.all_to_all(value, 'tm', 0, 0, axis_index_groups=[order], tiled=True)  20.2 us
    pallas_call x1, Pallas kernels, shards(): pl.pallas_call(lambda *refs: prepare(months, *refs), out_shape=[jax.Shape...  1.25 us
    pallas_call x1, Pallas kernels, shards(): pl.pallas_call(add_parts, out_shape=jax.ShapeDtypeStruct((own_blocks, hei...  0.7 us
    pallas_call x1, Pallas kernels, shards(): pl.pallas_call(tile_sums, out_shape=jax.ShapeDtypeStruct((size, own_block...  0.64 us

profile of v28, /device:TPU:0, one launch (start us, length us, event | category | flops | bytes accessed | tf_op | source)
XLA Modules:
  0.0 22.8 jit_solution(243524604881932)
XLA Ops:
  0.0 1.2 %shard_map.37 = (bf16[8,16,128]{2,1,0:T(8,128)(2,1)S(1)}, bf16[24,192,128]{2,1,0:T(8,128)(2,1)S(1)}, bf16[96,128]{1,0:T(8,128)(2,1)S(1)}, bf16[2,128,192]{2,1,0:T(8,128)(2,1)S(1)}, f32[48,192]{1,0:T(8,128)S(1)}) custom-call(bf16[24,48]{1,0:T(8,128)(2,1)} %bitcast.7, s32[2,17]{1,0:T(2,128)} %bitcast.8, bf16[17,192,128]{2,1,0:T(8,128)(2,1)} %bitcast.6), custom_call_target="tpu_custom_call" | custom-call | bytes 1671168 | tf_op jit(solution)/shard_map/pallas_call | solution.py:260
  1.3 11.0 %all_to_all.10.histories_ref = bf16[8,16,128]{2,1,0:T(8,128)(2,1)S(1)} all-to-all(bf16[8,16,128]{2,1,0:T(8,128)(2,1)S(1)} %get-tuple-element.10), channel_id=1, replica_groups={{10,2,4,6,0,8,12,14},{11,3,5,7,1,9,13,15},{26,18,20,22,16,24,28,30},{27..., dimensions={0} | all-to-all | bytes 65536 | tf_op jit(solution)/shard_map/all_to_all | solution.py:41
  12.3 0.6 %shard_map.38 = s16[8,104,128]{2,1,0:T(8,128)(2,1)S(1)} custom-call(bf16[8,16,128]{2,1,0:T(8,128)(2,1)S(1)} %all_to_all.10.histories_ref, bf16[96,128]{1,0:T(8,128)(2,1)S(1)} %get-tuple-element.11.pick_ref, bf16[2,128,192]{2,1,0:T(8,128)(2,1)S(1)} %get-tuple-element.12.columns_ref, f32[48,192]{1,0:T(8,128)S(1)} %get-tuple-element.13.same_ref, ...), custom_call_target="tpu_custom_call" | custom-call | flops 40108032 | bytes 1671168 | tf_op jit(solution)/shard_map/pallas_call | solution.py:284
  12.9 9.2 %all_to_all.11.coded_ref = s16[8,104,128]{2,1,0:T(8,128)(2,1)S(1)} all-to-all(s16[8,104,128]{2,1,0:T(8,128)(2,1)S(1)} %shard_map.38), channel_id=1, replica_groups={{10,14,12,8,6,4,2,0},{11,15,13,9,7,5,3,1},{26,30,28,24,22,20,18,16},{27..., dimensions={0} | all-to-all | bytes 425984 | tf_op jit(solution)/shard_map/all_to_all | solution.py:41
  22.1 0.7 %shard_map.39 = f32[2,48,128]{2,1,0:T(8,128)} custom-call(s16[8,104,128]{2,1,0:T(8,128)(2,1)S(1)} %all_to_all.11.coded_ref), custom_call_target="tpu_custom_call" | custom-call | tf_op jit(solution)/shard_map/pallas_call | solution.py:303

commit v29 on v27

--- a/solution.py
+++ b/solution.py
@@ -62,12 +62,6 @@
     own_blocks = block_count // size
     height = pick_ref.shape[0] // SOURCES
     packed_rows = pick_ref.shape[1] // size
-    group = sorted_ref.shape[0] // size
-
-    def clear(index):
-        sorted_ref[pl.ds(index * group, group)] = jnp.zeros((group,) + tiles_ref.shape[1:], sorted_ref.dtype)
-
-    each(size, clear)
     tracer = split(lax.broadcasted_iota(jnp.int32, (height, pick_ref.shape[1]), 0), months)[0]
     offset = lax.broadcasted_iota(jnp.int32, (height, pick_ref.shape[1]), 1) - tracer
     column_of = split(lax.broadcasted_iota(jnp.int32, columns_ref.shape[1:], 1), months)[0]
@@ -120,6 +114,12 @@
     month_of_column = split(lax.broadcasted_iota(jnp.int32, same_ref.shape, 1), months)[1]
     same_ref[...] = (month_of_row == month_of_column).astype(same_ref.dtype)
     padded_ref[...] = jnp.zeros(padded_ref.shape, padded_ref.dtype)
+    group = sorted_ref.shape[0] // size
+
+    def clear(index):
+        sorted_ref[pl.ds(index * group, group)] = jnp.zeros((group,) + sorted_ref.shape[1:], sorted_ref.dtype)
+
+    each(size, clear)
     taker = (packed_rows, padded_ref.shape[0])
     placer = (padded_ref.shape[1], packed_width)
     take = lax.broadcasted_iota(jnp.int32, taker, 1) - lax.broadcasted_iota(jnp.int32, taker, 0) * own_blocks

time: 23.1 us -> 23.1 us (level)
  no operation moved by 1% of the time
where the time goes in v29:
time: 23.1 us; the launch traced here: 22.8 us
  blocking collectives  20.2 us (87%)
  Pallas kernels  2.54 us (11%)
    all_to_all x2, blocking collectives, exchange(): lax.all_to_all(value, 'tm', 0, 0, axis_index_groups=[order], tiled=True)  20.2 us
    pallas_call x1, Pallas kernels, shards(): pl.pallas_call(lambda *refs: prepare(months, *refs), out_shape=[jax.Shape...  1.25 us
    pallas_call x1, Pallas kernels, shards(): pl.pallas_call(add_parts, out_shape=jax.ShapeDtypeStruct((own_blocks, hei...  0.7 us
    pallas_call x1, Pallas kernels, shards(): pl.pallas_call(tile_sums, out_shape=jax.ShapeDtypeStruct((size, own_block...  0.6 us

profile of v29, /device:TPU:0, one launch (start us, length us, event | category | flops | bytes accessed | tf_op | source)
XLA Modules:
  0.0 22.8 jit_solution(7035318240476861579)
XLA Ops:
  0.0 1.2 %shard_map.37 = (bf16[8,16,128]{2,1,0:T(8,128)(2,1)S(1)}, bf16[24,192,128]{2,1,0:T(8,128)(2,1)S(1)}, bf16[96,128]{1,0:T(8,128)(2,1)S(1)}, bf16[2,128,192]{2,1,0:T(8,128)(2,1)S(1)}, f32[48,192]{1,0:T(8,128)S(1)}) custom-call(bf16[24,48]{1,0:T(8,128)(2,1)} %bitcast.7, s32[2,17]{1,0:T(2,128)} %bitcast.8, bf16[17,192,128]{2,1,0:T(8,128)(2,1)} %bitcast.6), custom_call_target="tpu_custom_call" | custom-call | bytes 1671168 | tf_op jit(solution)/shard_map/pallas_call | solution.py:251
  1.3 11.0 %all_to_all.10.histories_ref = bf16[8,16,128]{2,1,0:T(8,128)(2,1)S(1)} all-to-all(bf16[8,16,128]{2,1,0:T(8,128)(2,1)S(1)} %get-tuple-element.10), channel_id=1, replica_groups={{10,2,4,6,0,8,12,14},{11,3,5,7,1,9,13,15},{26,18,20,22,16,24,28,30},{27..., dimensions={0} | all-to-all | bytes 65536 | tf_op jit(solution)/shard_map/all_to_all | solution.py:39
  12.3 0.6 %shard_map.38 = s16[8,104,128]{2,1,0:T(8,128)(2,1)S(1)} custom-call(bf16[8,16,128]{2,1,0:T(8,128)(2,1)S(1)} %all_to_all.10.histories_ref, bf16[96,128]{1,0:T(8,128)(2,1)S(1)} %get-tuple-element.11.pick_ref, bf16[2,128,192]{2,1,0:T(8,128)(2,1)S(1)} %get-tuple-element.12.columns_ref, f32[48,192]{1,0:T(8,128)S(1)} %get-tuple-element.13.same_ref, ...), custom_call_target="tpu_custom_call" | custom-call | flops 40108032 | bytes 1671168 | tf_op jit(solution)/shard_map/pallas_call | solution.py:275
  12.9 9.2 %all_to_all.11.coded_ref = s16[8,104,128]{2,1,0:T(8,128)(2,1)S(1)} all-to-all(s16[8,104,128]{2,1,0:T(8,128)(2,1)S(1)} %shard_map.38), channel_id=1, replica_groups={{10,14,12,8,6,4,2,0},{11,15,13,9,7,5,3,1},{26,30,28,24,22,20,18,16},{27..., dimensions={0} | all-to-all | bytes 425984 | tf_op jit(solution)/shard_map/all_to_all | solution.py:39
  22.1 0.7 %shard_map.39 = f32[2,48,128]{2,1,0:T(8,128)} custom-call(s16[8,104,128]{2,1,0:T(8,128)(2,1)S(1)} %all_to_all.11.coded_ref), custom_call_target="tpu_custom_call" | custom-call | tf_op jit(solution)/shard_map/pallas_call | solution.py:288

commit v30 on v29

--- a/solution.py
+++ b/solution.py
@@ -19,10 +19,14 @@
 
 def history_order(size):
     inner = [device for device in range(1, size) if device != centre(size)]
-    return [centre(size)] + inner[: size // 2 - 1] + [0] + inner[size // 2 - 1 :]
+    order = [centre(size)] + inner[: size // 2 - 1] + [0] + inner[size // 2 - 1 :]
+    changed = {0: size * 3 // 4, size * 3 // 4: 0}
+    return [changed.get(device, device) for device in order]
 
 
 def history_slot(device, size):
+    far = size * 3 // 4
+    device = jnp.where(device == 0, far, jnp.where(device == far, 0, device))
     after = device - (device > centre(size)).astype(jnp.int32)
     after = after + (after >= size // 2).astype(jnp.int32)
     return jnp.where(device == centre(size), 0, jnp.where(device == 0, size // 2, after))

time: 23.1 us -> 23.1 us (level)
  no operation moved by 1% of the time
where the time goes in v30:
time: 23.1 us; the launch traced here: 22.8 us
  blocking collectives  20.3 us (88%)
  Pallas kernels  2.55 us (11%)
    all_to_all x2, blocking collectives, exchange(): lax.all_to_all(value, 'tm', 0, 0, axis_index_groups=[order], tiled=True)  20.3 us
    pallas_call x1, Pallas kernels, shards(): pl.pallas_call(lambda *refs: prepare(months, *refs), out_shape=[jax.Shape...  1.25 us
    pallas_call x1, Pallas kernels, shards(): pl.pallas_call(add_parts, out_shape=jax.ShapeDtypeStruct((own_blocks, hei...  0.7 us
    pallas_call x1, Pallas kernels, shards(): pl.pallas_call(tile_sums, out_shape=jax.ShapeDtypeStruct((size, own_block...  0.6 us

profile of v30, /device:TPU:0, one launch (start us, length us, event | category | flops | bytes accessed | tf_op | source)
XLA Modules:
  0.0 22.8 jit_solution(2004669858782597401)
XLA Ops:
  0.0 1.2 %shard_map.37 = (bf16[8,16,128]{2,1,0:T(8,128)(2,1)S(1)}, bf16[24,192,128]{2,1,0:T(8,128)(2,1)S(1)}, bf16[96,128]{1,0:T(8,128)(2,1)S(1)}, bf16[2,128,192]{2,1,0:T(8,128)(2,1)S(1)}, f32[48,192]{1,0:T(8,128)S(1)}) custom-call(bf16[24,48]{1,0:T(8,128)(2,1)} %bitcast.7, s32[2,17]{1,0:T(2,128)} %bitcast.8, bf16[17,192,128]{2,1,0:T(8,128)(2,1)} %bitcast.6), custom_call_target="tpu_custom_call" | custom-call | bytes 1671168 | tf_op jit(solution)/shard_map/pallas_call | solution.py:255
  1.3 10.9 %all_to_all.10.histories_ref = bf16[8,16,128]{2,1,0:T(8,128)(2,1)S(1)} all-to-all(bf16[8,16,128]{2,1,0:T(8,128)(2,1)S(1)} %get-tuple-element.10), channel_id=1, replica_groups={{10,2,4,6,12,8,0,14},{11,3,5,7,13,9,1,15},{26,18,20,22,28,24,16,30},{27..., dimensions={0} | all-to-all | bytes 65536 | tf_op jit(solution)/shard_map/all_to_all | solution.py:43
  12.2 0.6 %shard_map.38 = s16[8,104,128]{2,1,0:T(8,128)(2,1)S(1)} custom-call(bf16[8,16,128]{2,1,0:T(8,128)(2,1)S(1)} %all_to_all.10.histories_ref, bf16[96,128]{1,0:T(8,128)(2,1)S(1)} %get-tuple-element.11.pick_ref, bf16[2,128,192]{2,1,0:T(8,128)(2,1)S(1)} %get-tuple-element.12.columns_ref, f32[48,192]{1,0:T(8,128)S(1)} %get-tuple-element.13.same_ref, ...), custom_call_target="tpu_custom_call" | custom-call | flops 40108032 | bytes 1671168 | tf_op jit(solution)/shard_map/pallas_call | solution.py:279
  12.8 9.3 %all_to_all.11.coded_ref = s16[8,104,128]{2,1,0:T(8,128)(2,1)S(1)} all-to-all(s16[8,104,128]{2,1,0:T(8,128)(2,1)S(1)} %shard_map.38), channel_id=1, replica_groups={{10,14,12,8,6,4,2,0},{11,15,13,9,7,5,3,1},{26,30,28,24,22,20,18,16},{27..., dimensions={0} | all-to-all | bytes 425984 | tf_op jit(solution)/shard_map/all_to_all | solution.py:43
  22.1 0.7 %shard_map.39 = f32[2,48,128]{2,1,0:T(8,128)} custom-call(s16[8,104,128]{2,1,0:T(8,128)(2,1)S(1)} %all_to_all.11.coded_ref), custom_call_target="tpu_custom_call" | custom-call | tf_op jit(solution)/shard_map/pallas_call | solution.py:292

commit v31 on v29

--- a/solution.py
+++ b/solution.py
@@ -108,7 +108,7 @@
     load_rows = pltpu.make_async_copy(rows_in, rows_ref, semaphores.at[0])
     load_blocks = pltpu.make_async_copy(blocks_in, blocks_ref, semaphores.at[1])
     load_tiles = pltpu.make_async_copy(tiles_in, tiles_ref, semaphores.at[2])
-    for load in (load_rows, load_blocks, load_tiles):
+    for load in (load_tiles, load_rows, load_blocks):
         load.start()
     month_of_row = split(lax.broadcasted_iota(jnp.int32, same_ref.shape, 0), months)[1]
     month_of_column = split(lax.broadcasted_iota(jnp.int32, same_ref.shape, 1), months)[1]
@@ -171,20 +171,23 @@
         widened = jnp.dot(rows, columns_ref[which], preferred_element_type=jnp.float32)
         wide.append((widened * same_ref[...]).astype(jnp.bfloat16))
 
-    def product(which, start):
-        tiles = jnp.concatenate([sorted_ref[start + block] for block in range(own_blocks)], axis=1)
-        return jnp.dot(wide[which], tiles, preferred_element_type=jnp.float32)
+    both = jnp.concatenate(wide, axis=1)
+
+    def side_by_side(start):
+        return jnp.concatenate([sorted_ref[start + block] for block in range(own_blocks)], axis=1)
 
     def code(slot):
         owner = sums_device(slot, size)
         start = owner * own_blocks
-        total = product(0, start)
-        if isinstance(slot, int):
-            if owner >= size // 2:
-                total += product(1, half_count + start)
+        tiles = side_by_side(start)
+        if isinstance(slot, int) and owner < size // 2:
+            total = jnp.dot(wide[0], tiles, preferred_element_type=jnp.float32)
         else:
-            upper = product(1, half_count + jnp.maximum(start, half_count))
-            total += jnp.where(owner >= size // 2, upper, 0.0)
+            upper = side_by_side(half_count + (start if isinstance(slot, int) else jnp.maximum(start, half_count)))
+            if not isinstance(slot, int):
+                upper = jnp.where(owner >= size // 2, upper, jnp.zeros_like(upper))
+            stacked = jnp.concatenate([tiles, upper], axis=0)
+            total = jnp.dot(both, stacked, preferred_element_type=jnp.float32)
         values = [total[:, block * cell_count : (block + 1) * cell_count] for block in range(own_blocks)]
         top = jnp.abs(values[0])
         for value in values[1:]:

time: 23.1 us -> 23.2 us (level)
  no operation moved by 1% of the time
where the time goes in v31:
time: 23.2 us; the launch traced here: 22.9 us
  blocking collectives  20.2 us (87%)
  Pallas kernels  2.7 us (12%)
    all_to_all x2, blocking collectives, exchange(): lax.all_to_all(value, 'tm', 0, 0, axis_index_groups=[order], tiled=True)  20.2 us
    pallas_call x1, Pallas kernels, shards(): pl.pallas_call(lambda *refs: prepare(months, *refs), out_shape=[jax.Shape...  1.34 us
    pallas_call x1, Pallas kernels, shards(): pl.pallas_call(add_parts, out_shape=jax.ShapeDtypeStruct((own_blocks, hei...  0.7 us
    pallas_call x1, Pallas kernels, shards(): pl.pallas_call(tile_sums, out_shape=jax.ShapeDtypeStruct((size, own_block...  0.66 us

profile of v31, /device:TPU:0, one launch (start us, length us, event | category | flops | bytes accessed | tf_op | source)
XLA Modules:
  0.0 22.9 jit_solution(11233027255152205995)
XLA Ops:
  0.0 1.3 %shard_map.37 = (bf16[8,16,128]{2,1,0:T(8,128)(2,1)S(1)}, bf16[24,192,128]{2,1,0:T(8,128)(2,1)S(1)}, bf16[96,128]{1,0:T(8,128)(2,1)S(1)}, bf16[2,128,192]{2,1,0:T(8,128)(2,1)S(1)}, f32[48,192]{1,0:T(8,128)S(1)}) custom-call(bf16[24,48]{1,0:T(8,128)(2,1)} %bitcast.7, s32[2,17]{1,0:T(2,128)} %bitcast.8, bf16[17,192,128]{2,1,0:T(8,128)(2,1)} %bitcast.6), custom_call_target="tpu_custom_call" | custom-call | bytes 1671168 | tf_op jit(solution)/shard_map/pallas_call | solution.py:254
  1.3 11.0 %all_to_all.10.histories_ref = bf16[8,16,128]{2,1,0:T(8,128)(2,1)S(1)} all-to-all(bf16[8,16,128]{2,1,0:T(8,128)(2,1)S(1)} %get-tuple-element.10), channel_id=1, replica_groups={{10,2,4,6,0,8,12,14},{11,3,5,7,1,9,13,15},{26,18,20,22,16,24,28,30},{27..., dimensions={0} | all-to-all | bytes 65536 | tf_op jit(solution)/shard_map/all_to_all | solution.py:39
  12.3 0.7 %shard_map.38 = s16[8,104,128]{2,1,0:T(8,128)(2,1)S(1)} custom-call(bf16[8,16,128]{2,1,0:T(8,128)(2,1)S(1)} %all_to_all.10.histories_ref, bf16[96,128]{1,0:T(8,128)(2,1)S(1)} %get-tuple-element.11.pick_ref, bf16[2,128,192]{2,1,0:T(8,128)(2,1)S(1)} %get-tuple-element.12.columns_ref, f32[48,192]{1,0:T(8,128)S(1)} %get-tuple-element.13.same_ref, ...), custom_call_target="tpu_custom_call" | custom-call | flops 40108032 | bytes 1671168 | tf_op jit(solution)/shard_map/pallas_call | solution.py:278
  13.0 9.2 %all_to_all.11.coded_ref = s16[8,104,128]{2,1,0:T(8,128)(2,1)S(1)} all-to-all(s16[8,104,128]{2,1,0:T(8,128)(2,1)S(1)} %shard_map.38), channel_id=1, replica_groups={{10,14,12,8,6,4,2,0},{11,15,13,9,7,5,3,1},{26,30,28,24,22,20,18,16},{27..., dimensions={0} | all-to-all | bytes 425984 | tf_op jit(solution)/shard_map/all_to_all | solution.py:39
  22.3 0.7 %shard_map.39 = f32[2,48,128]{2,1,0:T(8,128)} custom-call(s16[8,104,128]{2,1,0:T(8,128)(2,1)S(1)} %all_to_all.11.coded_ref), custom_call_target="tpu_custom_call" | custom-call | tf_op jit(solution)/shard_map/pallas_call | solution.py:291

commit v32 on v29

--- a/solution.py
+++ b/solution.py
@@ -108,8 +108,9 @@
     load_rows = pltpu.make_async_copy(rows_in, rows_ref, semaphores.at[0])
     load_blocks = pltpu.make_async_copy(blocks_in, blocks_ref, semaphores.at[1])
     load_tiles = pltpu.make_async_copy(tiles_in, tiles_ref, semaphores.at[2])
-    for load in (load_rows, load_blocks, load_tiles):
-        load.start()
+    load_blocks.start()
+    load_rows.start()
+    load_tiles.start(priority=1)
     month_of_row = split(lax.broadcasted_iota(jnp.int32, same_ref.shape, 0), months)[1]
     month_of_column = split(lax.broadcasted_iota(jnp.int32, same_ref.shape, 1), months)[1]
     same_ref[...] = (month_of_row == month_of_column).astype(same_ref.dtype)

time: 23.1 us -> 23.2 us (level)
  no operation moved by 1% of the time
where the time goes in v32:
time: 23.2 us; the launch traced here: 22.9 us
  blocking collectives  20.2 us (87%)
  Pallas kernels  2.68 us (12%)
    all_to_all x2, blocking collectives, exchange(): lax.all_to_all(value, 'tm', 0, 0, axis_index_groups=[order], tiled=True)  20.2 us
    pallas_call x1, Pallas kernels, shards(): pl.pallas_call(lambda *refs: prepare(months, *refs), out_shape=[jax.Shape...  1.38 us
    pallas_call x1, Pallas kernels, shards(): pl.pallas_call(add_parts, out_shape=jax.ShapeDtypeStruct((own_blocks, hei...  0.7 us
    pallas_call x1, Pallas kernels, shards(): pl.pallas_call(tile_sums, out_shape=jax.ShapeDtypeStruct((size, own_block...  0.6 us

profile of v32, /device:TPU:0, one launch (start us, length us, event | category | flops | bytes accessed | tf_op | source)
XLA Modules:
  0.0 22.9 jit_solution(14472857689226653444)
XLA Ops:
  0.0 1.4 %shard_map.37 = (bf16[8,16,128]{2,1,0:T(8,128)(2,1)S(1)}, bf16[24,192,128]{2,1,0:T(8,128)(2,1)S(1)}, bf16[96,128]{1,0:T(8,128)(2,1)S(1)}, bf16[2,128,192]{2,1,0:T(8,128)(2,1)S(1)}, f32[48,192]{1,0:T(8,128)S(1)}) custom-call(bf16[24,48]{1,0:T(8,128)(2,1)} %bitcast.7, s32[2,17]{1,0:T(2,128)} %bitcast.8, bf16[17,192,128]{2,1,0:T(8,128)(2,1)} %bitcast.6), custom_call_target="tpu_custom_call" | custom-call | bytes 1671168 | tf_op jit(solution)/shard_map/pallas_call | solution.py:252
  1.4 11.0 %all_to_all.10.histories_ref = bf16[8,16,128]{2,1,0:T(8,128)(2,1)S(1)} all-to-all(bf16[8,16,128]{2,1,0:T(8,128)(2,1)S(1)} %get-tuple-element.10), channel_id=1, replica_groups={{10,2,4,6,0,8,12,14},{11,3,5,7,1,9,13,15},{26,18,20,22,16,24,28,30},{27..., dimensions={0} | all-to-all | bytes 65536 | tf_op jit(solution)/shard_map/all_to_all | solution.py:39
  12.4 0.6 %shard_map.38 = s16[8,104,128]{2,1,0:T(8,128)(2,1)S(1)} custom-call(bf16[8,16,128]{2,1,0:T(8,128)(2,1)S(1)} %all_to_all.10.histories_ref, bf16[96,128]{1,0:T(8,128)(2,1)S(1)} %get-tuple-element.11.pick_ref, bf16[2,128,192]{2,1,0:T(8,128)(2,1)S(1)} %get-tuple-element.12.columns_ref, f32[48,192]{1,0:T(8,128)S(1)} %get-tuple-element.13.same_ref, ...), custom_call_target="tpu_custom_call" | custom-call | flops 40108032 | bytes 1671168 | tf_op jit(solution)/shard_map/pallas_call | solution.py:276
  13.0 9.2 %all_to_all.11.coded_ref = s16[8,104,128]{2,1,0:T(8,128)(2,1)S(1)} all-to-all(s16[8,104,128]{2,1,0:T(8,128)(2,1)S(1)} %shard_map.38), channel_id=1, replica_groups={{10,14,12,8,6,4,2,0},{11,15,13,9,7,5,3,1},{26,30,28,24,22,20,18,16},{27..., dimensions={0} | all-to-all | bytes 425984 | tf_op jit(solution)/shard_map/all_to_all | solution.py:39
  22.2 0.7 %shard_map.39 = f32[2,48,128]{2,1,0:T(8,128)} custom-call(s16[8,104,128]{2,1,0:T(8,128)(2,1)S(1)} %all_to_all.11.coded_ref), custom_call_target="tpu_custom_call" | custom-call | tf_op jit(solution)/shard_map/pallas_call | solution.py:289

commit v33 on v29

--- a/solution.py
+++ b/solution.py
@@ -78,12 +78,15 @@
         picked = offset == history_slot(owner, size) * packed_rows
         pick_ref[pl.ds(which * height, height)] = picked.astype(pick_ref.dtype)
         columns_ref[which] = (shift == block * source_width).astype(columns_ref.dtype)
-    load_tiles.wait()
 
     def place(slot):
         sorted_ref[places[slot] if places else place_of(slot)] = tiles_ref[slot]
 
-    each(slot_count, place)
+    middle = slot_count // 2
+    load_tiles[0].wait()
+    each(middle, place)
+    load_tiles[1].wait()
+    each(slot_count - middle, lambda slot: place(middle + slot))
 
 
 def prepare(
@@ -107,8 +110,14 @@
     own_blocks = sorted_ref.shape[0] // 3 * 2 // size
     load_rows = pltpu.make_async_copy(rows_in, rows_ref, semaphores.at[0])
     load_blocks = pltpu.make_async_copy(blocks_in, blocks_ref, semaphores.at[1])
-    load_tiles = pltpu.make_async_copy(tiles_in, tiles_ref, semaphores.at[2])
-    for load in (load_rows, load_blocks, load_tiles):
+    middle = tiles_ref.shape[0] // 2
+    load_tiles = [
+        pltpu.make_async_copy(
+            tiles_in.at[pl.ds(start, count)], tiles_ref.at[pl.ds(start, count)], semaphores.at[2 + half]
+        )
+        for half, (start, count) in enumerate([(0, middle), (middle, tiles_ref.shape[0] - middle)])
+    ]
+    for load in (load_rows, load_blocks, *load_tiles):
         load.start()
     month_of_row = split(lax.broadcasted_iota(jnp.int32, same_ref.shape, 0), months)[1]
     month_of_column = split(lax.broadcasted_iota(jnp.int32, same_ref.shape, 1), months)[1]
@@ -264,7 +273,7 @@
             pltpu.VMEM(padded_shape, rows.dtype),
             pltpu.SMEM(blocks.shape, blocks.dtype),
             pltpu.VMEM(tiles.shape, tiles.dtype),
-            pltpu.SemaphoreType.DMA((3,)),
+            pltpu.SemaphoreType.DMA((4,)),
         ],
         compiler_params=pltpu.CompilerParams(vmem_limit_bytes=24 * 1024 * 1024),
         cost_estimate=pl.CostEstimate(flops=0, bytes_accessed=tiles.size * 4, transcendentals=0),

time: 23.1 us -> 23 us (level)
  no operation moved by 1% of the time
where the time goes in v33:
time: 23 us; the launch traced here: 22.8 us
  blocking collectives  20.2 us (88%)
  Pallas kernels  2.51 us (11%)
    all_to_all x2, blocking collectives, exchange(): lax.all_to_all(value, 'tm', 0, 0, axis_index_groups=[order], tiled=True)  20.2 us
    pallas_call x1, Pallas kernels, shards(): pl.pallas_call(lambda *refs: prepare(months, *refs), out_shape=[jax.Shape...  1.22 us
    pallas_call x1, Pallas kernels, shards(): pl.pallas_call(add_parts, out_shape=jax.ShapeDtypeStruct((own_blocks, hei...  0.7 us
    pallas_call x1, Pallas kernels, shards(): pl.pallas_call(tile_sums, out_shape=jax.ShapeDtypeStruct((size, own_block...  0.6 us

profile of v33, /device:TPU:0, one launch (start us, length us, event | category | flops | bytes accessed | tf_op | source)
XLA Modules:
  0.0 22.8 jit_solution(16466703364238451638)
XLA Ops:
  0.0 1.2 %shard_map.37 = (bf16[8,16,128]{2,1,0:T(8,128)(2,1)S(1)}, bf16[24,192,128]{2,1,0:T(8,128)(2,1)S(1)}, bf16[96,128]{1,0:T(8,128)(2,1)S(1)}, bf16[2,128,192]{2,1,0:T(8,128)(2,1)S(1)}, f32[48,192]{1,0:T(8,128)S(1)}) custom-call(bf16[24,48]{1,0:T(8,128)(2,1)} %bitcast.7, s32[2,17]{1,0:T(2,128)} %bitcast.8, bf16[17,192,128]{2,1,0:T(8,128)(2,1)} %bitcast.6), custom_call_target="tpu_custom_call" | custom-call | bytes 1671168 | tf_op jit(solution)/shard_map/pallas_call | solution.py:260
  1.2 11.0 %all_to_all.10.histories_ref = bf16[8,16,128]{2,1,0:T(8,128)(2,1)S(1)} all-to-all(bf16[8,16,128]{2,1,0:T(8,128)(2,1)S(1)} %get-tuple-element.10), channel_id=1, replica_groups={{10,2,4,6,0,8,12,14},{11,3,5,7,1,9,13,15},{26,18,20,22,16,24,28,30},{27..., dimensions={0} | all-to-all | bytes 65536 | tf_op jit(solution)/shard_map/all_to_all | solution.py:39
  12.2 0.6 %shard_map.38 = s16[8,104,128]{2,1,0:T(8,128)(2,1)S(1)} custom-call(bf16[8,16,128]{2,1,0:T(8,128)(2,1)S(1)} %all_to_all.10.histories_ref, bf16[96,128]{1,0:T(8,128)(2,1)S(1)} %get-tuple-element.11.pick_ref, bf16[2,128,192]{2,1,0:T(8,128)(2,1)S(1)} %get-tuple-element.12.columns_ref, f32[48,192]{1,0:T(8,128)S(1)} %get-tuple-element.13.same_ref, ...), custom_call_target="tpu_custom_call" | custom-call | flops 40108032 | bytes 1671168 | tf_op jit(solution)/shard_map/pallas_call | solution.py:284
  12.8 9.2 %all_to_all.11.coded_ref = s16[8,104,128]{2,1,0:T(8,128)(2,1)S(1)} all-to-all(s16[8,104,128]{2,1,0:T(8,128)(2,1)S(1)} %shard_map.38), channel_id=1, replica_groups={{10,14,12,8,6,4,2,0},{11,15,13,9,7,5,3,1},{26,30,28,24,22,20,18,16},{27..., dimensions={0} | all-to-all | bytes 425984 | tf_op jit(solution)/shard_map/all_to_all | solution.py:39
  22.1 0.7 %shard_map.39 = f32[2,48,128]{2,1,0:T(8,128)} custom-call(s16[8,104,128]{2,1,0:T(8,128)(2,1)S(1)} %all_to_all.11.coded_ref), custom_call_target="tpu_custom_call" | custom-call | tf_op jit(solution)/shard_map/pallas_call | solution.py:297

commit v34 on v33

--- a/solution.py
+++ b/solution.py
@@ -9,6 +9,7 @@
 LEVELS = 128
 SMALLEST = 2.0**-126
 SCALE_ROWS = 8
+PARTS = 4
 WRITTEN_OUT = 17
 SOURCES = 2
 
@@ -51,6 +52,10 @@
             body(index)
     else:
         lax.fori_loop(0, count, lambda index, carry: (body(index), carry)[1], 0)
+
+
+def parts_of(count):
+    return [range(count * part // PARTS, count * (part + 1) // PARTS) for part in range(PARTS)]
 
 
 def arrange(
@@ -82,11 +87,9 @@
     def place(slot):
         sorted_ref[places[slot] if places else place_of(slot)] = tiles_ref[slot]
 
-    middle = slot_count // 2
-    load_tiles[0].wait()
-    each(middle, place)
-    load_tiles[1].wait()
-    each(slot_count - middle, lambda slot: place(middle + slot))
+    for load, part in zip(load_tiles, parts_of(slot_count)):
+        load.wait()
+        each(len(part), lambda slot, part=part: place(part.start + slot))
 
 
 def prepare(
@@ -110,12 +113,13 @@
     own_blocks = sorted_ref.shape[0] // 3 * 2 // size
     load_rows = pltpu.make_async_copy(rows_in, rows_ref, semaphores.at[0])
     load_blocks = pltpu.make_async_copy(blocks_in, blocks_ref, semaphores.at[1])
-    middle = tiles_ref.shape[0] // 2
     load_tiles = [
         pltpu.make_async_copy(
-            tiles_in.at[pl.ds(start, count)], tiles_ref.at[pl.ds(start, count)], semaphores.at[2 + half]
+            tiles_in.at[pl.ds(part.start, len(part))],
+            tiles_ref.at[pl.ds(part.start, len(part))],
+            semaphores.at[2 + index],
         )
-        for half, (start, count) in enumerate([(0, middle), (middle, tiles_ref.shape[0] - middle)])
+        for index, part in enumerate(parts_of(tiles_ref.shape[0]))
     ]
     for load in (load_rows, load_blocks, *load_tiles):
         load.start()
@@ -273,7 +277,7 @@
             pltpu.VMEM(padded_shape, rows.dtype),
             pltpu.SMEM(blocks.shape, blocks.dtype),
             pltpu.VMEM(tiles.shape, tiles.dtype),
-            pltpu.SemaphoreType.DMA((4,)),
+            pltpu.SemaphoreType.DMA((2 + PARTS,)),
         ],
         compiler_params=pltpu.CompilerParams(vmem_limit_bytes=24 * 1024 * 1024),
         cost_estimate=pl.CostEstimate(flops=0, bytes_accessed=tiles.size * 4, transcendentals=0),

time: 23 us -> 23.1 us (level)
  no operation moved by 1% of the time
where the time goes in v34:
time: 23.1 us; the launch traced here: 22.9 us
  blocking collectives  20.2 us (87%)
  Pallas kernels  2.62 us (11%)
    all_to_all x2, blocking collectives, exchange(): lax.all_to_all(value, 'tm', 0, 0, axis_index_groups=[order], tiled=True)  20.2 us
    pallas_call x1, Pallas kernels, shards(): pl.pallas_call(lambda *refs: prepare(months, *refs), out_shape=[jax.Shape...  1.32 us
    pallas_call x1, Pallas kernels, shards(): pl.pallas_call(add_parts, out_shape=jax.ShapeDtypeStruct((own_blocks, hei...  0.7 us
    pallas_call x1, Pallas kernels, shards(): pl.pallas_call(tile_sums, out_shape=jax.ShapeDtypeStruct((size, own_block...  0.6 us

profile of v34, /device:TPU:0, one launch (start us, length us, event | category | flops | bytes accessed | tf_op | source)
XLA Modules:
  0.0 22.9 jit_solution(4012168036344005493)
XLA Ops:
  0.0 1.3 %shard_map.37 = (bf16[8,16,128]{2,1,0:T(8,128)(2,1)S(1)}, bf16[24,192,128]{2,1,0:T(8,128)(2,1)S(1)}, bf16[96,128]{1,0:T(8,128)(2,1)S(1)}, bf16[2,128,192]{2,1,0:T(8,128)(2,1)S(1)}, f32[48,192]{1,0:T(8,128)S(1)}) custom-call(bf16[24,48]{1,0:T(8,128)(2,1)} %bitcast.7, s32[2,17]{1,0:T(2,128)} %bitcast.8, bf16[17,192,128]{2,1,0:T(8,128)(2,1)} %bitcast.6), custom_call_target="tpu_custom_call" | custom-call | bytes 1671168 | tf_op jit(solution)/shard_map/pallas_call | solution.py:264
  1.3 11.0 %all_to_all.10.histories_ref = bf16[8,16,128]{2,1,0:T(8,128)(2,1)S(1)} all-to-all(bf16[8,16,128]{2,1,0:T(8,128)(2,1)S(1)} %get-tuple-element.10), channel_id=1, replica_groups={{10,2,4,6,0,8,12,14},{11,3,5,7,1,9,13,15},{26,18,20,22,16,24,28,30},{27..., dimensions={0} | all-to-all | bytes 65536 | tf_op jit(solution)/shard_map/all_to_all | solution.py:40
  12.3 0.6 %shard_map.38 = s16[8,104,128]{2,1,0:T(8,128)(2,1)S(1)} custom-call(bf16[8,16,128]{2,1,0:T(8,128)(2,1)S(1)} %all_to_all.10.histories_ref, bf16[96,128]{1,0:T(8,128)(2,1)S(1)} %get-tuple-element.11.pick_ref, bf16[2,128,192]{2,1,0:T(8,128)(2,1)S(1)} %get-tuple-element.12.columns_ref, f32[48,192]{1,0:T(8,128)S(1)} %get-tuple-element.13.same_ref, ...), custom_call_target="tpu_custom_call" | custom-call | flops 40108032 | bytes 1671168 | tf_op jit(solution)/shard_map/pallas_call | solution.py:288
  12.9 9.2 %all_to_all.11.coded_ref = s16[8,104,128]{2,1,0:T(8,128)(2,1)S(1)} all-to-all(s16[8,104,128]{2,1,0:T(8,128)(2,1)S(1)} %shard_map.38), channel_id=1, replica_groups={{10,14,12,8,6,4,2,0},{11,15,13,9,7,5,3,1},{26,30,28,24,22,20,18,16},{27..., dimensions={0} | all-to-all | bytes 425984 | tf_op jit(solution)/shard_map/all_to_all | solution.py:40
  22.2 0.7 %shard_map.39 = f32[2,48,128]{2,1,0:T(8,128)} custom-call(s16[8,104,128]{2,1,0:T(8,128)(2,1)S(1)} %all_to_all.11.coded_ref), custom_call_target="tpu_custom_call" | custom-call | tf_op jit(solution)/shard_map/pallas_call | solution.py:301

commit v35 on v33

--- a/solution.py
+++ b/solution.py
@@ -82,7 +82,7 @@
     def place(slot):
         sorted_ref[places[slot] if places else place_of(slot)] = tiles_ref[slot]
 
-    middle = slot_count // 2
+    middle = slot_count * 2 // 3
     load_tiles[0].wait()
     each(middle, place)
     load_tiles[1].wait()
@@ -110,7 +110,7 @@
     own_blocks = sorted_ref.shape[0] // 3 * 2 // size
     load_rows = pltpu.make_async_copy(rows_in, rows_ref, semaphores.at[0])
     load_blocks = pltpu.make_async_copy(blocks_in, blocks_ref, semaphores.at[1])
-    middle = tiles_ref.shape[0] // 2
+    middle = tiles_ref.shape[0] * 2 // 3
     load_tiles = [
         pltpu.make_async_copy(
             tiles_in.at[pl.ds(start, count)], tiles_ref.at[pl.ds(start, count)], semaphores.at[2 + half]

time: 23 us -> 23 us (level)
  no operation moved by 1% of the time
where the time goes in v35:
time: 23 us; the launch traced here: 22.7 us
  blocking collectives  20.2 us (88%)
  Pallas kernels  2.49 us (11%)
    all_to_all x2, blocking collectives, exchange(): lax.all_to_all(value, 'tm', 0, 0, axis_index_groups=[order], tiled=True)  20.2 us
    pallas_call x1, Pallas kernels, shards(): pl.pallas_call(lambda *refs: prepare(months, *refs), out_shape=[jax.Shape...  1.2 us
    pallas_call x1, Pallas kernels, shards(): pl.pallas_call(add_parts, out_shape=jax.ShapeDtypeStruct((own_blocks, hei...  0.7 us
    pallas_call x1, Pallas kernels, shards(): pl.pallas_call(tile_sums, out_shape=jax.ShapeDtypeStruct((size, own_block...  0.6 us

profile of v35, /device:TPU:0, one launch (start us, length us, event | category | flops | bytes accessed | tf_op | source)
XLA Modules:
  0.0 22.7 jit_solution(13734048774288360293)
XLA Ops:
  0.0 1.2 %shard_map.37 = (bf16[8,16,128]{2,1,0:T(8,128)(2,1)S(1)}, bf16[24,192,128]{2,1,0:T(8,128)(2,1)S(1)}, bf16[96,128]{1,0:T(8,128)(2,1)S(1)}, bf16[2,128,192]{2,1,0:T(8,128)(2,1)S(1)}, f32[48,192]{1,0:T(8,128)S(1)}) custom-call(bf16[24,48]{1,0:T(8,128)(2,1)} %bitcast.7, s32[2,17]{1,0:T(2,128)} %bitcast.8, bf16[17,192,128]{2,1,0:T(8,128)(2,1)} %bitcast.6), custom_call_target="tpu_custom_call" | custom-call | bytes 1671168 | tf_op jit(solution)/shard_map/pallas_call | solution.py:260
  1.2 11.0 %all_to_all.10.histories_ref = bf16[8,16,128]{2,1,0:T(8,128)(2,1)S(1)} all-to-all(bf16[8,16,128]{2,1,0:T(8,128)(2,1)S(1)} %get-tuple-element.10), channel_id=1, replica_groups={{10,2,4,6,0,8,12,14},{11,3,5,7,1,9,13,15},{26,18,20,22,16,24,28,30},{27..., dimensions={0} | all-to-all | bytes 65536 | tf_op jit(solution)/shard_map/all_to_all | solution.py:39
  12.2 0.6 %shard_map.38 = s16[8,104,128]{2,1,0:T(8,128)(2,1)S(1)} custom-call(bf16[8,16,128]{2,1,0:T(8,128)(2,1)S(1)} %all_to_all.10.histories_ref, bf16[96,128]{1,0:T(8,128)(2,1)S(1)} %get-tuple-element.11.pick_ref, bf16[2,128,192]{2,1,0:T(8,128)(2,1)S(1)} %get-tuple-element.12.columns_ref, f32[48,192]{1,0:T(8,128)S(1)} %get-tuple-element.13.same_ref, ...), custom_call_target="tpu_custom_call" | custom-call | flops 40108032 | bytes 1671168 | tf_op jit(solution)/shard_map/pallas_call | solution.py:284
  12.8 9.2 %all_to_all.11.coded_ref = s16[8,104,128]{2,1,0:T(8,128)(2,1)S(1)} all-to-all(s16[8,104,128]{2,1,0:T(8,128)(2,1)S(1)} %shard_map.38), channel_id=1, replica_groups={{10,14,12,8,6,4,2,0},{11,15,13,9,7,5,3,1},{26,30,28,24,22,20,18,16},{27..., dimensions={0} | all-to-all | bytes 425984 | tf_op jit(solution)/shard_map/all_to_all | solution.py:39
  22.0 0.7 %shard_map.39 = f32[2,48,128]{2,1,0:T(8,128)} custom-call(s16[8,104,128]{2,1,0:T(8,128)(2,1)S(1)} %all_to_all.11.coded_ref), custom_call_target="tpu_custom_call" | custom-call | tf_op jit(solution)/shard_map/pallas_call | solution.py:297
